TPU v7x, 32 devices: a whole 2x2x4 slice. The times are simulated.
32 devices in a mesh: tm: 8 (over z, y), batch: 4 (over x, core).
Axes of the slice: x: 2, y: 2, z: 4, core: 2. Of those that a mesh axis runs over, the one named last changes fastest.
Arguments:
- inputs: bfloat16 [256, 4, 128], P('tm', 'batch'), may hold values from -6 to 6
- h_start: float32 [4, 128], P('batch'), may hold values from -4 to 4
- in_weight: bfloat16 [128, 384], replicated, may hold values from -0.5 to 0.5
- rec_weight: float32 [128, 384], replicated, may hold values from -0.5 to 0.5
- update_bias: float32 [128], replicated, may hold values from -1 to 14
- reset_bias: float32 [128], replicated, may hold values from -4 to 4
- cand_bias: float32 [128], replicated, may hold values from -3 to 3
- rec_bias: float32 [128], replicated, may hold values from -3 to 3
Outputs:
- states: float32 [256, 4, 128], P('tm', 'batch')
- residual_norms: float32 [2], replicated
All inputs are finite; a program needn't handle non-finite values.
Results may differ from a plain program's by a relative error of at most 0.0003.
Values sent between devices are 32-bit elements; how exact they have to be, the bound alone decides.
No kernel may reach another device: no remote copies, remote signals or barrier semaphores. Data moves between devices by JAX's collectives and lax.ppermute only.
A program may use at most 64 MiB of HBM per device.

v0:
```python
import jax
import jax.numpy as jnp
from jax import lax
from jax.sharding import PartitionSpec as P

ITERS = 2
BLOCK = 16


HIGH = lax.Precision.HIGHEST


def carried_in(value, axis, join, neutral):
    count, mine = (lax.axis_size(axis), lax.axis_index(axis))
    pieces = jax.tree.map(lambda part: lax.all_gather(part, axis), value)
    so_far = jax.tree.map(
        lambda part, zero: jnp.full_like(part, 0) + jnp.asarray(zero, part.dtype), value, neutral
    )

    def turn(position, so_far):
        longer = join(so_far, jax.tree.map(lambda part: part[position], pieces))
        return jax.tree.map(lambda new, old: jnp.where(position < mine, new, old), longer, so_far)

    return lax.fori_loop(0, count - 1, turn, so_far)


def passed_along(shard, axis, by):
    peers = lax.axis_size(axis)
    pairs = [(i, i + by) for i in range(peers) if 0 <= i + by < peers]
    return lax.ppermute(shard, axis, pairs)


def cell_parts(in_gates, previous, rec_weight, update_bias, reset_bias, cand_bias, rec_bias):
    units = rec_weight.shape[0]
    rec_gates = jnp.dot(previous, rec_weight, precision=HIGH)
    update_gate = jax.nn.sigmoid(in_gates[:, :units] + rec_gates[:, :units] + update_bias)
    reset_gate = jax.nn.sigmoid(
        in_gates[:, units : 2 * units] + rec_gates[:, units : 2 * units] + reset_bias
    )
    recur_term = rec_gates[:, 2 * units :] + rec_bias
    candidate = jnp.tanh(in_gates[:, 2 * units :] + cand_bias + reset_gate * recur_term)
    stepped = (1.0 - update_gate) * candidate + update_gate * previous
    return (update_gate, reset_gate, recur_term, candidate, stepped)


def jacobian(previous, update_gate, reset_gate, recur_term, candidate, rec_weight, identity):
    units = rec_weight.shape[0]
    coef_update = (previous - candidate) * update_gate * (1.0 - update_gate)
    common = (1.0 - update_gate) * (1.0 - candidate * candidate)
    coef_cand = common * reset_gate
    coef_reset = common * recur_term * reset_gate * (1.0 - reset_gate)
    return (
        identity * update_gate[..., None, :]
        + rec_weight[:, :units] * coef_update[..., None, :]
        + rec_weight[:, units : 2 * units] * coef_reset[..., None, :]
        + rec_weight[:, 2 * units :] * coef_cand[..., None, :]
    )


def combine(earlier, later):
    mat_early, vec_early = earlier
    mat_late, vec_late = later
    new_mat = jnp.einsum("...ij,...jk->...ik", mat_early, mat_late, precision=HIGH)
    new_vec = jnp.einsum("...j,...jk->...k", vec_early, mat_late, precision=HIGH) + vec_late
    return (new_mat, new_vec)


def solve_chain(mats, vecs, start, identity):
    step_count, units = vecs.shape
    blocks = step_count // BLOCK
    blk_mats = mats.reshape(blocks, BLOCK, units, units)
    blk_vecs = vecs.reshape(blocks, BLOCK, units)
    fold_mats, fold_vecs = (blk_mats, blk_vecs)
    while fold_mats.shape[1] > 1:
        fold_mats, fold_vecs = combine(
            (fold_mats[:, 0::2], fold_vecs[:, 0::2]), (fold_mats[:, 1::2], fold_vecs[:, 1::2])
        )
    fold_mats = fold_mats[:, 0]
    fold_vecs = fold_vecs[:, 0]
    incl_mats, incl_vecs = lax.associative_scan(combine, (fold_mats, fold_vecs), axis=0)
    whole_mat = incl_mats[-1]
    whole_vec = incl_vecs[-1]
    zero_vec = jnp.zeros((units,), jnp.float32)
    earlier_mat, earlier_vec = carried_in(
        (whole_mat, whole_vec), "tm", combine, (identity, zero_vec)
    )
    entering = jnp.dot(start, earlier_mat, precision=HIGH) + earlier_vec
    excl_mats = jnp.concatenate([identity[None], incl_mats[:-1]], axis=0)
    excl_vecs = jnp.concatenate([jnp.zeros((1, units), jnp.float32), incl_vecs[:-1]], axis=0)
    block_starts = jnp.einsum("j,bjk->bk", entering, excl_mats, precision=HIGH) + excl_vecs

    def advance(carried, item):
        one_mat, one_vec = item
        carried = jnp.einsum("bj,bjk->bk", carried, one_mat, precision=HIGH) + one_vec
        return (carried, carried)

    final_rows, walked = lax.scan(
        advance, block_starts, (jnp.moveaxis(blk_mats, 1, 0), jnp.moveaxis(blk_vecs, 1, 0))
    )
    return jnp.moveaxis(walked, 0, 1).reshape(step_count, units)


def per_device(
    inputs, h_start, in_weight, rec_weight, update_bias, reset_bias, cand_bias, rec_bias
):
    step_count = inputs.shape[0]
    units = rec_weight.shape[0]
    is_first = lax.axis_index("tm") == 0
    start = h_start[0]
    identity = jnp.eye(units, dtype=jnp.float32)
    in_gates = jnp.dot(inputs[:, 0, :], in_weight, preferred_element_type=jnp.float32)
    total_steps = step_count * lax.axis_size("tm")
    position = lax.axis_index("tm") * step_count + jnp.arange(step_count, dtype=jnp.int32)
    weights = (position.astype(jnp.float32) + 1.0) / total_steps
    first_row = jnp.where(is_first, start, jnp.zeros_like(start))
    previous = jnp.zeros((step_count, units), jnp.float32).at[0].set(first_row)
    current = previous
    partials = []

    def record(current, stepped):
        local_sum = jnp.sum(weights[:, None] * (current - stepped) ** 2)
        return lax.psum(local_sum, ("tm", "batch"))

    for newton in range(ITERS):
        update_gate, reset_gate, recur_term, candidate, stepped = cell_parts(
            in_gates, previous, rec_weight, update_bias, reset_bias, cand_bias, rec_bias
        )
        if newton > 0:
            partials.append(record(current, stepped))
        mats = jacobian(
            previous, update_gate, reset_gate, recur_term, candidate, rec_weight, identity
        )
        offsets = stepped - jnp.einsum("tj,tjk->tk", previous, mats, precision=HIGH)
        current = solve_chain(mats, offsets, start, identity)
        arrived = passed_along(current[-1], "tm", 1)
        previous = jnp.concatenate(
            [jnp.where(is_first, start, arrived)[None, :], current[:-1]], axis=0
        )
    parts = cell_parts(in_gates, previous, rec_weight, update_bias, reset_bias, cand_bias, rec_bias)
    partials.append(record(current, parts[4]))
    totals = jnp.stack(partials)
    denom = lax.axis_size("batch") * units * (total_steps + 1) / 2.0
    residual_norms = jnp.sqrt(totals / denom + 1e-06)
    return (current[:, None, :], residual_norms)


def solution(mesh):
    in_specs = (P("tm", "batch", None), P("batch", None), P(), P(), P(), P(), P(), P())
    out_specs = (P("tm", "batch", None), P())
    return jax.shard_map(
        per_device, mesh=mesh, in_specs=in_specs, out_specs=out_specs, check_vma=False
    )
```

profile of v0, /device:TPU:0, one launch (start us, length us, event | category | flops | bytes accessed | tf_op | source)
XLA Modules:
  0.0 190.9 jit_solution(15308826519464431079)
XLA Ops:
  0.8 0.9 fusion.179
  1.7 0.7 broadcast_select_fusion.4
  2.4 1.2 fusion.110
  3.5 0.8 fusion.156
  4.4 0.7 fusion.113
  5.1 0.7 subtract_multiply_fusion.2
  5.8 2.2 %fusion.40 = f32[32,1,128]{2,1,0:T(1,128)S(1)} fusion(f32[32,128,1]{1,2,0:T(1,128)S(1)} %bitcast.400, f32[32,128]{1,0:T(8,128)S(1)} %get-tuple-element.406, f32[128,128]{1,0:T(8,128)S(1)} %get-tuple-element.397, f32[32,128]{1,0:T(8,128)S(1)} %get-tuple-element.405, f32[128,128]{1,0:T(8,128)S(1)} %get-tuple-element.398, ...), kind=kOutput, calls=%fused_computation.53 | convolution fusion | flops 9961472 | bytes 360448 | tf_op jit(solution)/shard_map/tj,tjk->tk/dot_general | solution.py:133
  8.0 0.6 multiply_add_fusion.3
  8.6 1.1 fusion.74
  9.7 1.0 fusion.79
  10.8 0.7 fusion.84
  11.4 0.5 fusion.89
  12.0 0.4 fusion.94
  12.4 0.3 fusion.105
  12.9 0.3 fusion.99
  13.8 32.4 %all_gather.12 = f32[8,128,128]{2,1,0:T(8,128)S(1)} all-gather(f32[1,128,128]{2,1,0:T(8,128)S(1)} %get-tuple-element.402), channel_id=1, replica_groups=mesh['tm'=8,'batch'=4] {'tm'}, dimensions={0}, use_global_device_ids=true | all-gather | bytes 589824 | tf_op jit(solution)/shard_map/all_gather | solution.py:15
  46.2 20.6 %all-gather = f32[8,1,128]{2,1,0:T(1,128)S(1)} all-gather(f32[1,1,128]{2,1,0:T(1,128)S(1)} %get-tuple-element.410), channel_id=1, replica_groups=mesh['tm'=8,'batch'=4] {'tm'}, dimensions={0}, use_global_device_ids=true | all-gather | bytes 4608 | tf_op jit(solution)/shard_map/all_gather | solution.py:15
  66.7 3.5 %while.59 = (s32[]{:T(128)}, f32[128,128]{0,1:T(8,128)S(1)}, f32[128]{0:T(128)S(1)}, s32[]{:T(128)}, f32[8,128,128]{2,1,0:T(8,128)S(1)}, /*index=5*/f32[8,128]{1,0:T(8,128)S(1)}, s32[]{:T(128)}, s32[]{:T(128)}) while((s32[]{:T(128)}, f32[128,128]{0,1:T(8,128)S(1)}, f32[128]{0:T(128)S(1)}, s32[]{:T(128)}, ...), condition=%wide.region_1.2_spmd.clone, body=%wide.region_0.1_spmd.clone.sunk | while | flops 25379332 | bytes 464500 | solution.py:24
  66.8 0.3 fusion.234
  67.3 0.3 fusion.234
  67.8 0.3 fusion.234
  68.3 0.3 fusion.234
  68.8 0.3 fusion.234
  69.3 0.3 fusion.234
  69.8 0.3 fusion.234
  70.8 0.6 multiply_add_fusion.2
  71.4 4.0 %while.57 = (s32[]{:T(128)}, f32[2,128]{1,0:T(2,128)S(1)}, f32[16,2,128]{2,1,0:T(2,128)S(1)}, f32[16,2,128,128]{3,2,1,0:T(8,128)S(1)}, f32[16,2,128]{2,1,0:T(2,128)S(1)}, /*index=5*/s32[]{:T(128)}) while((s32[]{:T(128)}, f32[2,128]{1,0:T(2,128)S(1)}, f32[16,2,128]{2,1,0:T(2,128)S(1)}, f32[16,2,128,128]{3,2,1,0:T(8,128)S(1)}, ...), condition=%wide.region_3.4_spmd, body=%wide.region_2.3_spmd.sunk | while | flops 393474 | bytes 137301 | solution.py:97
  71.4 0.2 fusion.226
  72.6 0.2 fusion.226
  72.9 0.2 fusion.226
  73.6 0.2 fusion.226
  73.9 0.2 fusion.226
  74.1 0.2 fusion.226
  74.8 0.2 fusion.226
  75.4 1.5 collective-permute-start
  76.8 1.1 collective-permute-done
  78.3 2.2 %fusion.32 = f32[32,1,128]{2,1,0:T(1,128)S(1)} fusion(f32[32,128,1]{1,2,0:T(1,128)S(1)} %bitcast.385, f32[32,128]{1,0:T(8,128)S(1)} %get-tuple-element.404, f32[32,128]{1,0:T(8,128)S(1)} %get-tuple-element.403, f32[32,128]{1,0:T(8,128)S(1)} %get-tuple-element.388, f32[32,128]{1,0:T(8,128)S(1)} %get-tuple-element.389, ...), kind=kOutput, calls=%fused_computation.43 | convolution fusion | flops 9961472 | bytes 360448 | tf_op jit(solution)/shard_map/tj,tjk->tk/dot_general | solution.py:133
  80.5 0.6 multiply_add_fusion.1
  81.1 1.1 fusion.60
  82.2 1.0 fusion.76
  83.3 0.7 fusion.82
  83.9 0.5 fusion.86
  84.5 0.4 fusion.92
  84.9 0.3 fusion.104
  85.4 0.3 fusion.96
  86.2 31.2 %all_gather.14 = f32[8,128,128]{2,1,0:T(8,128)S(1)} all-gather(f32[1,128,128]{2,1,0:T(8,128)S(1)} %get-tuple-element.400), channel_id=1, replica_groups=mesh['tm'=8,'batch'=4] {'tm'}, dimensions={0}, use_global_device_ids=true | all-gather | bytes 589824 | tf_op jit(solution)/shard_map/all_gather | solution.py:15
  117.5 19.0 %all-gather.1 = f32[8,1,128]{2,1,0:T(1,128)S(1)} all-gather(f32[1,1,128]{2,1,0:T(1,128)S(1)} %get-tuple-element.408), channel_id=1, replica_groups=mesh['tm'=8,'batch'=4] {'tm'}, dimensions={0}, use_global_device_ids=true | all-gather | bytes 4608 | tf_op jit(solution)/shard_map/all_gather | solution.py:15
  136.5 3.5 %while.60 = (s32[]{:T(128)}, f32[128,128]{0,1:T(8,128)S(1)}, f32[128]{0:T(128)S(1)}, s32[]{:T(128)}, f32[8,128,128]{2,1,0:T(8,128)S(1)}, /*index=5*/f32[8,128]{1,0:T(8,128)S(1)}, s32[]{:T(128)}, s32[]{:T(128)}) while((s32[]{:T(128)}, f32[128,128]{0,1:T(8,128)S(1)}, f32[128]{0:T(128)S(1)}, s32[]{:T(128)}, ...), condition=%wide.region_5.6_spmd.clone, body=%wide.region_4.5_spmd.clone.sunk | while | flops 25379332 | bytes 464500 | solution.py:24
  136.5 0.3 fusion.240
  137.0 0.3 fusion.240
  137.5 0.3 fusion.240
  138.0 0.3 fusion.240
  138.5 0.3 fusion.240
  139.1 0.3 fusion.240
  139.6 0.3 fusion.240
  140.5 0.6 multiply_add_fusion
  141.1 4.0 %while.58 = (s32[]{:T(128)}, f32[2,128]{1,0:T(2,128)S(1)}, f32[16,2,128]{2,1,0:T(2,128)S(1)}, f32[16,2,128,128]{3,2,1,0:T(8,128)S(1)}, f32[16,2,128]{2,1,0:T(2,128)S(1)}, /*index=5*/s32[]{:T(128)}) while((s32[]{:T(128)}, f32[2,128]{1,0:T(2,128)S(1)}, f32[16,2,128]{2,1,0:T(2,128)S(1)}, f32[16,2,128,128]{3,2,1,0:T(8,128)S(1)}, ...), condition=%wide.region_7.8_spmd, body=%wide.region_6.7_spmd.sunk | while | flops 393474 | bytes 137301 | solution.py:97
  141.1 0.2 fusion.229
  145.1 1.3 collective-permute-start.1
  146.4 1.3 collective-permute-done.1
  147.7 0.2 fusion.155
  147.9 0.7 multiply_reduce_fusion
  148.6 40.5 %all-reduce.9 = (f32[1]{0:T(128)}, f32[1]{0:T(128)}) all-reduce(f32[1]{0:T(128)} %bitcast.126, f32[1]{0:T(128)} %bitcast.122), channel_id=1, replica_groups=mesh['tm'=8,'batch'=4] {'tm','batch'}, use_global_device_ids=true, to_apply=%region_11.12 | all-reduce | flops 2 | bytes 16 | tf_op jit(solution)/shard_map/psum | solution.py:122
  189.1 1.8 fusion.167
  (192 shorter events, 11.7 us)
Async XLA Ops:
  0.6 2.9 %copy-start = (bf16[128,384]{1,0:T(8,128)(2,1)S(1)}, bf16[128,384]{1,0:T(8,128)(2,1)}, u32[]{:S(2)}) copy-start(bf16[128,384]{1,0:T(8,128)(2,1)} %param.20) | copy-start | bytes 294916
  0.7 7.3 %copy-start.1 = (f32[128,128]{0,1:T(8,128)}, f32[128,128]{0,1:T(8,128)S(1)}, u32[]{:S(2)}) copy-start(f32[128,128]{0,1:T(8,128)S(1)} %fusion.108) | copy-start | bytes 196612
  10.7 3.0 %copy-start.11 = (pred[2]{0:T(512)(128)(4,1)S(1)}, pred[2]{0:T(512)(128)(4,1)}, u32[]{:S(2)}) copy-start(pred[2]{0:T(512)(128)(4,1)} %constant.111.clone.1) | copy-start | bytes 10
  11.4 55.3 %copy-start.3 = (f32[128,128]{0,1:T(8,128)S(1)}, f32[128,128]{0,1:T(8,128)}, u32[]{:S(2)}) copy-start(f32[128,128]{0,1:T(8,128)} %copy-done.1) | copy-start | bytes 196612
  12.7 57.7 %copy-start.7 = (f32[1,128]{1,0:T(1,128)S(1)}, f32[1,128]{1,0:T(1,128)}, u32[]{:S(2)}) copy-start(f32[1,128]{1,0:T(1,128)} %param.19) | copy-start | bytes 1540
  70.3 7.7 %copy-start.4 = (f32[128,384]{1,0:T(8,128)S(1)}, f32[128,384]{1,0:T(8,128)}, u32[]{:S(2)}) copy-start(f32[128,384]{1,0:T(8,128)} %param.21) | copy-start | bytes 589828
  70.3 7.9 %copy-start.6 = (f32[128]{0:T(128)S(1)}, f32[128]{0:T(128)}, u32[]{:S(2)}) copy-start(f32[128]{0:T(128)} %param.25) | copy-start | bytes 1540
  70.3 7.9 %copy-start.8 = (f32[128]{0:T(128)S(1)}, f32[128]{0:T(128)}, u32[]{:S(2)}) copy-start(f32[128]{0:T(128)} %param.22) | copy-start | bytes 1540
  70.3 7.9 %copy-start.9 = (f32[128]{0:T(128)S(1)}, f32[128]{0:T(128)}, u32[]{:S(2)}) copy-start(f32[128]{0:T(128)} %param.24) | copy-start | bytes 1540
  70.3 7.9 %copy-start.10 = (f32[128]{0:T(128)S(1)}, f32[128]{0:T(128)}, u32[]{:S(2)}) copy-start(f32[128]{0:T(128)} %param.23) | copy-start | bytes 1540
  75.4 2.6 %collective-permute-start = (f32[128]{0:T(128)S(1)}, f32[128]{0:T(128)S(1)}, u32[]{:S(2)}, u32[]{:S(2)}) collective-permute-start(f32[128]{0:T(128)S(1)} %slice_bitcast_fusion.26), channel_id=1, source_target_pairs={{0,4},{4,8},{8,12},{12,16},{16,20},{20,24},{24,28},{1,5},{5,9},{9,... | collective-permute-start | bytes 1544 | tf_op jit(solution)/shard_map/ppermute | solution.py:30
  83.9 52.6 %copy-start.2 = (f32[128,128]{0,1:T(8,128)S(1)}, f32[128,128]{0,1:T(8,128)}, u32[]{:S(2)}) copy-start(f32[128,128]{0,1:T(8,128)} %copy-done.1) | copy-start | bytes 196612
  145.1 45.9 %copy-start.5 = (f32[2,16,128]{2,1,0:T(8,128)}, f32[2,16,128]{2,1,0:T(8,128)S(1)}, u32[]{:S(2)}) copy-start(f32[2,16,128]{2,1,0:T(8,128)S(1)} %copy.40) | copy-start | bytes 49156
  145.1 2.6 %collective-permute-start.1 = (f32[128]{0:T(128)S(1)}, f32[128]{0:T(128)S(1)}, u32[]{:S(2)}, u32[]{:S(2)}) collective-permute-start(f32[128]{0:T(128)S(1)} %slice_bitcast_fusion.24), channel_id=1, source_target_pairs={{0,4},{4,8},{8,12},{12,16},{16,20},{20,24},{24,28},{1,5},{5,9},{9,... | collective-permute-start | bytes 1544 | tf_op jit(solution)/shard_map/ppermute | solution.py:30
where the time goes:
time: 191 us
  blocking collectives  144 us (75%)
  matrix products  31.1 us (16%)
  other arithmetic  7.66 us (4%)
  starting transfers between devices  2.76 us (1%)
  waiting for transfers between devices  2.35 us (1%)
    all_gather x4, blocking collectives, carried_in(): pieces = jax.tree.map(lambda part: lax.all_gather(part, axis), value)  103 us
    psum x1, blocking collectives, record(): return lax.psum(local_sum, ('tm', 'batch'))  40.5 us
    dot_general x24, matrix products, combine(): jnp.einsum('...ij,...jk->...ik', mat_early, mat_late, precision=HIGH)  9.4 us
    dot_general x32, matrix products, advance(): jnp.einsum('bj,bjk->bk', carried, one_mat, precision=HIGH) + one_vec  7.44 us
    dot_general x24, matrix products, combine(): jnp.einsum('...j,...jk->...k', vec_early, mat_late, precision=HIGH)  6.71 us
    dot_general x2, matrix products, per_device(): offsets = stepped - jnp.einsum('tj,tjk->tk', previous, mats, precision=HIGH)  4.34 us
  transfers between devices with their start and end apart: 2, of which 2 were waited for; matrix products, arithmetic and copies ran while one was open for 0% of the time, Pallas kernels for 0%

commit v1 on v0

v1 whole, which is shorter than its diff:
```python
import functools

import jax
import jax.numpy as jnp
from jax import lax
from jax.experimental import pallas as pl
from jax.experimental.pallas import tpu as pltpu
from jax.sharding import PartitionSpec as P

ITERS = 2
BLOCK = 4
WINDOW = 4
PAD = 16
F32 = jnp.float32
BF16 = jnp.bfloat16


def halves(value):
    high = value.astype(BF16)
    return high, (value - high.astype(F32)).astype(BF16)


def paired_rows(value):
    return jnp.concatenate(halves(value), axis=1)


def paired_cols(value):
    both = jnp.concatenate(halves(value), axis=1)
    return jnp.concatenate([both, both], axis=0)


def product(rows, cols):
    width = cols.shape[1]
    both = jnp.dot(paired_rows(rows), paired_cols(cols), preferred_element_type=F32)
    return both[:, :width] + both[:, width:]


def as_column(row):
    units = row.shape[1]
    return jnp.broadcast_to(row, (units, units)).T


def row_times(column, matrix):
    return jnp.sum(column * matrix, axis=0, keepdims=True)


def cell(gates, previous, rec_weight, rec_bias):
    units = previous.shape[1]
    rec = product(previous, rec_weight)
    update = jax.nn.sigmoid(gates[:, :units] + rec[:, :units])
    reset = jax.nn.sigmoid(gates[:, units : 2 * units] + rec[:, units : 2 * units])
    recur = rec[:, 2 * units :] + rec_bias
    cand = jnp.tanh(gates[:, 2 * units :] + reset * recur)
    stepped = (1.0 - update) * cand + update * previous
    return update, reset, recur, cand, stepped


def entering_state(first, maps):
    mine = lax.axis_index("tm")
    state = first
    for back in range(len(maps), 0, -1):
        state = jnp.where(mine >= back, through(state, maps[back - 1]), state)
    return state


def through(state, one_map):
    units = state.shape[1]
    column = as_column(state - one_map[units + 1 : units + 2, :])
    return row_times(column, one_map[:units, :]) + one_map[units : units + 1, :]


def fold(parts, prev_ref, weight_ref, coef_refs, mats_ref, vecs_ref, map_ref):
    update, reset, recur, cand, stepped = parts
    steps, units = update.shape
    previous = prev_ref[...]
    update_ref, coef_update_ref, coef_reset_ref, coef_cand_ref, step_ref = coef_refs
    common = (1.0 - update) * (1.0 - cand * cand)
    update_ref[...] = update
    coef_update_ref[...] = (previous - cand) * update * (1.0 - update)
    coef_reset_ref[...] = common * recur * reset * (1.0 - reset)
    coef_cand_ref[...] = common * reset
    step_ref[...] = stepped
    row = lax.broadcasted_iota(jnp.int32, (units, units), 0)
    col = lax.broadcasted_iota(jnp.int32, (units, units), 1)

    def slope(t):
        return (
            weight_ref[:, :units] * coef_update_ref[t : t + 1, :]
            + weight_ref[:, units : 2 * units] * coef_reset_ref[t : t + 1, :]
            + weight_ref[:, 2 * units :] * coef_cand_ref[t : t + 1, :]
        )

    def stacked(mat, vec):
        return jnp.concatenate([mat, jnp.broadcast_to(vec, (PAD, units))], axis=0)

    blocks = steps // BLOCK
    for inner in range(BLOCK):
        for block in range(blocks):
            t = block * BLOCK + inner
            keep = update_ref[t : t + 1, :]
            if inner == 0:
                mat = slope(t) + jnp.where(row == col, keep, 0.0)
                vec = step_ref[t : t + 1, :]
            else:
                before = stacked(mats_ref[t - 1], vecs_ref[t - 1 : t, :] - prev_ref[t : t + 1, :])
                after = product(before, slope(t)) + before * keep
                mat = after[:units]
                vec = after[units : units + 1] + step_ref[t : t + 1, :]
            mats_ref[t] = mat
            vecs_ref[t : t + 1, :] = vec

    items = [(b * BLOCK, (b + 1) * BLOCK - 1) for b in range(blocks)]
    free = steps
    while len(items) > 1:
        joined = []
        for (first, early), (second, late) in zip(items[0::2], items[1::2]):
            before = stacked(mats_ref[early], vecs_ref[early : early + 1, :] - prev_ref[second : second + 1, :])
            after = product(before, mats_ref[late])
            mats_ref[free] = after[:units]
            vecs_ref[free : free + 1, :] = after[units : units + 1] + vecs_ref[late : late + 1, :]
            joined.append((first, free))
            free += 1
        items = joined
    last = items[0][1]
    map_ref[:units, :] = mats_ref[last]
    map_ref[units : units + 1, :] = vecs_ref[last : last + 1, :]
    map_ref[units + 1 : units + 2, :] = prev_ref[0:1, :]
    map_ref[units + 2 :, :] = jnp.zeros((6, units), F32)


def unfold(entering, prev_ref, mats_ref, vecs_ref, out_ref):
    steps = prev_ref.shape[0]
    blocks = steps // BLOCK
    starts = {0: entering}
    slots = {(b, 1): (b + 1) * BLOCK - 1 for b in range(blocks)}
    free, span = steps, 2
    while span <= blocks:
        for b in range(0, blocks, span):
            slots[(b, span)] = free
            free += 1
        span *= 2
    columns = {}
    for b in range(blocks):
        pass
    order = sorted(range(blocks), key=lambda b: (bin(b).count("1"), b))
    for b in order:
        t = b * BLOCK
        column = as_column(starts[b] - prev_ref[t : t + 1, :])
        span = 2
        while b % span == 0 and b + span < blocks:
            slot = slots[(b, span)]
            starts[b + span] = row_times(column, mats_ref[slot]) + vecs_ref[slot : slot + 1, :]
            span *= 2
        for inner in range(BLOCK):
            state = row_times(column, mats_ref[t + inner]) + vecs_ref[t + inner : t + inner + 1, :]
            out_ref[t + inner : t + inner + 1, :] = state
        if b % 2 == 0 and b + 1 < blocks:
            starts[b + 1] = state


def shift_in(entering, states_ref, prev_ref):
    steps = states_ref.shape[0]
    prev_ref[0:1, :] = entering
    prev_ref[1:steps, :] = states_ref[0 : steps - 1, :]


def weighted_square(states, stepped):
    steps = states.shape[0]
    mine, count = lax.axis_index("tm"), lax.axis_size("tm")
    position = mine * steps + lax.broadcasted_iota(jnp.int32, states.shape, 0)
    weights = (position.astype(F32) + 1.0) / (steps * count)
    return jnp.sum(weights * (states - stepped) ** 2, axis=(0, 1), keepdims=True)


def first_kernel(
    inputs_ref, start_ref, in_weight_ref, weight_ref, update_bias_ref, reset_bias_ref,
    cand_bias_ref, rec_bias_ref,
    gates_ref, prev_ref, mats_ref, vecs_ref, map_ref, *coef_refs
):
    steps, units = prev_ref.shape
    gates = jnp.dot(inputs_ref[...], in_weight_ref[...], preferred_element_type=F32)
    bias = jnp.concatenate([update_bias_ref[...], reset_bias_ref[...], cand_bias_ref[...]], axis=1)
    gates = gates + bias
    gates_ref[...] = gates
    at_start = (lax.axis_index("tm") == 0) & (lax.broadcasted_iota(jnp.int32, (steps, units), 0) == 0)
    previous = jnp.where(at_start, start_ref[...], 0.0)
    prev_ref[...] = previous
    parts = cell(gates, previous, weight_ref[...], rec_bias_ref[...])
    fold(parts, prev_ref, weight_ref, coef_refs, mats_ref, vecs_ref, map_ref)


def hop_kernel(start_ref, arrived_ref, map_ref, *refs):
    maps, sent_ref = refs[:-1], refs[-1]
    first = jnp.where(lax.axis_index("tm") < WINDOW, start_ref[...], arrived_ref[0:1, :])
    state = through(entering_state(first, maps), map_ref)
    sent_ref[...] = jnp.broadcast_to(state, sent_ref.shape)


def next_kernel(
    last, near, start_ref, arrived_ref, gates_ref, old_prev_ref, old_mats_ref, old_vecs_ref, weight_ref,
    rec_bias_ref, sums_ref, *refs
):
    maps, refs = refs[:near], refs[near:]
    if last:
        states_ref, new_sums_ref, prev_ref = refs
    else:
        new_sums_ref, prev_ref, mats_ref, vecs_ref, map_ref, states_ref, *coef_refs = refs
    first = jnp.where(lax.axis_index("tm") < WINDOW, start_ref[...], arrived_ref[0:1, :])
    entering = entering_state(first, maps)
    unfold(entering, old_prev_ref, old_mats_ref, old_vecs_ref, states_ref)
    shift_in(entering, states_ref, prev_ref)
    parts = cell(gates_ref[...], prev_ref[...], weight_ref[...], rec_bias_ref[...])
    done = weighted_square(states_ref[...], parts[4])
    row = lax.broadcasted_iota(jnp.int32, sums_ref.shape, 0)
    new_sums_ref[...] = jnp.where(row == (1 if last else 0), done, sums_ref[...])
    if not last:
        fold(parts, prev_ref, weight_ref, coef_refs, mats_ref, vecs_ref, map_ref)


def call(kernel, args, outs, scratch=(), flops=0):
    return pl.pallas_call(
        kernel,
        out_shape=[jax.ShapeDtypeStruct(shape, F32) for shape in outs],
        in_specs=[pl.BlockSpec(memory_space=pltpu.VMEM)] * len(args),
        out_specs=[pl.BlockSpec(memory_space=pltpu.VMEM)] * len(outs),
        scratch_shapes=[pltpu.VMEM(shape, F32) for shape in scratch],
        compiler_params=pltpu.CompilerParams(vmem_limit_bytes=32 * 1024 * 1024),
    )(*args)


def shifted(value, by):
    count = lax.axis_size("tm")
    return lax.ppermute(value, "tm", [(i, i + by) for i in range(count - by)])


def summed(value):
    for axis in ("batch", "tm"):
        count, by = lax.axis_size(axis), 1
        while by < count:
            value = value + lax.ppermute(value, axis, [(i, i ^ by) for i in range(count)])
            by *= 2
    return value


def carry(start, own_map):
    count = lax.axis_size("tm")
    units = start.shape[1]
    maps = [shifted(own_map, back) for back in range(1, min(WINDOW, count))]
    arrived = jnp.zeros((8, units), F32)
    for hop in range(-(-count // WINDOW) - 1):
        (sent,) = call(hop_kernel, [start, arrived, own_map, *maps], [(8, units)])
        arrived = shifted(sent, WINDOW)
    return arrived, maps


def per_device(
    inputs, h_start, in_weight, rec_weight, update_bias, reset_bias, cand_bias, rec_bias
):
    steps, sequences = inputs.shape[0], inputs.shape[1]
    units = rec_weight.shape[0]
    row = lambda value: value.reshape(1, units)
    start = h_start
    slots = steps + steps // BLOCK
    rows = (steps, units)
    fold_outs = [rows, (slots, units, units), (slots, units), (units + 8, units)]
    coefs = [rows] * 5
    gates, prev, mats, vecs, own_map = call(
        first_kernel,
        [inputs.reshape(steps, -1), start, in_weight, rec_weight, row(update_bias), row(reset_bias),
         row(cand_bias), row(rec_bias)],
        [(steps, 3 * units)] + fold_outs,
        coefs,
    )
    sums = jnp.zeros((8, units), F32)
    for newton in range(ITERS):
        last = newton == ITERS - 1
        arrived, maps = carry(start, own_map)
        args = [start, arrived, gates, prev, mats, vecs, rec_weight, row(rec_bias), sums, *maps]
        kernel = functools.partial(next_kernel, last, len(maps))
        if last:
            states, sums = call(kernel, args, [rows, (8, units)], [rows])
        else:
            sums, prev, mats, vecs, own_map = call(
                kernel, args, [(8, units)] + fold_outs, [rows] + coefs
            )
    totals = summed(sums)[:ITERS, 0]
    denom = lax.axis_size("batch") * sequences * units * (steps * lax.axis_size("tm") + 1) / 2.0
    residual_norms = jnp.sqrt(totals / denom + 1e-06)
    return (states.reshape(steps, sequences, units), residual_norms)


def solution(mesh):
    in_specs = (P("tm", "batch", None), P("batch", None), P(), P(), P(), P(), P(), P())
    out_specs = (P("tm", "batch", None), P())
    return jax.shard_map(
        per_device, mesh=mesh, in_specs=in_specs, out_specs=out_specs, check_vma=False
    )
```

time: 191 us -> 71.3 us (0.37)
  blocking collectives: 144 us -> 0 us
  starting transfers between devices: 2.76 us -> 36.2 us
  matrix products: 31.1 us -> 0 us
  waiting for transfers between devices: 2.35 us -> 18.5 us
  Pallas kernels: 0 us -> 7.25 us
  other arithmetic: 7.66 us -> 0.65 us
  local copies, waits for them, and re-layouts: 1.72 us -> 7.37 us
    all_gather x4 -> x0, blocking collectives: 103 us -> none  [carried_in(): pieces = jax.tree.map(lambda part: lax.all_gather(part, axis), value)]
    psum x1 -> x0, blocking collectives: 40.5 us -> none  [record(): return lax.psum(local_sum, ('tm', 'batch'))]
    ppermute x2 -> x13, starting transfers between devices: 2.76 us -> 36.2 us  [the longest x8 31.6 us: shifted(): return lax.ppermute(value, 'tm', [(i, i + by) for i in range(count - by)])]
    dot_general x90 -> x0, matrix products: 31.1 us -> none  [the longest x24 9.4 us: combine(): jnp.einsum('...ij,...jk->...ik', mat_early, mat_late, precision=HIGH)]
    ppermute x2 -> x13, waiting for transfers between devices: 2.35 us -> 18.5 us  [the longest x5 12.1 us: summed(): lax.ppermute(value, axis, [(i, i ^ by) for i in range(count)])]
    unnamed x24 -> x22, local copies, waits for them, and re-layouts: 0.06 us -> 7.37 us
    pallas_call x0 -> x5, Pallas kernels: none -> 7.25 us  [call(): pl.pallas_call(kernel, out_shape=[jax.ShapeDtypeStruct(shape, F32) for sh...]
    add x16 -> x5, other arithmetic: 2.48 us -> 0.02 us  [summed(): value + lax.ppermute(value, axis, [(i, i ^ by) for i in range(count)])]
  transfers between devices with their start and end apart: 2 -> 13, of which waited for: 2 -> 9; matrix products, arithmetic and copies ran while one was open for 0% -> 0% of each run, Pallas kernels for 0% -> 0%
where the time goes in v1:
time: 71.3 us; the launch traced here: 70.8 us
  starting transfers between devices  36.2 us (51%)
  waiting for transfers between devices  18.5 us (26%)
  local copies, waits for them, and re-layouts  7.37 us (10%)
  Pallas kernels  7.25 us (10%)
  between operations  0.77 us (1%)
    ppermute x8, starting transfers between devices, shifted(): return lax.ppermute(value, 'tm', [(i, i + by) for i in range(count - by)])  31.6 us
    ppermute x5, waiting for transfers between devices, summed(): lax.ppermute(value, axis, [(i, i ^ by) for i in range(count)])  12.1 us
    unnamed x22, local copies, waits for them, and re-layouts  7.37 us
    pallas_call x5, Pallas kernels, call(): pl.pallas_call(kernel, out_shape=[jax.ShapeDtypeStruct(shape, F32) for sh...  7.25 us
    ppermute x8, waiting for transfers between devices, shifted(): return lax.ppermute(value, 'tm', [(i, i + by) for i in range(count - by)])  6.43 us
    ppermute x5, starting transfers between devices, summed(): lax.ppermute(value, axis, [(i, i ^ by) for i in range(count)])  4.66 us
  transfers between devices with their start and end apart: 13, of which 9 were waited for; matrix products, arithmetic and copies ran while one was open for 0% of the time, Pallas kernels for 0%

profile of v1, /device:TPU:0, one launch (start us, length us, event | category | flops | bytes accessed | tf_op | source)
XLA Modules:
  0.0 70.8 jit_solution(13233361233752849041)
XLA Ops:
  0.6 0.0 copy-start
  0.6 0.9 %copy-done = f32[128,384]{1,0:T(8,128)S(1)} copy-done((f32[128,384]{1,0:T(8,128)S(1)}, f32[128,384]{1,0:T(8,128)}, u32[]{:S(2)}) %copy-start) | copy-done | bytes 196632
  1.6 0.0 copy-start.3
  1.6 0.9 %copy-done.3 = bf16[128,384]{1,0:T(8,128)(2,1)S(1)} copy-done((bf16[128,384]{1,0:T(8,128)(2,1)S(1)}, bf16[128,384]{1,0:T(8,128)(2,1)}, u32[]{:S(2)}) %copy-start.3) | copy-done | bytes 98328
  2.5 0.0 copy-start.4
  2.5 0.7 copy-done.4
  3.1 0.0 copy-start.6
  3.1 0.7 copy-done.6
  3.8 0.0 copy-start.7
  3.8 0.7 copy-done.7
  4.5 0.0 copy-start.8
  4.5 0.7 copy-done.8
  5.1 0.0 copy-start.9
  5.1 0.7 copy-done.9
  5.8 0.0 copy-start.10
  5.8 0.7 copy-done.10
  6.4 0.0 copy-start.2
  6.4 1.9 %shard_map.95 = (f32[32,384]{1,0:T(8,128)S(1)}, f32[32,128]{1,0:T(8,128)S(1)}, f32[40,128,128]{2,1,0:T(8,128)S(1)}, f32[40,128]{1,0:T(8,128)S(1)}, f32[136,128]{1,0:T(8,128)S(1)}) custom-call(bf16[32,128]{1,0:T(8,128)(2,1)S(1)} %bitcast.8, f32[1,128]{1,0:T(1,128)S(1)} %copy-done.4, bf16[128,384]{1,0:T(8,128)(2,1)S(1)} %copy-done.3, f32[128,384]{1,0:T(8,128)S(1)} %copy-done, ...), custom_call_target="tpu_custom_call" | custom-call | tf_op jit(solution)/shard_map/pallas_call | solution.py:221
  8.4 5.9 %collective-permute-start.2 = (f32[136,128]{1,0:T(8,128)S(1)}, f32[136,128]{1,0:T(8,128)S(1)}, u32[]{:S(2)}, u32[]{:S(2)}) collective-permute-start(f32[136,128]{1,0:T(8,128)S(1)} %get-tuple-element.14.map_ref), channel_id=1, source_target_pairs={{0,12},{4,16},{8,20},{12,24},{16,28},{1,13},{5,17},{9,21},{13,25},... | collective-permute-start | bytes 208904 | tf_op jit(solution)/shard_map/ppermute | solution.py:233
  14.3 3.5 %collective-permute-start.1 = (f32[136,128]{1,0:T(8,128)S(1)}, f32[136,128]{1,0:T(8,128)S(1)}, u32[]{:S(2)}, u32[]{:S(2)}) collective-permute-start(f32[136,128]{1,0:T(8,128)S(1)} %get-tuple-element.14.map_ref), channel_id=1, source_target_pairs={{0,8},{4,12},{8,16},{12,20},{16,24},{20,28},{1,9},{5,13},{9,17},{1... | collective-permute-start | bytes 208904 | tf_op jit(solution)/shard_map/ppermute | solution.py:233
  17.7 3.4 %collective-permute-start = (f32[136,128]{1,0:T(8,128)S(1)}, f32[136,128]{1,0:T(8,128)S(1)}, u32[]{:S(2)}, u32[]{:S(2)}) collective-permute-start(f32[136,128]{1,0:T(8,128)S(1)} %get-tuple-element.14.map_ref), channel_id=1, source_target_pairs={{0,4},{4,8},{8,12},{12,16},{16,20},{20,24},{24,28},{1,5},{5,9},{9,... | collective-permute-start | bytes 208904 | tf_op jit(solution)/shard_map/ppermute | solution.py:233
  21.2 0.0 collective-permute-done.2.refs_2_
  21.2 0.0 collective-permute-done.1.refs_1_
  21.2 1.9 %collective-permute-done.refs_0_ = f32[136,128]{1,0:T(8,128)S(1)} collective-permute-done((f32[136,128]{1,0:T(8,128)S(1)}, f32[136,128]{1,0:T(8,128)S(1)}, u32[]{:S(2)}, u32[]{:S(2)}) %collective-permute-start) | collective-permute-done | bytes 69664 | tf_op jit(solution)/shard_map/ppermute | solution.py:233
  23.1 0.4 shard_map.96
  23.6 4.7 %collective-permute-start.3 = (f32[8,128]{1,0:T(8,128)S(1)}, f32[8,128]{1,0:T(8,128)S(1)}, u32[]{:S(2)}, u32[]{:S(2)}) collective-permute-start(f32[8,128]{1,0:T(8,128)S(1)} %shard_map.96), channel_id=1, source_target_pairs={{0,16},{4,20},{8,24},{12,28},{1,17},{5,21},{9,25},{13,29},{2,18},{... | collective-permute-start | bytes 12296 | tf_op jit(solution)/shard_map/ppermute | solution.py:233
  28.2 1.3 %collective-permute-done.3.arrived_ref = f32[8,128]{1,0:T(8,128)S(1)} collective-permute-done((f32[8,128]{1,0:T(8,128)S(1)}, f32[8,128]{1,0:T(8,128)S(1)}, u32[]{:S(2)}, u32[]{:S(2)}) %collective-permute-start.3) | collective-permute-done | bytes 4128 | tf_op jit(solution)/shard_map/ppermute | solution.py:233
  29.6 0.0 copy-start.1
  29.6 0.9 %copy-done.1 = f32[128,384]{1,0:T(8,128)S(1)} copy-done((f32[128,384]{1,0:T(8,128)S(1)}, f32[128,384]{1,0:T(8,128)}, u32[]{:S(2)}) %copy-start.1) | copy-done | bytes 196632
  30.5 0.0 copy-start.5
  30.5 0.7 copy-done.5
  31.1 2.8 %shard_map.97 = (f32[8,128]{1,0:T(8,128)S(1)}, f32[32,128]{1,0:T(8,128)S(1)}, f32[40,128,128]{2,1,0:T(8,128)S(1)}, f32[40,128]{1,0:T(8,128)S(1)}, f32[136,128]{1,0:T(8,128)S(1)}) custom-call(f32[1,128]{1,0:T(1,128)S(1)} %copy-done.5, f32[8,128]{1,0:T(8,128)S(1)} %collective-permute-done.3.arrived_ref, f32[32,384]{1,0:T(8,128)S(1)} %get-tuple-element.15.gates_ref, ...), custom_call_target="tpu_custom_call" | custom-call | tf_op jit(solution)/shard_map/pallas_call | solution.py:221
  33.9 1.3 %collective-permute-start.6 = (f32[136,128]{1,0:T(8,128)S(1)}, f32[136,128]{1,0:T(8,128)S(1)}, u32[]{:S(2)}, u32[]{:S(2)}) collective-permute-start(f32[136,128]{1,0:T(8,128)S(1)} %get-tuple-element.19.map_ref), channel_id=1, source_target_pairs={{0,12},{4,16},{8,20},{12,24},{16,28},{1,13},{5,17},{9,21},{13,25},... | collective-permute-start | bytes 208904 | tf_op jit(solution)/shard_map/ppermute | solution.py:233
  35.2 4.8 %collective-permute-start.5 = (f32[136,128]{1,0:T(8,128)S(1)}, f32[136,128]{1,0:T(8,128)S(1)}, u32[]{:S(2)}, u32[]{:S(2)}) collective-permute-start(f32[136,128]{1,0:T(8,128)S(1)} %get-tuple-element.19.map_ref), channel_id=1, source_target_pairs={{0,8},{4,12},{8,16},{12,20},{16,24},{20,28},{1,9},{5,13},{9,17},{1... | collective-permute-start | bytes 208904 | tf_op jit(solution)/shard_map/ppermute | solution.py:233
  40.1 4.2 %collective-permute-start.4 = (f32[136,128]{1,0:T(8,128)S(1)}, f32[136,128]{1,0:T(8,128)S(1)}, u32[]{:S(2)}, u32[]{:S(2)}) collective-permute-start(f32[136,128]{1,0:T(8,128)S(1)} %get-tuple-element.19.map_ref), channel_id=1, source_target_pairs={{0,4},{4,8},{8,12},{12,16},{16,20},{20,24},{24,28},{1,5},{5,9},{9,... | collective-permute-start | bytes 208904 | tf_op jit(solution)/shard_map/ppermute | solution.py:233
  44.3 0.0 collective-permute-done.6.refs_2_
  44.3 0.0 collective-permute-done.5.refs_1_
  44.3 1.9 %collective-permute-done.4.refs_0_ = f32[136,128]{1,0:T(8,128)S(1)} collective-permute-done((f32[136,128]{1,0:T(8,128)S(1)}, f32[136,128]{1,0:T(8,128)S(1)}, u32[]{:S(2)}, u32[]{:S(2)}) %collective-permute-start.4) | collective-permute-done | bytes 69664 | tf_op jit(solution)/shard_map/ppermute | solution.py:233
  46.2 0.4 shard_map.98
  46.6 3.8 %collective-permute-start.7 = (f32[8,128]{1,0:T(8,128)S(1)}, f32[8,128]{1,0:T(8,128)S(1)}, u32[]{:S(2)}, u32[]{:S(2)}) collective-permute-start(f32[8,128]{1,0:T(8,128)S(1)} %shard_map.98), channel_id=1, source_target_pairs={{0,16},{4,20},{8,24},{12,28},{1,17},{5,21},{9,25},{13,29},{2,18},{... | collective-permute-start | bytes 12296 | tf_op jit(solution)/shard_map/ppermute | solution.py:233
  50.4 1.3 %collective-permute-done.7.arrived_ref = f32[8,128]{1,0:T(8,128)S(1)} collective-permute-done((f32[8,128]{1,0:T(8,128)S(1)}, f32[8,128]{1,0:T(8,128)S(1)}, u32[]{:S(2)}, u32[]{:S(2)}) %collective-permute-start.7) | collective-permute-done | bytes 4128 | tf_op jit(solution)/shard_map/ppermute | solution.py:233
  51.7 0.0 copy-done.2
  51.7 1.6 %shard_map.99 = (f32[32,128]{1,0:T(8,128)}, f32[8,128]{1,0:T(8,128)S(1)}) custom-call(f32[1,128]{1,0:T(1,128)S(1)} %copy-done.5, f32[8,128]{1,0:T(8,128)S(1)} %collective-permute-done.7.arrived_ref, f32[32,384]{1,0:T(8,128)S(1)} %get-tuple-element.15.gates_ref, f32[32,128]{1,0:T(8,128)S(1)} %get-tuple-element.20.old_prev_ref, ...), custom_call_target="tpu_custom_call" | custom-call | tf_op jit(solution)/shard_map/pallas_call | solution.py:221
  53.4 0.0 collective-permute-start.8
  53.4 1.2 %collective-permute-done.8 = f32[8,128]{1,0:T(8,128)S(1)} collective-permute-done((f32[8,128]{1,0:T(8,128)S(1)}, f32[8,128]{1,0:T(8,128)S(1)}, u32[]{:S(2)}, u32[]{:S(2)}) %collective-permute-start.8) | collective-permute-done | bytes 4128 | tf_op jit(solution)/shard_map/ppermute | solution.py:240
  54.6 1.5 %collective-permute-start.9 = (f32[8,128]{1,0:T(8,128)S(1)}, f32[8,128]{1,0:T(8,128)S(1)}, u32[]{:S(2)}, u32[]{:S(2)}) collective-permute-start(f32[8,128]{1,0:T(8,128)S(1)} %add.19), channel_id=1, source_target_pairs={{0,2},{1,3},{2,0},{3,1},{4,6},{5,7},{6,4},{7,5},{8,10},{9,11},{10,... | collective-permute-start | bytes 12296 | tf_op jit(solution)/shard_map/ppermute | solution.py:240
  56.0 2.1 %collective-permute-done.9 = f32[8,128]{1,0:T(8,128)S(1)} collective-permute-done((f32[8,128]{1,0:T(8,128)S(1)}, f32[8,128]{1,0:T(8,128)S(1)}, u32[]{:S(2)}, u32[]{:S(2)}) %collective-permute-start.9) | collective-permute-done | bytes 4128 | tf_op jit(solution)/shard_map/ppermute | solution.py:240
  58.2 0.0 collective-permute-start.10
  58.2 3.6 %collective-permute-done.10 = f32[8,128]{1,0:T(8,128)S(1)} collective-permute-done((f32[8,128]{1,0:T(8,128)S(1)}, f32[8,128]{1,0:T(8,128)S(1)}, u32[]{:S(2)}, u32[]{:S(2)}) %collective-permute-start.10) | collective-permute-done | bytes 4128 | tf_op jit(solution)/shard_map/ppermute | solution.py:240
  61.8 0.0 collective-permute-start.11
  61.8 3.6 %collective-permute-done.11 = f32[8,128]{1,0:T(8,128)S(1)} collective-permute-done((f32[8,128]{1,0:T(8,128)S(1)}, f32[8,128]{1,0:T(8,128)S(1)}, u32[]{:S(2)}, u32[]{:S(2)}) %collective-permute-start.11) | collective-permute-done | bytes 4128 | tf_op jit(solution)/shard_map/ppermute | solution.py:240
  65.4 3.2 %collective-permute-start.12 = (f32[8,128]{1,0:T(8,128)S(1)}, f32[8,128]{1,0:T(8,128)S(1)}, u32[]{:S(2)}, u32[]{:S(2)}) collective-permute-start(f32[8,128]{1,0:T(8,128)S(1)} %add.22), channel_id=1, source_target_pairs={{0,16},{4,20},{8,24},{12,28},{16,0},{20,4},{24,8},{28,12},{1,17},{... | collective-permute-start | bytes 12296 | tf_op jit(solution)/shard_map/ppermute | solution.py:240
  68.6 1.6 %collective-permute-done.12 = f32[8,128]{1,0:T(8,128)S(1)} collective-permute-done((f32[8,128]{1,0:T(8,128)S(1)}, f32[8,128]{1,0:T(8,128)S(1)}, u32[]{:S(2)}, u32[]{:S(2)}) %collective-permute-start.12) | collective-permute-done | bytes 4128 | tf_op jit(solution)/shard_map/ppermute | solution.py:240
  70.2 0.6 sqrt_reduce_fusion
  (6 shorter events, 0.0 us)
Async XLA Ops:
  0.6 0.9 %copy-start = (f32[128,384]{1,0:T(8,128)S(1)}, f32[128,384]{1,0:T(8,128)}, u32[]{:S(2)}) copy-start(f32[128,384]{1,0:T(8,128)} %weight_ref.5) | copy-start | bytes 589828
  1.6 0.9 %copy-start.3 = (bf16[128,384]{1,0:T(8,128)(2,1)S(1)}, bf16[128,384]{1,0:T(8,128)(2,1)}, u32[]{:S(2)}) copy-start(bf16[128,384]{1,0:T(8,128)(2,1)} %in_weight_ref.1) | copy-start | bytes 294916
  2.5 0.7 copy-start.4
  3.1 0.7 copy-start.6
  3.8 0.7 copy-start.7
  4.5 0.7 copy-start.8
  5.1 0.7 copy-start.9
  5.8 0.7 copy-start.10
  6.4 45.3 %copy-start.2 = (f32[128,384]{1,0:T(8,128)S(1)}, f32[128,384]{1,0:T(8,128)}, u32[]{:S(2)}) copy-start(f32[128,384]{1,0:T(8,128)} %weight_ref.5) | copy-start | bytes 589828
  8.4 12.8 %collective-permute-start.2 = (f32[136,128]{1,0:T(8,128)S(1)}, f32[136,128]{1,0:T(8,128)S(1)}, u32[]{:S(2)}, u32[]{:S(2)}) collective-permute-start(f32[136,128]{1,0:T(8,128)S(1)} %get-tuple-element.14.map_ref), channel_id=1, source_target_pairs={{0,12},{4,16},{8,20},{12,24},{16,28},{1,13},{5,17},{9,21},{13,25},... | collective-permute-start | bytes 208904 | tf_op jit(solution)/shard_map/ppermute | solution.py:233
  14.3 6.9 %collective-permute-start.1 = (f32[136,128]{1,0:T(8,128)S(1)}, f32[136,128]{1,0:T(8,128)S(1)}, u32[]{:S(2)}, u32[]{:S(2)}) collective-permute-start(f32[136,128]{1,0:T(8,128)S(1)} %get-tuple-element.14.map_ref), channel_id=1, source_target_pairs={{0,8},{4,12},{8,16},{12,20},{16,24},{20,28},{1,9},{5,13},{9,17},{1... | collective-permute-start | bytes 208904 | tf_op jit(solution)/shard_map/ppermute | solution.py:233
  17.7 5.4 %collective-permute-start = (f32[136,128]{1,0:T(8,128)S(1)}, f32[136,128]{1,0:T(8,128)S(1)}, u32[]{:S(2)}, u32[]{:S(2)}) collective-permute-start(f32[136,128]{1,0:T(8,128)S(1)} %get-tuple-element.14.map_ref), channel_id=1, source_target_pairs={{0,4},{4,8},{8,12},{12,16},{16,20},{20,24},{24,28},{1,5},{5,9},{9,... | collective-permute-start | bytes 208904 | tf_op jit(solution)/shard_map/ppermute | solution.py:233
  23.6 6.0 %collective-permute-start.3 = (f32[8,128]{1,0:T(8,128)S(1)}, f32[8,128]{1,0:T(8,128)S(1)}, u32[]{:S(2)}, u32[]{:S(2)}) collective-permute-start(f32[8,128]{1,0:T(8,128)S(1)} %shard_map.96), channel_id=1, source_target_pairs={{0,16},{4,20},{8,24},{12,28},{1,17},{5,21},{9,25},{13,29},{2,18},{... | collective-permute-start | bytes 12296 | tf_op jit(solution)/shard_map/ppermute | solution.py:233
  29.6 0.9 %copy-start.1 = (f32[128,384]{1,0:T(8,128)S(1)}, f32[128,384]{1,0:T(8,128)}, u32[]{:S(2)}) copy-start(f32[128,384]{1,0:T(8,128)} %weight_ref.5) | copy-start | bytes 589828
  30.5 0.7 copy-start.5
  33.9 10.3 %collective-permute-start.6 = (f32[136,128]{1,0:T(8,128)S(1)}, f32[136,128]{1,0:T(8,128)S(1)}, u32[]{:S(2)}, u32[]{:S(2)}) collective-permute-start(f32[136,128]{1,0:T(8,128)S(1)} %get-tuple-element.19.map_ref), channel_id=1, source_target_pairs={{0,12},{4,16},{8,20},{12,24},{16,28},{1,13},{5,17},{9,21},{13,25},... | collective-permute-start | bytes 208904 | tf_op jit(solution)/shard_map/ppermute | solution.py:233
  35.2 9.0 %collective-permute-start.5 = (f32[136,128]{1,0:T(8,128)S(1)}, f32[136,128]{1,0:T(8,128)S(1)}, u32[]{:S(2)}, u32[]{:S(2)}) collective-permute-start(f32[136,128]{1,0:T(8,128)S(1)} %get-tuple-element.19.map_ref), channel_id=1, source_target_pairs={{0,8},{4,12},{8,16},{12,20},{16,24},{20,28},{1,9},{5,13},{9,17},{1... | collective-permute-start | bytes 208904 | tf_op jit(solution)/shard_map/ppermute | solution.py:233
  40.1 6.1 %collective-permute-start.4 = (f32[136,128]{1,0:T(8,128)S(1)}, f32[136,128]{1,0:T(8,128)S(1)}, u32[]{:S(2)}, u32[]{:S(2)}) collective-permute-start(f32[136,128]{1,0:T(8,128)S(1)} %get-tuple-element.19.map_ref), channel_id=1, source_target_pairs={{0,4},{4,8},{8,12},{12,16},{16,20},{20,24},{24,28},{1,5},{5,9},{9,... | collective-permute-start | bytes 208904 | tf_op jit(solution)/shard_map/ppermute | solution.py:233
  46.6 5.1 %collective-permute-start.7 = (f32[8,128]{1,0:T(8,128)S(1)}, f32[8,128]{1,0:T(8,128)S(1)}, u32[]{:S(2)}, u32[]{:S(2)}) collective-permute-start(f32[8,128]{1,0:T(8,128)S(1)} %shard_map.98), channel_id=1, source_target_pairs={{0,16},{4,20},{8,24},{12,28},{1,17},{5,21},{9,25},{13,29},{2,18},{... | collective-permute-start | bytes 12296 | tf_op jit(solution)/shard_map/ppermute | solution.py:233
  53.4 1.2 %collective-permute-start.8 = (f32[8,128]{1,0:T(8,128)S(1)}, f32[8,128]{1,0:T(8,128)S(1)}, u32[]{:S(2)}, u32[]{:S(2)}) collective-permute-start(f32[8,128]{1,0:T(8,128)S(1)} %get-tuple-element.25), channel_id=1, source_target_pairs={{0,1},{1,0},{2,3},{3,2},{4,5},{5,4},{6,7},{7,6},{8,9},{9,8},{10,11... | collective-permute-start | bytes 12296 | tf_op jit(solution)/shard_map/ppermute | solution.py:240
  54.6 3.6 %collective-permute-start.9 = (f32[8,128]{1,0:T(8,128)S(1)}, f32[8,128]{1,0:T(8,128)S(1)}, u32[]{:S(2)}, u32[]{:S(2)}) collective-permute-start(f32[8,128]{1,0:T(8,128)S(1)} %add.19), channel_id=1, source_target_pairs={{0,2},{1,3},{2,0},{3,1},{4,6},{5,7},{6,4},{7,5},{8,10},{9,11},{10,... | collective-permute-start | bytes 12296 | tf_op jit(solution)/shard_map/ppermute | solution.py:240
  58.2 3.6 %collective-permute-start.10 = (f32[8,128]{1,0:T(8,128)S(1)}, f32[8,128]{1,0:T(8,128)S(1)}, u32[]{:S(2)}, u32[]{:S(2)}) collective-permute-start(f32[8,128]{1,0:T(8,128)S(1)} %add.20), channel_id=1, source_target_pairs={{0,4},{4,0},{8,12},{12,8},{16,20},{20,16},{24,28},{28,24},{1,5},{5... | collective-permute-start | bytes 12296 | tf_op jit(solution)/shard_map/ppermute | solution.py:240
  61.8 3.6 %collective-permute-start.11 = (f32[8,128]{1,0:T(8,128)S(1)}, f32[8,128]{1,0:T(8,128)S(1)}, u32[]{:S(2)}, u32[]{:S(2)}) collective-permute-start(f32[8,128]{1,0:T(8,128)S(1)} %add.21), channel_id=1, source_target_pairs={{0,8},{4,12},{8,0},{12,4},{16,24},{20,28},{24,16},{28,20},{1,9},{5... | collective-permute-start | bytes 12296 | tf_op jit(solution)/shard_map/ppermute | solution.py:240
  65.4 4.8 %collective-permute-start.12 = (f32[8,128]{1,0:T(8,128)S(1)}, f32[8,128]{1,0:T(8,128)S(1)}, u32[]{:S(2)}, u32[]{:S(2)}) collective-permute-start(f32[8,128]{1,0:T(8,128)S(1)} %add.22), channel_id=1, source_target_pairs={{0,16},{4,20},{8,24},{12,28},{16,0},{20,4},{24,8},{28,12},{1,17},{... | collective-permute-start | bytes 12296 | tf_op jit(solution)/shard_map/ppermute | solution.py:240

commit v2 on v1

--- a/solution.py
+++ b/solution.py
@@ -55,12 +55,18 @@
     return update, reset, recur, cand, stepped
 
 
-def entering_state(first, maps):
-    mine = lax.axis_index("tm")
+def walk(first, refs, place, stop):
     state = first
-    for back in range(len(maps), 0, -1):
-        state = jnp.where(mine >= back, through(state, maps[back - 1]), state)
+    for other in range(stop):
+        state = through(state, refs[place ^ other])
     return state
+
+
+def group_start(consts_ref, arrived_refs):
+    start = consts_ref[0:1, :]
+    if not arrived_refs:
+        return start
+    return jnp.where(lax.axis_index("tm") < WINDOW, start, arrived_refs[0][0:1, :])
 
 
 def through(state, one_map):
@@ -139,9 +145,6 @@
             slots[(b, span)] = free
             free += 1
         span *= 2
-    columns = {}
-    for b in range(blocks):
-        pass
     order = sorted(range(blocks), key=lambda b: (bin(b).count("1"), b))
     for b in order:
         t = b * BLOCK
@@ -173,14 +176,28 @@
 
 
 def first_kernel(
-    inputs_ref, start_ref, in_weight_ref, weight_ref, update_bias_ref, reset_bias_ref,
-    cand_bias_ref, rec_bias_ref,
-    gates_ref, prev_ref, mats_ref, vecs_ref, map_ref, *coef_refs
+    inputs_hbm, start_hbm, in_weight_hbm, weight_hbm, update_bias_hbm, reset_bias_hbm, cand_bias_hbm,
+    rec_bias_hbm,
+    gates_ref, prev_ref, mats_ref, vecs_ref, map_ref, weight_ref, consts_ref,
+    inputs_ref, in_weight_ref, bias_ref, start_ref, rec_bias_ref, sems, *coef_refs
 ):
     steps, units = prev_ref.shape
-    gates = jnp.dot(inputs_ref[...], in_weight_ref[...], preferred_element_type=F32)
-    bias = jnp.concatenate([update_bias_ref[...], reset_bias_ref[...], cand_bias_ref[...]], axis=1)
-    gates = gates + bias
+    moves = [
+        (inputs_hbm, inputs_ref), (in_weight_hbm, in_weight_ref), (weight_hbm, weight_ref),
+        (update_bias_hbm, bias_ref.at[:, pl.ds(0, units)]),
+        (reset_bias_hbm, bias_ref.at[:, pl.ds(units, units)]),
+        (cand_bias_hbm, bias_ref.at[:, pl.ds(2 * units, units)]),
+        (start_hbm, start_ref), (rec_bias_hbm, rec_bias_ref),
+    ]
+    copies = [pltpu.make_async_copy(src, dst, sems.at[i]) for i, (src, dst) in enumerate(moves)]
+    for copy in copies:
+        copy.start()
+    for copy in copies:
+        copy.wait()
+    consts_ref[0:1, :] = start_ref[...]
+    consts_ref[1:2, :] = rec_bias_ref[...]
+    consts_ref[2:, :] = jnp.zeros((6, units), F32)
+    gates = jnp.dot(inputs_ref[...], in_weight_ref[...], preferred_element_type=F32) + bias_ref[...]
     gates_ref[...] = gates
     at_start = (lax.axis_index("tm") == 0) & (lax.broadcasted_iota(jnp.int32, (steps, units), 0) == 0)
     previous = jnp.where(at_start, start_ref[...], 0.0)
@@ -189,67 +206,84 @@
     fold(parts, prev_ref, weight_ref, coef_refs, mats_ref, vecs_ref, map_ref)
 
 
-def hop_kernel(start_ref, arrived_ref, map_ref, *refs):
-    maps, sent_ref = refs[:-1], refs[-1]
-    first = jnp.where(lax.axis_index("tm") < WINDOW, start_ref[...], arrived_ref[0:1, :])
-    state = through(entering_state(first, maps), map_ref)
-    sent_ref[...] = jnp.broadcast_to(state, sent_ref.shape)
-
-
-def next_kernel(
-    last, near, start_ref, arrived_ref, gates_ref, old_prev_ref, old_mats_ref, old_vecs_ref, weight_ref,
-    rec_bias_ref, sums_ref, *refs
-):
-    maps, refs = refs[:near], refs[near:]
+def hop_kernel(held, consts_ref, *refs):
+    maps, arrived, sent_ref = refs[:held], refs[held:-1], refs[-1]
+    first = group_start(consts_ref, arrived)
+    place = lax.rem(lax.axis_index("tm"), held)
+    for mine in range(held):
+
+        @pl.when(place == mine)
+        def _():
+            state = walk(first, maps, mine, held)
+            sent_ref[...] = jnp.broadcast_to(state, sent_ref.shape)
+
+
+def next_kernel(newton, held, hops, *refs):
+    last = newton == ITERS - 1
+    consts_ref, gates_ref, old_prev_ref, old_mats_ref, old_vecs_ref, weight_ref = refs[:6]
+    maps, refs = refs[6 : 6 + held], refs[6 + held :]
+    arrived, refs = refs[: min(hops, 1)], refs[min(hops, 1) :]
+    if newton > 0:
+        sums_ref, refs = refs[0], refs[1:]
     if last:
-        states_ref, new_sums_ref, prev_ref = refs
+        states_ref, new_sums_ref, prev_ref, enter_ref = refs
     else:
-        new_sums_ref, prev_ref, mats_ref, vecs_ref, map_ref, states_ref, *coef_refs = refs
-    first = jnp.where(lax.axis_index("tm") < WINDOW, start_ref[...], arrived_ref[0:1, :])
-    entering = entering_state(first, maps)
+        new_sums_ref, prev_ref, mats_ref, vecs_ref, map_ref, states_ref, enter_ref, *coef_refs = refs
+    first = group_start(consts_ref, arrived)
+    place = lax.rem(lax.axis_index("tm"), held)
+    for mine in range(held):
+
+        @pl.when(place == mine)
+        def _():
+            enter_ref[...] = walk(first, maps, mine, mine)
+
+    entering = enter_ref[...]
     unfold(entering, old_prev_ref, old_mats_ref, old_vecs_ref, states_ref)
     shift_in(entering, states_ref, prev_ref)
-    parts = cell(gates_ref[...], prev_ref[...], weight_ref[...], rec_bias_ref[...])
+    parts = cell(gates_ref[...], prev_ref[...], weight_ref[...], consts_ref[1:2, :])
     done = weighted_square(states_ref[...], parts[4])
-    row = lax.broadcasted_iota(jnp.int32, sums_ref.shape, 0)
-    new_sums_ref[...] = jnp.where(row == (1 if last else 0), done, sums_ref[...])
+    row = lax.broadcasted_iota(jnp.int32, new_sums_ref.shape, 0)
+    new_sums_ref[...] = jnp.where(row == newton, done, sums_ref[...] if newton > 0 else 0.0)
     if not last:
         fold(parts, prev_ref, weight_ref, coef_refs, mats_ref, vecs_ref, map_ref)
 
 
-def call(kernel, args, outs, scratch=(), flops=0):
+def call(kernel, args, outs, scratch=(), space=pltpu.VMEM):
+    args = [pltpu.with_memory_space_constraint(arg, space) for arg in args]
     return pl.pallas_call(
         kernel,
         out_shape=[jax.ShapeDtypeStruct(shape, F32) for shape in outs],
-        in_specs=[pl.BlockSpec(memory_space=pltpu.VMEM)] * len(args),
+        in_specs=[pl.BlockSpec(memory_space=space)] * len(args),
         out_specs=[pl.BlockSpec(memory_space=pltpu.VMEM)] * len(outs),
-        scratch_shapes=[pltpu.VMEM(shape, F32) for shape in scratch],
+        scratch_shapes=[pltpu.VMEM(one, F32) if isinstance(one, tuple) else one for one in scratch],
         compiler_params=pltpu.CompilerParams(vmem_limit_bytes=32 * 1024 * 1024),
     )(*args)
 
 
-def shifted(value, by):
-    count = lax.axis_size("tm")
-    return lax.ppermute(value, "tm", [(i, i + by) for i in range(count - by)])
-
-
-def summed(value):
-    for axis in ("batch", "tm"):
-        count, by = lax.axis_size(axis), 1
-        while by < count:
-            value = value + lax.ppermute(value, axis, [(i, i ^ by) for i in range(count)])
-            by *= 2
+def exchanged(value, axis, by):
+    return lax.ppermute(value, axis, [(i, i ^ by) for i in range(lax.axis_size(axis))])
+
+
+def summed(value, axis):
+    count, by = lax.axis_size(axis), 1
+    while by < count:
+        radix = min(8, count // by)
+        terms = [value] + [exchanged(value, axis, k * by) for k in range(1, radix)]
+        while len(terms) > 1:
+            terms = [a + b for a, b in zip(terms[0::2], terms[1::2])]
+        value = terms[0]
+        by *= radix
     return value
 
 
-def carry(start, own_map):
-    count = lax.axis_size("tm")
-    units = start.shape[1]
-    maps = [shifted(own_map, back) for back in range(1, min(WINDOW, count))]
-    arrived = jnp.zeros((8, units), F32)
-    for hop in range(-(-count // WINDOW) - 1):
-        (sent,) = call(hop_kernel, [start, arrived, own_map, *maps], [(8, units)])
-        arrived = shifted(sent, WINDOW)
+def carry(consts, own_map):
+    count, units = lax.axis_size("tm"), consts.shape[1]
+    held = min(WINDOW, count)
+    maps = [own_map] + [exchanged(own_map, "tm", k) for k in range(1, held)]
+    arrived = []
+    for hop in range(count // held - 1):
+        (sent,) = call(functools.partial(hop_kernel, held), [consts, *maps, *arrived], [(8, units)])
+        arrived = [lax.ppermute(sent, "tm", [(i, (i + held) % count) for i in range(count)])]
     return arrived, maps
 
 
@@ -259,31 +293,32 @@
     steps, sequences = inputs.shape[0], inputs.shape[1]
     units = rec_weight.shape[0]
     row = lambda value: value.reshape(1, units)
-    start = h_start
     slots = steps + steps // BLOCK
-    rows = (steps, units)
+    rows, wide = (steps, units), (steps, 3 * units)
     fold_outs = [rows, (slots, units, units), (slots, units), (units + 8, units)]
     coefs = [rows] * 5
-    gates, prev, mats, vecs, own_map = call(
+    gates, prev, mats, vecs, own_map, weight, consts = call(
         first_kernel,
-        [inputs.reshape(steps, -1), start, in_weight, rec_weight, row(update_bias), row(reset_bias),
+        [inputs.reshape(steps, -1), h_start, in_weight, rec_weight, row(update_bias), row(reset_bias),
          row(cand_bias), row(rec_bias)],
-        [(steps, 3 * units)] + fold_outs,
-        coefs,
+        [wide] + fold_outs + [rec_weight.shape, (8, units)],
+        [pltpu.VMEM((steps, in_weight.shape[0]), BF16), pltpu.VMEM(in_weight.shape, BF16), (1, 3 * units),
+         (1, units), (1, units), pltpu.SemaphoreType.DMA((8,))] + coefs,
+        space=pltpu.HBM,
     )
-    sums = jnp.zeros((8, units), F32)
+    sums = []
     for newton in range(ITERS):
-        last = newton == ITERS - 1
-        arrived, maps = carry(start, own_map)
-        args = [start, arrived, gates, prev, mats, vecs, rec_weight, row(rec_bias), sums, *maps]
-        kernel = functools.partial(next_kernel, last, len(maps))
-        if last:
-            states, sums = call(kernel, args, [rows, (8, units)], [rows])
+        arrived, maps = carry(consts, own_map)
+        args = [consts, gates, prev, mats, vecs, weight, *maps, *arrived, *sums]
+        kernel = functools.partial(next_kernel, newton, len(maps), len(arrived))
+        if newton == ITERS - 1:
+            states, total = call(kernel, args, [rows, (8, units)], [rows, (1, units)])
         else:
-            sums, prev, mats, vecs, own_map = call(
-                kernel, args, [(8, units)] + fold_outs, [rows] + coefs
+            total, prev, mats, vecs, own_map = call(
+                kernel, args, [(8, units)] + fold_outs, [rows, (1, units)] + coefs
             )
-    totals = summed(sums)[:ITERS, 0]
+        sums = [total]
+    totals = summed(summed(total, "batch"), "tm")[:ITERS, 0]
     denom = lax.axis_size("batch") * sequences * units * (steps * lax.axis_size("tm") + 1) / 2.0
     residual_norms = jnp.sqrt(totals / denom + 1e-06)
     return (states.reshape(steps, sequences, units), residual_norms)

time: 71.3 us -> 51.8 us (0.73)
  starting transfers between devices: 36.2 us -> 27 us
  local copies, waits for them, and re-layouts: 7.37 us -> 0 us
  waiting for transfers between devices: 18.5 us -> 15.5 us
    ppermute x13 -> x18, starting transfers between devices: 36.2 us -> 27 us  [the longest x16 21.6 us: exchanged(): lax.ppermute(value, axis, [(i, i ^ by) for i in range(lax.axis_size(axis))])]
    unnamed x22 -> x0, local copies, waits for them, and re-layouts: 7.37 us -> none
    ppermute x13 -> x18, waiting for transfers between devices: 18.5 us -> 15.5 us  [the longest x16 11.8 us: exchanged(): lax.ppermute(value, axis, [(i, i ^ by) for i in range(lax.axis_size(axis))])]
  transfers between devices with their start and end apart: 13 -> 18, of which waited for: 9 -> 13; matrix products, arithmetic and copies ran while one was open for 0% -> 0% of each run, Pallas kernels for 0% -> 0%
where the time goes in v2:
time: 51.8 us; the launch traced here: 51.6 us
  starting transfers between devices  27 us (52%)
  waiting for transfers between devices  15.5 us (30%)
  Pallas kernels  7.69 us (15%)
  between operations  0.68 us (1%)
  other arithmetic  0.65 us (1%)
    ppermute x16, starting transfers between devices, exchanged(): lax.ppermute(value, axis, [(i, i ^ by) for i in range(lax.axis_size(axis))])  21.6 us
    ppermute x16, waiting for transfers between devices, exchanged(): lax.ppermute(value, axis, [(i, i ^ by) for i in range(lax.axis_size(axis))])  11.8 us
    pallas_call x5, Pallas kernels, call(): pl.pallas_call(kernel, out_shape=[jax.ShapeDtypeStruct(shape, F32) for sh...  7.69 us
    ppermute x2, starting transfers between devices, carry(): lax.ppermute(sent, 'tm', [(i, (i + held) % count) for i in range(count)])  5.41 us
    ppermute x2, waiting for transfers between devices, carry(): lax.ppermute(sent, 'tm', [(i, (i + held) % count) for i in range(count)])  3.73 us
  transfers between devices with their start and end apart: 18, of which 13 were waited for; matrix products, arithmetic and copies ran while one was open for 0% of the time, Pallas kernels for 0%

profile of v2, /device:TPU:0, one launch (start us, length us, event | category | flops | bytes accessed | tf_op | source)
XLA Modules:
  0.0 51.6 jit_solution(6691416949654186933)
XLA Ops:
  0.6 3.0 %shard_map.95 = (f32[32,384]{1,0:T(8,128)S(1)}, f32[32,128]{1,0:T(8,128)S(1)}, f32[40,128,128]{2,1,0:T(8,128)S(1)}, f32[40,128]{1,0:T(8,128)S(1)}, f32[136,128]{...) custom-call(bf16[32,128]{1,0:T(8,128)(2,1)} %bitcast.8, f32[1,128]{1,0:T(1,128)} %start_hbm.1, ...), custom_call_target="tpu_custom_call" | custom-call | tf_op jit(solution)/shard_map/pallas_call | solution.py:253
  3.7 4.0 %collective-permute-start.2 = (f32[136,128]{1,0:T(8,128)S(1)}, f32[136,128]{1,0:T(8,128)S(1)}, u32[]{:S(2)}, u32[]{:S(2)}) collective-permute-start(f32[136,128]{1,0:T(8,128)S(1)} %get-tuple-element.22.refs_0_.refs_6_), channel_id=1, source_target_pairs={{0,12},{4,8},{8,4},{12,0},{16,28},{20,24},{24,20},{28,16},{1,13},{... | collective-permute-start | bytes 208904 | tf_op jit(solution)/shard_map/ppermute | solution.py:264
  7.7 0.4 collective-permute-start.1
  8.2 0.2 collective-permute-start
  8.4 1.9 %collective-permute-done.2.refs_3_.refs_9_ = f32[136,128]{1,0:T(8,128)S(1)} collective-permute-done((f32[136,128]{1,0:T(8,128)S(1)}, f32[136,128]{1,0:T(8,128)S(1)}, u32[]{:S(2)}, u32[]{:S(2)}) %collective-permute-start.2) | collective-permute-done | bytes 69664 | tf_op jit(solution)/shard_map/ppermute | solution.py:264
  10.3 1.8 %collective-permute-done.1.refs_2_.refs_8_ = f32[136,128]{1,0:T(8,128)S(1)} collective-permute-done((f32[136,128]{1,0:T(8,128)S(1)}, f32[136,128]{1,0:T(8,128)S(1)}, u32[]{:S(2)}, u32[]{:S(2)}) %collective-permute-start.1) | collective-permute-done | bytes 69664 | tf_op jit(solution)/shard_map/ppermute | solution.py:264
  12.0 0.4 collective-permute-done.refs_1_.refs_7_
  12.5 0.4 shard_map.96
  12.9 2.7 %collective-permute-start.3 = (f32[8,128]{1,0:T(8,128)S(1)}, f32[8,128]{1,0:T(8,128)S(1)}, u32[]{:S(2)}, u32[]{:S(2)}) collective-permute-start(f32[8,128]{1,0:T(8,128)S(1)} %shard_map.96), channel_id=1, source_target_pairs={{0,16},{4,20},{8,24},{12,28},{16,0},{20,4},{24,8},{28,12},{1,17},{... | collective-permute-start | bytes 12296 | tf_op jit(solution)/shard_map/ppermute | solution.py:286
  15.6 1.9 %collective-permute-done.3.refs_10_ = f32[8,128]{1,0:T(8,128)S(1)} collective-permute-done((f32[8,128]{1,0:T(8,128)S(1)}, f32[8,128]{1,0:T(8,128)S(1)}, u32[]{:S(2)}, u32[]{:S(2)}) %collective-permute-start.3) | collective-permute-done | bytes 4128 | tf_op jit(solution)/shard_map/ppermute | solution.py:286
  17.5 2.4 %shard_map.97 = (f32[8,128]{1,0:T(8,128)S(1)}, f32[32,128]{1,0:T(8,128)S(1)}, f32[40,128,128]{2,1,0:T(8,128)S(1)}, f32[40,128]{1,0:T(8,128)S(1)}, f32[136,128]{1,0:T(8,128)S(1)}) custom-call(f32[8,128]{1,0:T(8,128)S(1)} %get-tuple-element.16.consts_ref.refs_0_, f32[32,384]{1,0:T(8,128)S(1)} %get-tuple-element.17.refs_1_, ...), custom_call_target="tpu_custom_call" | custom-call | tf_op jit(solution)/shard_map/pallas_call | solution.py:253
  20.0 1.9 %collective-permute-start.6 = (f32[136,128]{1,0:T(8,128)S(1)}, f32[136,128]{1,0:T(8,128)S(1)}, u32[]{:S(2)}, u32[]{:S(2)}) collective-permute-start(f32[136,128]{1,0:T(8,128)S(1)} %get-tuple-element.26.refs_0_.refs_6_), channel_id=1, source_target_pairs={{0,12},{4,8},{8,4},{12,0},{16,28},{20,24},{24,20},{28,16},{1,13},{... | collective-permute-start | bytes 208904 | tf_op jit(solution)/shard_map/ppermute | solution.py:264
  21.9 0.2 collective-permute-start.5
  22.1 1.4 %collective-permute-start.4 = (f32[136,128]{1,0:T(8,128)S(1)}, f32[136,128]{1,0:T(8,128)S(1)}, u32[]{:S(2)}, u32[]{:S(2)}) collective-permute-start(f32[136,128]{1,0:T(8,128)S(1)} %get-tuple-element.26.refs_0_.refs_6_), channel_id=1, source_target_pairs={{0,4},{4,0},{8,12},{12,8},{16,20},{20,16},{24,28},{28,24},{1,5},{5... | collective-permute-start | bytes 208904 | tf_op jit(solution)/shard_map/ppermute | solution.py:264
  23.5 1.7 %collective-permute-done.6.refs_3_.refs_9_ = f32[136,128]{1,0:T(8,128)S(1)} collective-permute-done((f32[136,128]{1,0:T(8,128)S(1)}, f32[136,128]{1,0:T(8,128)S(1)}, u32[]{:S(2)}, u32[]{:S(2)}) %collective-permute-start.6) | collective-permute-done | bytes 69664 | tf_op jit(solution)/shard_map/ppermute | solution.py:264
  25.2 1.0 %collective-permute-done.5.refs_2_.refs_8_ = f32[136,128]{1,0:T(8,128)S(1)} collective-permute-done((f32[136,128]{1,0:T(8,128)S(1)}, f32[136,128]{1,0:T(8,128)S(1)}, u32[]{:S(2)}, u32[]{:S(2)}) %collective-permute-start.5) | collective-permute-done | bytes 69664 | tf_op jit(solution)/shard_map/ppermute | solution.py:264
  26.2 0.2 collective-permute-done.4.refs_1_.refs_7_
  26.4 0.4 shard_map.98
  26.9 2.8 %collective-permute-start.7 = (f32[8,128]{1,0:T(8,128)S(1)}, f32[8,128]{1,0:T(8,128)S(1)}, u32[]{:S(2)}, u32[]{:S(2)}) collective-permute-start(f32[8,128]{1,0:T(8,128)S(1)} %shard_map.98), channel_id=1, source_target_pairs={{0,16},{4,20},{8,24},{12,28},{16,0},{20,4},{24,8},{28,12},{1,17},{... | collective-permute-start | bytes 12296 | tf_op jit(solution)/shard_map/ppermute | solution.py:286
  29.6 1.8 %collective-permute-done.7.refs_10_ = f32[8,128]{1,0:T(8,128)S(1)} collective-permute-done((f32[8,128]{1,0:T(8,128)S(1)}, f32[8,128]{1,0:T(8,128)S(1)}, u32[]{:S(2)}, u32[]{:S(2)}) %collective-permute-start.7) | collective-permute-done | bytes 4128 | tf_op jit(solution)/shard_map/ppermute | solution.py:286
  31.5 1.3 %shard_map.99 = (f32[32,128]{1,0:T(8,128)}, f32[8,128]{1,0:T(8,128)S(1)}) custom-call(f32[8,128]{1,0:T(8,128)S(1)} %get-tuple-element.16.consts_ref.refs_0_, f32[32,384]{1,0:T(8,128)S(1)} %get-tuple-element.17.refs_1_, f32[32,128]{1,0:T(8,128)S(1)} %get-tuple-element.23.refs_2_, f32[40,128,128]{2,1,0:T(8,128)S(1)} %get-tuple-element.24.refs_3_, ...), custom_call_target="tpu_custom_call" | custom-call | tf_op jit(solution)/shard_map/pallas_call | solution.py:253
  32.8 0.0 collective-permute-start.10
  32.8 1.6 %collective-permute-start.9 = (f32[8,128]{1,0:T(8,128)S(1)}, f32[8,128]{1,0:T(8,128)S(1)}, u32[]{:S(2)}, u32[]{:S(2)}) collective-permute-start(f32[8,128]{1,0:T(8,128)S(1)} %get-tuple-element.29), channel_id=1, source_target_pairs={{0,2},{1,3},{2,0},{3,1},{4,6},{5,7},{6,4},{7,5},{8,10},{9,11},{10,... | collective-permute-start | bytes 12296 | tf_op jit(solution)/shard_map/ppermute | solution.py:264
  34.4 0.2 collective-permute-start.8
  34.6 1.2 %collective-permute-done.10 = f32[8,128]{1,0:T(8,128)S(1)} collective-permute-done((f32[8,128]{1,0:T(8,128)S(1)}, f32[8,128]{1,0:T(8,128)S(1)}, u32[]{:S(2)}, u32[]{:S(2)}) %collective-permute-start.10) | collective-permute-done | bytes 4128 | tf_op jit(solution)/shard_map/ppermute | solution.py:264
  35.8 0.6 %collective-permute-done.9 = f32[8,128]{1,0:T(8,128)S(1)} collective-permute-done((f32[8,128]{1,0:T(8,128)S(1)}, f32[8,128]{1,0:T(8,128)S(1)}, u32[]{:S(2)}, u32[]{:S(2)}) %collective-permute-start.9) | collective-permute-done | bytes 4128 | tf_op jit(solution)/shard_map/ppermute | solution.py:264
  36.4 0.0 collective-permute-done.8
  36.4 5.0 %collective-permute-start.17 = (f32[8,128]{1,0:T(8,128)S(1)}, f32[8,128]{1,0:T(8,128)S(1)}, u32[]{:S(2)}, u32[]{:S(2)}) collective-permute-start(f32[8,128]{1,0:T(8,128)S(1)} %add_add_fusion.1), channel_id=1, source_target_pairs={{0,28},{4,24},{8,20},{12,16},{16,12},{20,8},{24,4},{28,0},{1,29},{... | collective-permute-start | bytes 12296 | tf_op jit(solution)/shard_map/ppermute | solution.py:264
  41.4 0.0 collective-permute-start.16
  41.5 0.7 %collective-permute-start.15 = (f32[8,128]{1,0:T(8,128)S(1)}, f32[8,128]{1,0:T(8,128)S(1)}, u32[]{:S(2)}, u32[]{:S(2)}) collective-permute-start(f32[8,128]{1,0:T(8,128)S(1)} %add_add_fusion.1), channel_id=1, source_target_pairs={{0,20},{4,16},{8,28},{12,24},{16,4},{20,0},{24,12},{28,8},{1,21},{... | collective-permute-start | bytes 12296 | tf_op jit(solution)/shard_map/ppermute | solution.py:264
  42.1 2.3 %collective-permute-start.14 = (f32[8,128]{1,0:T(8,128)S(1)}, f32[8,128]{1,0:T(8,128)S(1)}, u32[]{:S(2)}, u32[]{:S(2)}) collective-permute-start(f32[8,128]{1,0:T(8,128)S(1)} %add_add_fusion.1), channel_id=1, source_target_pairs={{0,16},{4,20},{8,24},{12,28},{16,0},{20,4},{24,8},{28,12},{1,17},{... | collective-permute-start | bytes 12296 | tf_op jit(solution)/shard_map/ppermute | solution.py:264
  44.5 2.3 %collective-permute-start.13 = (f32[8,128]{1,0:T(8,128)S(1)}, f32[8,128]{1,0:T(8,128)S(1)}, u32[]{:S(2)}, u32[]{:S(2)}) collective-permute-start(f32[8,128]{1,0:T(8,128)S(1)} %add_add_fusion.1), channel_id=1, source_target_pairs={{0,12},{4,8},{8,4},{12,0},{16,28},{20,24},{24,20},{28,16},{1,13},{... | collective-permute-start | bytes 12296 | tf_op jit(solution)/shard_map/ppermute | solution.py:264
  46.7 0.0 collective-permute-done.17
  46.7 0.6 %collective-permute-start.12 = (f32[8,128]{1,0:T(8,128)S(1)}, f32[8,128]{1,0:T(8,128)S(1)}, u32[]{:S(2)}, u32[]{:S(2)}) collective-permute-start(f32[8,128]{1,0:T(8,128)S(1)} %add_add_fusion.1), channel_id=1, source_target_pairs={{0,8},{4,12},{8,0},{12,4},{16,24},{20,28},{24,16},{28,20},{1,9},{5... | collective-permute-start | bytes 12296 | tf_op jit(solution)/shard_map/ppermute | solution.py:264
  47.3 0.0 collective-permute-done.16
  47.3 0.6 %collective-permute-start.11 = (f32[8,128]{1,0:T(8,128)S(1)}, f32[8,128]{1,0:T(8,128)S(1)}, u32[]{:S(2)}, u32[]{:S(2)}) collective-permute-start(f32[8,128]{1,0:T(8,128)S(1)} %add_add_fusion.1), channel_id=1, source_target_pairs={{0,4},{4,0},{8,12},{12,8},{16,20},{20,16},{24,28},{28,24},{1,5},{5... | collective-permute-start | bytes 12296 | tf_op jit(solution)/shard_map/ppermute | solution.py:264
  47.9 0.0 collective-permute-done.15
  48.0 0.0 collective-permute-done.14
  48.0 1.0 %collective-permute-done.13 = f32[8,128]{1,0:T(8,128)S(1)} collective-permute-done((f32[8,128]{1,0:T(8,128)S(1)}, f32[8,128]{1,0:T(8,128)S(1)}, u32[]{:S(2)}, u32[]{:S(2)}) %collective-permute-start.13) | collective-permute-done | bytes 4128 | tf_op jit(solution)/shard_map/ppermute | solution.py:264
  49.0 1.4 %collective-permute-done.12 = f32[8,128]{1,0:T(8,128)S(1)} collective-permute-done((f32[8,128]{1,0:T(8,128)S(1)}, f32[8,128]{1,0:T(8,128)S(1)}, u32[]{:S(2)}, u32[]{:S(2)}) %collective-permute-start.12) | collective-permute-done | bytes 4128 | tf_op jit(solution)/shard_map/ppermute | solution.py:264
  50.3 0.6 %collective-permute-done.11 = f32[8,128]{1,0:T(8,128)S(1)} collective-permute-done((f32[8,128]{1,0:T(8,128)S(1)}, f32[8,128]{1,0:T(8,128)S(1)}, u32[]{:S(2)}, u32[]{:S(2)}) %collective-permute-start.11) | collective-permute-done | bytes 4128 | tf_op jit(solution)/shard_map/ppermute | solution.py:264
  50.9 0.6 %sqrt_reduce_fusion = f32[2]{0:T(128)} fusion(f32[8,128]{1,0:T(8,128)S(1)} %add_add_fusion), kind=kLoop, calls=%fused_computation.2 | loop fusion | flops 4 | bytes 16 | tf_op jit(solution)/shard_map/sqrt | solution.py:323
  (2 shorter events, 0.0 us)
Async XLA Ops:
  3.7 6.6 %collective-permute-start.2 = (f32[136,128]{1,0:T(8,128)S(1)}, f32[136,128]{1,0:T(8,128)S(1)}, u32[]{:S(2)}, u32[]{:S(2)}) collective-permute-start(f32[136,128]{1,0:T(8,128)S(1)} %get-tuple-element.22.refs_0_.refs_6_), channel_id=1, source_target_pairs={{0,12},{4,8},{8,4},{12,0},{16,28},{20,24},{24,20},{28,16},{1,13},{... | collective-permute-start | bytes 208904 | tf_op jit(solution)/shard_map/ppermute | solution.py:264
  7.7 4.3 %collective-permute-start.1 = (f32[136,128]{1,0:T(8,128)S(1)}, f32[136,128]{1,0:T(8,128)S(1)}, u32[]{:S(2)}, u32[]{:S(2)}) collective-permute-start(f32[136,128]{1,0:T(8,128)S(1)} %get-tuple-element.22.refs_0_.refs_6_), channel_id=1, source_target_pairs={{0,8},{4,12},{8,0},{12,4},{16,24},{20,28},{24,16},{28,20},{1,9},{5... | collective-permute-start | bytes 208904 | tf_op jit(solution)/shard_map/ppermute | solution.py:264
  8.2 4.3 %collective-permute-start = (f32[136,128]{1,0:T(8,128)S(1)}, f32[136,128]{1,0:T(8,128)S(1)}, u32[]{:S(2)}, u32[]{:S(2)}) collective-permute-start(f32[136,128]{1,0:T(8,128)S(1)} %get-tuple-element.22.refs_0_.refs_6_), channel_id=1, source_target_pairs={{0,4},{4,0},{8,12},{12,8},{16,20},{20,16},{24,28},{28,24},{1,5},{5... | collective-permute-start | bytes 208904 | tf_op jit(solution)/shard_map/ppermute | solution.py:264
  12.9 4.6 %collective-permute-start.3 = (f32[8,128]{1,0:T(8,128)S(1)}, f32[8,128]{1,0:T(8,128)S(1)}, u32[]{:S(2)}, u32[]{:S(2)}) collective-permute-start(f32[8,128]{1,0:T(8,128)S(1)} %shard_map.96), channel_id=1, source_target_pairs={{0,16},{4,20},{8,24},{12,28},{16,0},{20,4},{24,8},{28,12},{1,17},{... | collective-permute-start | bytes 12296 | tf_op jit(solution)/shard_map/ppermute | solution.py:286
  20.0 5.3 %collective-permute-start.6 = (f32[136,128]{1,0:T(8,128)S(1)}, f32[136,128]{1,0:T(8,128)S(1)}, u32[]{:S(2)}, u32[]{:S(2)}) collective-permute-start(f32[136,128]{1,0:T(8,128)S(1)} %get-tuple-element.26.refs_0_.refs_6_), channel_id=1, source_target_pairs={{0,12},{4,8},{8,4},{12,0},{16,28},{20,24},{24,20},{28,16},{1,13},{... | collective-permute-start | bytes 208904 | tf_op jit(solution)/shard_map/ppermute | solution.py:264
  21.9 4.3 %collective-permute-start.5 = (f32[136,128]{1,0:T(8,128)S(1)}, f32[136,128]{1,0:T(8,128)S(1)}, u32[]{:S(2)}, u32[]{:S(2)}) collective-permute-start(f32[136,128]{1,0:T(8,128)S(1)} %get-tuple-element.26.refs_0_.refs_6_), channel_id=1, source_target_pairs={{0,8},{4,12},{8,0},{12,4},{16,24},{20,28},{24,16},{28,20},{1,9},{5... | collective-permute-start | bytes 208904 | tf_op jit(solution)/shard_map/ppermute | solution.py:264
  22.1 4.3 %collective-permute-start.4 = (f32[136,128]{1,0:T(8,128)S(1)}, f32[136,128]{1,0:T(8,128)S(1)}, u32[]{:S(2)}, u32[]{:S(2)}) collective-permute-start(f32[136,128]{1,0:T(8,128)S(1)} %get-tuple-element.26.refs_0_.refs_6_), channel_id=1, source_target_pairs={{0,4},{4,0},{8,12},{12,8},{16,20},{20,16},{24,28},{28,24},{1,5},{5... | collective-permute-start | bytes 208904 | tf_op jit(solution)/shard_map/ppermute | solution.py:264
  26.9 4.6 %collective-permute-start.7 = (f32[8,128]{1,0:T(8,128)S(1)}, f32[8,128]{1,0:T(8,128)S(1)}, u32[]{:S(2)}, u32[]{:S(2)}) collective-permute-start(f32[8,128]{1,0:T(8,128)S(1)} %shard_map.98), channel_id=1, source_target_pairs={{0,16},{4,20},{8,24},{12,28},{16,0},{20,4},{24,8},{28,12},{1,17},{... | collective-permute-start | bytes 12296 | tf_op jit(solution)/shard_map/ppermute | solution.py:286
  32.8 3.0 %collective-permute-start.10 = (f32[8,128]{1,0:T(8,128)S(1)}, f32[8,128]{1,0:T(8,128)S(1)}, u32[]{:S(2)}, u32[]{:S(2)}) collective-permute-start(f32[8,128]{1,0:T(8,128)S(1)} %get-tuple-element.29), channel_id=1, source_target_pairs={{0,3},{1,2},{2,1},{3,0},{4,7},{5,6},{6,5},{7,4},{8,11},{9,10},{10,... | collective-permute-start | bytes 12296 | tf_op jit(solution)/shard_map/ppermute | solution.py:264
  32.8 3.6 %collective-permute-start.9 = (f32[8,128]{1,0:T(8,128)S(1)}, f32[8,128]{1,0:T(8,128)S(1)}, u32[]{:S(2)}, u32[]{:S(2)}) collective-permute-start(f32[8,128]{1,0:T(8,128)S(1)} %get-tuple-element.29), channel_id=1, source_target_pairs={{0,2},{1,3},{2,0},{3,1},{4,6},{5,7},{6,4},{7,5},{8,10},{9,11},{10,... | collective-permute-start | bytes 12296 | tf_op jit(solution)/shard_map/ppermute | solution.py:264
  34.4 2.0 %collective-permute-start.8 = (f32[8,128]{1,0:T(8,128)S(1)}, f32[8,128]{1,0:T(8,128)S(1)}, u32[]{:S(2)}, u32[]{:S(2)}) collective-permute-start(f32[8,128]{1,0:T(8,128)S(1)} %get-tuple-element.29), channel_id=1, source_target_pairs={{0,1},{1,0},{2,3},{3,2},{4,5},{5,4},{6,7},{7,6},{8,9},{9,8},{10,11... | collective-permute-start | bytes 12296 | tf_op jit(solution)/shard_map/ppermute | solution.py:264
  36.4 10.3 %collective-permute-start.17 = (f32[8,128]{1,0:T(8,128)S(1)}, f32[8,128]{1,0:T(8,128)S(1)}, u32[]{:S(2)}, u32[]{:S(2)}) collective-permute-start(f32[8,128]{1,0:T(8,128)S(1)} %add_add_fusion.1), channel_id=1, source_target_pairs={{0,28},{4,24},{8,20},{12,16},{16,12},{20,8},{24,4},{28,0},{1,29},{... | collective-permute-start | bytes 12296 | tf_op jit(solution)/shard_map/ppermute | solution.py:264
  41.4 5.9 %collective-permute-start.16 = (f32[8,128]{1,0:T(8,128)S(1)}, f32[8,128]{1,0:T(8,128)S(1)}, u32[]{:S(2)}, u32[]{:S(2)}) collective-permute-start(f32[8,128]{1,0:T(8,128)S(1)} %add_add_fusion.1), channel_id=1, source_target_pairs={{0,24},{4,28},{8,16},{12,20},{16,8},{20,12},{24,0},{28,4},{1,25},{... | collective-permute-start | bytes 12296 | tf_op jit(solution)/shard_map/ppermute | solution.py:264
  41.5 6.5 %collective-permute-start.15 = (f32[8,128]{1,0:T(8,128)S(1)}, f32[8,128]{1,0:T(8,128)S(1)}, u32[]{:S(2)}, u32[]{:S(2)}) collective-permute-start(f32[8,128]{1,0:T(8,128)S(1)} %add_add_fusion.1), channel_id=1, source_target_pairs={{0,20},{4,16},{8,28},{12,24},{16,4},{20,0},{24,12},{28,8},{1,21},{... | collective-permute-start | bytes 12296 | tf_op jit(solution)/shard_map/ppermute | solution.py:264
  42.1 5.8 %collective-permute-start.14 = (f32[8,128]{1,0:T(8,128)S(1)}, f32[8,128]{1,0:T(8,128)S(1)}, u32[]{:S(2)}, u32[]{:S(2)}) collective-permute-start(f32[8,128]{1,0:T(8,128)S(1)} %add_add_fusion.1), channel_id=1, source_target_pairs={{0,16},{4,20},{8,24},{12,28},{16,0},{20,4},{24,8},{28,12},{1,17},{... | collective-permute-start | bytes 12296 | tf_op jit(solution)/shard_map/ppermute | solution.py:264
  44.5 4.5 %collective-permute-start.13 = (f32[8,128]{1,0:T(8,128)S(1)}, f32[8,128]{1,0:T(8,128)S(1)}, u32[]{:S(2)}, u32[]{:S(2)}) collective-permute-start(f32[8,128]{1,0:T(8,128)S(1)} %add_add_fusion.1), channel_id=1, source_target_pairs={{0,12},{4,8},{8,4},{12,0},{16,28},{20,24},{24,20},{28,16},{1,13},{... | collective-permute-start | bytes 12296 | tf_op jit(solution)/shard_map/ppermute | solution.py:264
  46.7 3.6 %collective-permute-start.12 = (f32[8,128]{1,0:T(8,128)S(1)}, f32[8,128]{1,0:T(8,128)S(1)}, u32[]{:S(2)}, u32[]{:S(2)}) collective-permute-start(f32[8,128]{1,0:T(8,128)S(1)} %add_add_fusion.1), channel_id=1, source_target_pairs={{0,8},{4,12},{8,0},{12,4},{16,24},{20,28},{24,16},{28,20},{1,9},{5... | collective-permute-start | bytes 12296 | tf_op jit(solution)/shard_map/ppermute | solution.py:264
  47.3 3.6 %collective-permute-start.11 = (f32[8,128]{1,0:T(8,128)S(1)}, f32[8,128]{1,0:T(8,128)S(1)}, u32[]{:S(2)}, u32[]{:S(2)}) collective-permute-start(f32[8,128]{1,0:T(8,128)S(1)} %add_add_fusion.1), channel_id=1, source_target_pairs={{0,4},{4,0},{8,12},{12,8},{16,20},{20,16},{24,28},{28,24},{1,5},{5... | collective-permute-start | bytes 12296 | tf_op jit(solution)/shard_map/ppermute | solution.py:264

commit v3 on v2

--- a/solution.py
+++ b/solution.py
@@ -58,7 +58,7 @@
 def walk(first, refs, place, stop):
     state = first
     for other in range(stop):
-        state = through(state, refs[place ^ other])
+        state = through(state, refs[place ^ other] if len(refs) > 1 else refs[0].at[other])
     return state
 
 
@@ -128,10 +128,12 @@
             free += 1
         items = joined
     last = items[0][1]
-    map_ref[:units, :] = mats_ref[last]
-    map_ref[units : units + 1, :] = vecs_ref[last : last + 1, :]
-    map_ref[units + 1 : units + 2, :] = prev_ref[0:1, :]
-    map_ref[units + 2 :, :] = jnp.zeros((6, units), F32)
+    copies = [map_ref] if len(map_ref.shape) == 2 else [map_ref.at[i] for i in range(map_ref.shape[0])]
+    for one in copies:
+        one[:units, :] = mats_ref[last]
+        one[units : units + 1, :] = vecs_ref[last : last + 1, :]
+        one[units + 1 : units + 2, :] = prev_ref[0:1, :]
+        one[units + 2 :, :] = jnp.zeros((6, units), F32)
 
 
 def unfold(entering, prev_ref, mats_ref, vecs_ref, out_ref):
@@ -206,8 +208,8 @@
     fold(parts, prev_ref, weight_ref, coef_refs, mats_ref, vecs_ref, map_ref)
 
 
-def hop_kernel(held, consts_ref, *refs):
-    maps, arrived, sent_ref = refs[:held], refs[held:-1], refs[-1]
+def hop_kernel(held, pieces, consts_ref, *refs):
+    maps, arrived, sent_ref = refs[:pieces], refs[pieces:-1], refs[-1]
     first = group_start(consts_ref, arrived)
     place = lax.rem(lax.axis_index("tm"), held)
     for mine in range(held):
@@ -218,10 +220,10 @@
             sent_ref[...] = jnp.broadcast_to(state, sent_ref.shape)
 
 
-def next_kernel(newton, held, hops, *refs):
+def next_kernel(newton, held, pieces, hops, *refs):
     last = newton == ITERS - 1
     consts_ref, gates_ref, old_prev_ref, old_mats_ref, old_vecs_ref, weight_ref = refs[:6]
-    maps, refs = refs[6 : 6 + held], refs[6 + held :]
+    maps, refs = refs[6 : 6 + pieces], refs[6 + pieces :]
     arrived, refs = refs[: min(hops, 1)], refs[min(hops, 1) :]
     if newton > 0:
         sums_ref, refs = refs[0], refs[1:]
@@ -242,8 +244,12 @@
     shift_in(entering, states_ref, prev_ref)
     parts = cell(gates_ref[...], prev_ref[...], weight_ref[...], consts_ref[1:2, :])
     done = weighted_square(states_ref[...], parts[4])
-    row = lax.broadcasted_iota(jnp.int32, new_sums_ref.shape, 0)
-    new_sums_ref[...] = jnp.where(row == newton, done, sums_ref[...] if newton > 0 else 0.0)
+    lane = lax.broadcasted_iota(jnp.int32, (1, prev_ref.shape[1]), 1)
+    sums = jnp.where(lane == newton, done, sums_ref[0:1, :] if newton > 0 else 0.0)
+    if last:
+        new_sums_ref[...] = jnp.broadcast_to(sums[None], new_sums_ref.shape)
+    else:
+        new_sums_ref[...] = jnp.broadcast_to(sums, new_sums_ref.shape)
     if not last:
         fold(parts, prev_ref, weight_ref, coef_refs, mats_ref, vecs_ref, map_ref)
 
@@ -264,25 +270,17 @@
     return lax.ppermute(value, axis, [(i, i ^ by) for i in range(lax.axis_size(axis))])
 
 
-def summed(value, axis):
-    count, by = lax.axis_size(axis), 1
-    while by < count:
-        radix = min(8, count // by)
-        terms = [value] + [exchanged(value, axis, k * by) for k in range(1, radix)]
-        while len(terms) > 1:
-            terms = [a + b for a, b in zip(terms[0::2], terms[1::2])]
-        value = terms[0]
-        by *= radix
-    return value
-
-
-def carry(consts, own_map):
+def carry(consts, own_map, newton):
     count, units = lax.axis_size("tm"), consts.shape[1]
     held = min(WINDOW, count)
-    maps = [own_map] + [exchanged(own_map, "tm", k) for k in range(1, held)]
+    if newton == 0:
+        groups = [list(range(first, first + held)) for first in range(0, count, held)]
+        maps = [lax.all_to_all(own_map, "tm", 0, 0, axis_index_groups=groups)]
+    else:
+        maps = [own_map] + [exchanged(own_map, "tm", k) for k in range(1, held)]
     arrived = []
     for hop in range(count // held - 1):
-        (sent,) = call(functools.partial(hop_kernel, held), [consts, *maps, *arrived], [(8, units)])
+        (sent,) = call(functools.partial(hop_kernel, held, len(maps)), [consts, *maps, *arrived], [(8, units)])
         arrived = [lax.ppermute(sent, "tm", [(i, (i + held) % count) for i in range(count)])]
     return arrived, maps
 
@@ -301,24 +299,25 @@
         first_kernel,
         [inputs.reshape(steps, -1), h_start, in_weight, rec_weight, row(update_bias), row(reset_bias),
          row(cand_bias), row(rec_bias)],
-        [wide] + fold_outs + [rec_weight.shape, (8, units)],
+        [wide] + fold_outs[:3] + [(min(WINDOW, lax.axis_size("tm")), units + 8, units), rec_weight.shape, (8, units)],
         [pltpu.VMEM((steps, in_weight.shape[0]), BF16), pltpu.VMEM(in_weight.shape, BF16), (1, 3 * units),
          (1, units), (1, units), pltpu.SemaphoreType.DMA((8,))] + coefs,
         space=pltpu.HBM,
     )
     sums = []
+    devices = lax.axis_size(("tm", "batch"))
     for newton in range(ITERS):
-        arrived, maps = carry(consts, own_map)
+        arrived, maps = carry(consts, own_map, newton)
         args = [consts, gates, prev, mats, vecs, weight, *maps, *arrived, *sums]
-        kernel = functools.partial(next_kernel, newton, len(maps), len(arrived))
+        kernel = functools.partial(next_kernel, newton, min(WINDOW, lax.axis_size('tm')), len(maps), len(arrived))
         if newton == ITERS - 1:
-            states, total = call(kernel, args, [rows, (8, units)], [rows, (1, units)])
+            states, total = call(kernel, args, [rows, (devices, 1, units)], [rows, (1, units)])
         else:
             total, prev, mats, vecs, own_map = call(
                 kernel, args, [(8, units)] + fold_outs, [rows, (1, units)] + coefs
             )
         sums = [total]
-    totals = summed(summed(total, "batch"), "tm")[:ITERS, 0]
+    totals = jnp.sum(lax.all_to_all(total, ("tm", "batch"), 0, 0, tiled=True), axis=(0, 1))[:ITERS]
     denom = lax.axis_size("batch") * sequences * units * (steps * lax.axis_size("tm") + 1) / 2.0
     residual_norms = jnp.sqrt(totals / denom + 1e-06)
     return (states.reshape(steps, sequences, units), residual_norms)

time: 51.8 us -> 48.3 us (0.932)
  blocking collectives: 0 us -> 23.4 us
  starting transfers between devices: 27 us -> 8.82 us
  waiting for transfers between devices: 15.5 us -> 6.89 us
    all_to_all x0 -> x2, blocking collectives: none -> 23.4 us  [the longest x1 12.1 us: per_device(): lax.all_to_all(total, ('tm', 'batch'), 0, 0, tiled=True)]
    ppermute x16 -> x3, starting transfers between devices: 21.6 us -> 3.55 us  [exchanged(): lax.ppermute(value, axis, [(i, i ^ by) for i in range(lax.axis_size(axis))])]
    ppermute x16 -> x3, waiting for transfers between devices: 11.8 us -> 3.01 us  [exchanged(): lax.ppermute(value, axis, [(i, i ^ by) for i in range(lax.axis_size(axis))])]
  transfers between devices with their start and end apart: 18 -> 5, of which waited for: 13 -> 4; matrix products, arithmetic and copies ran while one was open for 0% -> 0% of each run, Pallas kernels for 0% -> 0%
where the time goes in v3:
time: 48.3 us; the launch traced here: 48 us
  blocking collectives  23.4 us (48%)
  starting transfers between devices  8.82 us (18%)
  Pallas kernels  7.69 us (16%)
  waiting for transfers between devices  6.89 us (14%)
  between operations  0.67 us (1%)
  other arithmetic  0.57 us (1%)
    all_to_all x1, blocking collectives, per_device(): lax.all_to_all(total, ('tm', 'batch'), 0, 0, tiled=True)  12.1 us
    all_to_all x1, blocking collectives, carry(): maps = [lax.all_to_all(own_map, 'tm', 0, 0, axis_index_groups=groups)]  11.2 us
    pallas_call x5, Pallas kernels, call(): pl.pallas_call(kernel, out_shape=[jax.ShapeDtypeStruct(shape, F32) for sh...  7.69 us
    ppermute x2, starting transfers between devices, carry(): lax.ppermute(sent, 'tm', [(i, (i + held) % count) for i in range(count)])  5.27 us
    ppermute x2, waiting for transfers between devices, carry(): lax.ppermute(sent, 'tm', [(i, (i + held) % count) for i in range(count)])  3.89 us
    ppermute x3, starting transfers between devices, exchanged(): lax.ppermute(value, axis, [(i, i ^ by) for i in range(lax.axis_size(axis))])  3.55 us
    ppermute x3, waiting for transfers between devices, exchanged(): lax.ppermute(value, axis, [(i, i ^ by) for i in range(lax.axis_size(axis))])  3.01 us
  transfers between devices with their start and end apart: 5, of which 4 were waited for; matrix products, arithmetic and copies ran while one was open for 0% of the time, Pallas kernels for 0%

profile of v3, /device:TPU:0, one launch (start us, length us, event | category | flops | bytes accessed | tf_op | source)
XLA Modules:
  0.0 48.0 jit_solution(2401096461670232031)
XLA Ops:
  0.6 3.0 %shard_map.95 = (f32[32,384]{1,0:T(8,128)S(1)}, f32[32,128]{1,0:T(8,128)S(1)}, f32[40,128,128]{2,1,0:T(8,128)S(1)}, f32[40,128]{1,0:T(8,128)S(1)}, f32[4,136,128...) custom-call(bf16[32,128]{1,0:T(8,128)(2,1)} %bitcast.8, f32[1,128]{1,0:T(1,128)} %start_hbm.1, ...), custom_call_target="tpu_custom_call" | custom-call | tf_op jit(solution)/shard_map/pallas_call | solution.py:259
  3.7 11.2 %all_to_all.10.refs_0_.refs_6_ = f32[4,136,128]{2,1,0:T(8,128)S(1)} all-to-all(f32[4,136,128]{2,1,0:T(8,128)S(1)} %get-tuple-element.22), channel_id=1, replica_groups={{0,4,8,12},{16,20,24,28},{1,5,9,13},{17,21,25,29},{2,6,10,14},{18,22,26..., dimensions={0} | all-to-all | bytes 557056 | tf_op jit(solution)/shard_map/all_to_all | solution.py:278
  14.9 0.4 shard_map.96
  15.4 2.6 %collective-permute-start = (f32[8,128]{1,0:T(8,128)S(1)}, f32[8,128]{1,0:T(8,128)S(1)}, u32[]{:S(2)}, u32[]{:S(2)}) collective-permute-start(f32[8,128]{1,0:T(8,128)S(1)} %shard_map.96), channel_id=1, source_target_pairs={{0,16},{4,20},{8,24},{12,28},{16,0},{20,4},{24,8},{28,12},{1,17},{... | collective-permute-start | bytes 12296 | tf_op jit(solution)/shard_map/ppermute | solution.py:284
  18.0 1.9 %collective-permute-done.refs_7_ = f32[8,128]{1,0:T(8,128)S(1)} collective-permute-done((f32[8,128]{1,0:T(8,128)S(1)}, f32[8,128]{1,0:T(8,128)S(1)}, u32[]{:S(2)}, u32[]{:S(2)}) %collective-permute-start) | collective-permute-done | bytes 4128 | tf_op jit(solution)/shard_map/ppermute | solution.py:284
  20.0 2.4 %shard_map.97 = (f32[8,128]{1,0:T(8,128)S(1)}, f32[32,128]{1,0:T(8,128)S(1)}, f32[40,128,128]{2,1,0:T(8,128)S(1)}, f32[40,128]{1,0:T(8,128)S(1)}, f32[136,128]{1,0:T(8,128)S(1)}) custom-call(f32[8,128]{1,0:T(8,128)S(1)} %get-tuple-element.16.consts_ref.refs_0_, f32[32,384]{1,0:T(8,128)S(1)} %get-tuple-element.17.refs_1_, ...), custom_call_target="tpu_custom_call" | custom-call | tf_op jit(solution)/shard_map/pallas_call | solution.py:259
  22.4 1.0 %collective-permute-start.3 = (f32[136,128]{1,0:T(8,128)S(1)}, f32[136,128]{1,0:T(8,128)S(1)}, u32[]{:S(2)}, u32[]{:S(2)}) collective-permute-start(f32[136,128]{1,0:T(8,128)S(1)} %get-tuple-element.26.refs_0_.refs_6_), channel_id=1, source_target_pairs={{0,12},{4,8},{8,4},{12,0},{16,28},{20,24},{24,20},{28,16},{1,13},{... | collective-permute-start | bytes 208904 | tf_op jit(solution)/shard_map/ppermute | solution.py:270
  23.4 1.3 %collective-permute-start.2 = (f32[136,128]{1,0:T(8,128)S(1)}, f32[136,128]{1,0:T(8,128)S(1)}, u32[]{:S(2)}, u32[]{:S(2)}) collective-permute-start(f32[136,128]{1,0:T(8,128)S(1)} %get-tuple-element.26.refs_0_.refs_6_), channel_id=1, source_target_pairs={{0,8},{4,12},{8,0},{12,4},{16,24},{20,28},{24,16},{28,20},{1,9},{5... | collective-permute-start | bytes 208904 | tf_op jit(solution)/shard_map/ppermute | solution.py:270
  24.7 1.3 %collective-permute-start.1 = (f32[136,128]{1,0:T(8,128)S(1)}, f32[136,128]{1,0:T(8,128)S(1)}, u32[]{:S(2)}, u32[]{:S(2)}) collective-permute-start(f32[136,128]{1,0:T(8,128)S(1)} %get-tuple-element.26.refs_0_.refs_6_), channel_id=1, source_target_pairs={{0,4},{4,0},{8,12},{12,8},{16,20},{20,16},{24,28},{28,24},{1,5},{5... | collective-permute-start | bytes 208904 | tf_op jit(solution)/shard_map/ppermute | solution.py:270
  26.0 1.7 %collective-permute-done.3.refs_3_.refs_9_ = f32[136,128]{1,0:T(8,128)S(1)} collective-permute-done((f32[136,128]{1,0:T(8,128)S(1)}, f32[136,128]{1,0:T(8,128)S(1)}, u32[]{:S(2)}, u32[]{:S(2)}) %collective-permute-start.3) | collective-permute-done | bytes 69664 | tf_op jit(solution)/shard_map/ppermute | solution.py:270
  27.7 0.0 collective-permute-done.2.refs_2_.refs_8_
  27.7 1.3 %collective-permute-done.1.refs_1_.refs_7_ = f32[136,128]{1,0:T(8,128)S(1)} collective-permute-done((f32[136,128]{1,0:T(8,128)S(1)}, f32[136,128]{1,0:T(8,128)S(1)}, u32[]{:S(2)}, u32[]{:S(2)}) %collective-permute-start.1) | collective-permute-done | bytes 69664 | tf_op jit(solution)/shard_map/ppermute | solution.py:270
  29.0 0.4 shard_map.98
  29.4 2.6 %collective-permute-start.4 = (f32[8,128]{1,0:T(8,128)S(1)}, f32[8,128]{1,0:T(8,128)S(1)}, u32[]{:S(2)}, u32[]{:S(2)}) collective-permute-start(f32[8,128]{1,0:T(8,128)S(1)} %shard_map.98), channel_id=1, source_target_pairs={{0,16},{4,20},{8,24},{12,28},{16,0},{20,4},{24,8},{28,12},{1,17},{... | collective-permute-start | bytes 12296 | tf_op jit(solution)/shard_map/ppermute | solution.py:284
  32.1 2.0 %collective-permute-done.4.refs_10_ = f32[8,128]{1,0:T(8,128)S(1)} collective-permute-done((f32[8,128]{1,0:T(8,128)S(1)}, f32[8,128]{1,0:T(8,128)S(1)}, u32[]{:S(2)}, u32[]{:S(2)}) %collective-permute-start.4) | collective-permute-done | bytes 4128 | tf_op jit(solution)/shard_map/ppermute | solution.py:284
  34.0 1.3 %shard_map.99 = (f32[32,128]{1,0:T(8,128)}, f32[32,1,128]{2,1,0:T(1,128)S(1)}) custom-call(f32[8,128]{1,0:T(8,128)S(1)} %get-tuple-element.16.consts_ref.refs_0_, f32[32,384]{1,0:T(8,128)S(1)} %get-tuple-element.17.refs_1_, f32[32,128]{1,0:T(8,128)S(1)} %get-tuple-element.23.refs_2_, f32[40,128,128]{2,1,0:T(8,128)S(1)} %get-tuple-element.24.refs_3_, ...), custom_call_target="tpu_custom_call" | custom-call | tf_op jit(solution)/shard_map/pallas_call | solution.py:259
  35.3 12.1 %all_to_all.11 = f32[32,1,128]{2,1,0:T(1,128)S(1)} all-to-all(f32[32,1,128]{2,1,0:T(1,128)S(1)} %get-tuple-element.29), channel_id=1, replica_groups=mesh['tm'=8,'batch'=4] {'tm','batch'}, dimensions={0} | all-to-all | bytes 32768 | tf_op jit(solution)/shard_map/all_to_all | solution.py:320
  47.4 0.1 reduce_sum.9
  47.5 0.5 %add_sqrt_fusion = f32[2]{0:T(128)} fusion(f32[128]{0:T(128)S(1)} %reduce_sum.9), kind=kLoop, calls=%fused_computation | loop fusion | flops 4 | bytes 16 | tf_op jit(solution)/shard_map/sqrt | solution.py:322
Async XLA Ops:
  15.4 4.6 %collective-permute-start = (f32[8,128]{1,0:T(8,128)S(1)}, f32[8,128]{1,0:T(8,128)S(1)}, u32[]{:S(2)}, u32[]{:S(2)}) collective-permute-start(f32[8,128]{1,0:T(8,128)S(1)} %shard_map.96), channel_id=1, source_target_pairs={{0,16},{4,20},{8,24},{12,28},{16,0},{20,4},{24,8},{28,12},{1,17},{... | collective-permute-start | bytes 12296 | tf_op jit(solution)/shard_map/ppermute | solution.py:284
  22.4 5.3 %collective-permute-start.3 = (f32[136,128]{1,0:T(8,128)S(1)}, f32[136,128]{1,0:T(8,128)S(1)}, u32[]{:S(2)}, u32[]{:S(2)}) collective-permute-start(f32[136,128]{1,0:T(8,128)S(1)} %get-tuple-element.26.refs_0_.refs_6_), channel_id=1, source_target_pairs={{0,12},{4,8},{8,4},{12,0},{16,28},{20,24},{24,20},{28,16},{1,13},{... | collective-permute-start | bytes 208904 | tf_op jit(solution)/shard_map/ppermute | solution.py:270
  23.4 4.3 %collective-permute-start.2 = (f32[136,128]{1,0:T(8,128)S(1)}, f32[136,128]{1,0:T(8,128)S(1)}, u32[]{:S(2)}, u32[]{:S(2)}) collective-permute-start(f32[136,128]{1,0:T(8,128)S(1)} %get-tuple-element.26.refs_0_.refs_6_), channel_id=1, source_target_pairs={{0,8},{4,12},{8,0},{12,4},{16,24},{20,28},{24,16},{28,20},{1,9},{5... | collective-permute-start | bytes 208904 | tf_op jit(solution)/shard_map/ppermute | solution.py:270
  24.7 4.3 %collective-permute-start.1 = (f32[136,128]{1,0:T(8,128)S(1)}, f32[136,128]{1,0:T(8,128)S(1)}, u32[]{:S(2)}, u32[]{:S(2)}) collective-permute-start(f32[136,128]{1,0:T(8,128)S(1)} %get-tuple-element.26.refs_0_.refs_6_), channel_id=1, source_target_pairs={{0,4},{4,0},{8,12},{12,8},{16,20},{20,16},{24,28},{28,24},{1,5},{5... | collective-permute-start | bytes 208904 | tf_op jit(solution)/shard_map/ppermute | solution.py:270
  29.4 4.6 %collective-permute-start.4 = (f32[8,128]{1,0:T(8,128)S(1)}, f32[8,128]{1,0:T(8,128)S(1)}, u32[]{:S(2)}, u32[]{:S(2)}) collective-permute-start(f32[8,128]{1,0:T(8,128)S(1)} %shard_map.98), channel_id=1, source_target_pairs={{0,16},{4,20},{8,24},{12,28},{16,0},{20,4},{24,8},{28,12},{1,17},{... | collective-permute-start | bytes 12296 | tf_op jit(solution)/shard_map/ppermute | solution.py:284

commit v4 on v2

v4 whole, which is shorter than its diff:
```python
import functools

import jax
import jax.numpy as jnp
from jax import lax
from jax.experimental import pallas as pl
from jax.experimental.pallas import tpu as pltpu
from jax.sharding import PartitionSpec as P

ITERS = 2
SPAN = 4
CHAINS = 16
PAD = 16
F32 = jnp.float32
BF16 = jnp.bfloat16


def halves(value):
    high = value.astype(BF16)
    return high, (value - high.astype(F32)).astype(BF16)


def paired_rows(value):
    return jnp.concatenate(halves(value), axis=1)


def paired_cols(value):
    both = jnp.concatenate(halves(value), axis=1)
    return jnp.concatenate([both, both], axis=0)


def product(rows, cols):
    width = cols.shape[1]
    both = jnp.dot(paired_rows(rows), paired_cols(cols), preferred_element_type=F32)
    return both[:, :width] + both[:, width:]


def as_column(row):
    units = row.shape[1]
    return jnp.broadcast_to(row, (units, units)).T


def row_times(column, matrix):
    return jnp.sum(column * matrix, axis=0, keepdims=True)


def cell(gates, previous, rec_weight, rec_bias):
    units = previous.shape[1]
    rec = product(previous, rec_weight)
    update = jax.nn.sigmoid(gates[:, :units] + rec[:, :units])
    reset = jax.nn.sigmoid(gates[:, units : 2 * units] + rec[:, units : 2 * units])
    recur = rec[:, 2 * units :] + rec_bias
    cand = jnp.tanh(gates[:, 2 * units :] + reset * recur)
    stepped = (1.0 - update) * cand + update * previous
    return update, reset, recur, cand, stepped


def group_start(consts_ref, arrived_refs):
    start = consts_ref[0:1, :]
    if not arrived_refs:
        return start
    return jnp.where(lax.axis_index("tm") < SPAN, start, arrived_refs[0][0:1, :])


def through(state, one_map):
    units = state.shape[1]
    column = as_column(state - one_map[units + 1 : units + 2, :])
    return row_times(column, one_map[:units, :]) + one_map[units : units + 1, :]


def joins(steps):
    size = steps // CHAINS
    slots = {(b, 1): (b + 1) * size - 1 for b in range(CHAINS)}
    free, span = steps, 2
    while span <= CHAINS:
        for b in range(0, CHAINS, span):
            slots[(b, span)] = free
            free += 1
        span *= 2
    return slots


def fold(parts, prev_ref, weight_ref, coef_refs, mats_ref, vecs_ref, map_ref):
    update, reset, recur, cand, stepped = parts
    steps, units = update.shape
    size = steps // CHAINS
    previous = prev_ref[...]
    update_ref, coef_update_ref, coef_reset_ref, coef_cand_ref, step_ref = coef_refs
    common = (1.0 - update) * (1.0 - cand * cand)
    update_ref[...] = update
    coef_update_ref[...] = (previous - cand) * update * (1.0 - update)
    coef_reset_ref[...] = common * recur * reset * (1.0 - reset)
    coef_cand_ref[...] = common * reset
    step_ref[...] = stepped
    row = lax.broadcasted_iota(jnp.int32, (units, units), 0)
    col = lax.broadcasted_iota(jnp.int32, (units, units), 1)

    def slope(t):
        return (
            weight_ref[:, :units] * coef_update_ref[pl.ds(t, 1), :]
            + weight_ref[:, units : 2 * units] * coef_reset_ref[pl.ds(t, 1), :]
            + weight_ref[:, 2 * units :] * coef_cand_ref[pl.ds(t, 1), :]
        )

    def stacked(mat, vec):
        return jnp.concatenate([mat, jnp.broadcast_to(vec, (PAD, units))], axis=0)

    for block in range(CHAINS):
        t = block * size
        mats_ref[t] = slope(t) + jnp.where(row == col, update_ref[t : t + 1, :], 0.0)
        vecs_ref[t : t + 1, :] = step_ref[t : t + 1, :]

    def advance(inner, carried):
        for block in range(CHAINS):
            t = block * size + inner
            shifted = vecs_ref[pl.ds(t - 1, 1), :] - prev_ref[pl.ds(t, 1), :]
            before = stacked(mats_ref[t - 1], shifted)
            after = product(before, slope(t)) + before * update_ref[pl.ds(t, 1), :]
            mats_ref[t] = after[:units]
            vecs_ref[pl.ds(t, 1), :] = after[units : units + 1] + step_ref[pl.ds(t, 1), :]
        return carried

    lax.fori_loop(1, size, advance, 0)

    slots = joins(steps)
    for (first, span), slot in slots.items():
        if span > 1:
            second = first + span // 2
            early, late = slots[(first, span // 2)], slots[(second, span // 2)]
            shifted = vecs_ref[early : early + 1, :] - prev_ref[second * size : second * size + 1, :]
            after = product(stacked(mats_ref[early], shifted), mats_ref[late])
            mats_ref[slot] = after[:units]
            vecs_ref[slot : slot + 1, :] = after[units : units + 1] + vecs_ref[late : late + 1, :]
    last = slots[(0, CHAINS)]
    map_ref[:units, :] = mats_ref[last]
    map_ref[units : units + 1, :] = vecs_ref[last : last + 1, :]
    map_ref[units + 1 : units + 2, :] = prev_ref[0:1, :]
    map_ref[units + 2 :, :] = jnp.zeros((6, units), F32)


def unfold(entering, prev_ref, mats_ref, vecs_ref, out_ref):
    steps = prev_ref.shape[0]
    size = steps // CHAINS
    slots = joins(steps)
    starts = {0: entering}
    for b in sorted(range(CHAINS), key=lambda b: (bin(b).count("1"), -b)):
        t = b * size
        column = as_column(starts[b] - prev_ref[t : t + 1, :])
        span = 1
        while b % (2 * span) == 0 and b + span < CHAINS:
            slot = slots[(b, span)]
            starts[b + span] = row_times(column, mats_ref[slot]) + vecs_ref[slot : slot + 1, :]
            span *= 2
        for inner in range(size):
            state = row_times(column, mats_ref[t + inner]) + vecs_ref[t + inner : t + inner + 1, :]
            out_ref[t + inner : t + inner + 1, :] = state


def shift_in(entering, states_ref, prev_ref):
    steps = states_ref.shape[0]
    prev_ref[0:1, :] = entering
    prev_ref[1:steps, :] = states_ref[0 : steps - 1, :]


def weighted_square(states, stepped):
    steps = states.shape[0]
    group, count = lax.axis_index("tm") // SPAN, lax.axis_size("tm") // SPAN
    position = group * steps + lax.broadcasted_iota(jnp.int32, states.shape, 0)
    weights = (position.astype(F32) + 1.0) / (steps * count)
    return jnp.sum(weights * (states - stepped) ** 2, axis=(0, 1), keepdims=True)


def send_on(start, map_ref, sent_ref):
    sent_ref[...] = jnp.broadcast_to(through(start, map_ref), sent_ref.shape)


def fetch_kernel(
    inputs_hbm, start_hbm, in_weight_hbm, weight_hbm, update_bias_hbm, reset_bias_hbm, cand_bias_hbm,
    rec_bias_hbm,
    wide_ref, in_weight_ref, weight_ref, bias_ref, consts_ref,
    inputs_ref, start_ref, rec_bias_ref, sems
):
    units = weight_ref.shape[0]
    moves = [
        (inputs_hbm, inputs_ref), (in_weight_hbm, in_weight_ref), (weight_hbm, weight_ref),
        (update_bias_hbm, bias_ref.at[:, pl.ds(0, units)]),
        (reset_bias_hbm, bias_ref.at[:, pl.ds(units, units)]),
        (cand_bias_hbm, bias_ref.at[:, pl.ds(2 * units, units)]),
        (start_hbm, start_ref), (rec_bias_hbm, rec_bias_ref),
    ]
    copies = [pltpu.make_async_copy(src, dst, sems.at[i]) for i, (src, dst) in enumerate(moves)]
    for copy in copies:
        copy.start()
    for copy in copies:
        copy.wait()
    wide_ref[...] = inputs_ref[...].astype(F32)
    consts_ref[0:1, :] = start_ref[...]
    consts_ref[1:2, :] = rec_bias_ref[...]
    consts_ref[2:, :] = jnp.zeros((6, units), F32)


def first_kernel(consts_ref, in_weight_ref, bias_ref, weight_ref, *refs):
    shares, refs = refs[:SPAN], refs[SPAN:]
    gates_ref, prev_ref, mats_ref, vecs_ref, map_ref, sent_ref, held_ref, *coef_refs = refs
    steps, units = prev_ref.shape
    mine = lax.axis_index("tm")
    place = lax.rem(mine, SPAN)
    for k in range(SPAN):
        held_ref[k] = shares[k][...]
    inputs = jnp.concatenate([held_ref[place ^ j] for j in range(SPAN)], axis=0).astype(BF16)
    gates = jnp.dot(inputs, in_weight_ref[...], preferred_element_type=F32) + bias_ref[...]
    gates_ref[...] = gates
    start = consts_ref[0:1, :]
    at_start = (mine < SPAN) & (lax.broadcasted_iota(jnp.int32, (steps, units), 0) == 0)
    previous = jnp.where(at_start, start, 0.0)
    prev_ref[...] = previous
    parts = cell(gates, previous, weight_ref[...], consts_ref[1:2, :])
    fold(parts, prev_ref, weight_ref, coef_refs, mats_ref, vecs_ref, map_ref)
    send_on(start, map_ref, sent_ref)


def hop_kernel(consts_ref, map_ref, arrived_ref, sent_ref):
    send_on(group_start(consts_ref, [arrived_ref]), map_ref, sent_ref)


def next_kernel(newton, hops, *refs):
    last = newton == ITERS - 1
    consts_ref, gates_ref, old_prev_ref, old_mats_ref, old_vecs_ref, weight_ref = refs[:6]
    arrived, refs = refs[6 : 6 + hops], refs[6 + hops :]
    if newton > 0:
        sums_ref, refs = refs[0], refs[1:]
    if last:
        out_ref, new_sums_ref, prev_ref, states_ref = refs
    else:
        new_sums_ref, prev_ref, mats_ref, vecs_ref, map_ref, sent_ref, states_ref, *coef_refs = refs
    entering = group_start(consts_ref, arrived)
    unfold(entering, old_prev_ref, old_mats_ref, old_vecs_ref, states_ref)
    shift_in(entering, states_ref, prev_ref)
    if last:
        share = out_ref.shape[0]
        first = pl.multiple_of(lax.rem(lax.axis_index("tm"), SPAN) * share, share)
        out_ref[...] = states_ref[pl.ds(first, share), :]
    parts = cell(gates_ref[...], prev_ref[...], weight_ref[...], consts_ref[1:2, :])
    done = weighted_square(states_ref[...], parts[4])
    lane = lax.broadcasted_iota(jnp.int32, new_sums_ref.shape, 1)
    new_sums_ref[...] = jnp.where(lane == newton, done, sums_ref[...] if newton > 0 else 0.0)
    if not last:
        fold(parts, prev_ref, weight_ref, coef_refs, mats_ref, vecs_ref, map_ref)
        send_on(consts_ref[0:1, :], map_ref, sent_ref)


def call(kernel, args, outs, scratch=(), space=pltpu.VMEM):
    args = [pltpu.with_memory_space_constraint(arg, space) for arg in args]
    return pl.pallas_call(
        kernel,
        out_shape=[jax.ShapeDtypeStruct(o, F32) if isinstance(o, tuple) else o for o in outs],
        in_specs=[pl.BlockSpec(memory_space=space)] * len(args),
        out_specs=[pl.BlockSpec(memory_space=pltpu.VMEM)] * len(outs),
        scratch_shapes=[pltpu.VMEM(one, F32) if isinstance(one, tuple) else one for one in scratch],
        compiler_params=pltpu.CompilerParams(vmem_limit_bytes=24 * 1024 * 1024),
    )(*args)


def exchanged(value, axis, by):
    return lax.ppermute(value, axis, [(i, i ^ by) for i in range(lax.axis_size(axis))])


def summed(value, axis, by=1):
    count = lax.axis_size(axis)
    while by < count:
        radix = min(4, count // by)
        terms = [value] + [exchanged(value, axis, k * by) for k in range(1, radix)]
        while len(terms) > 1:
            terms = [a + b for a, b in zip(terms[0::2], terms[1::2])]
        value = terms[0]
        by *= radix
    return value


def carry(consts, own_map, sent):
    count = lax.axis_size("tm")
    ring = [(i, (i + SPAN) % count) for i in range(count)]
    arrived = []
    for hop in range(count // SPAN - 1):
        if hop > 0:
            (sent,) = call(hop_kernel, [consts, own_map, *arrived], [sent.shape])
        arrived = [lax.ppermute(sent, "tm", ring)]
    return arrived


def per_device(
    inputs, h_start, in_weight, rec_weight, update_bias, reset_bias, cand_bias, rec_bias
):
    share, sequences = inputs.shape[0], inputs.shape[1]
    units = rec_weight.shape[0]
    row = lambda value: value.reshape(1, units)
    steps = share * SPAN
    slots = steps + CHAINS
    rows, wide = (steps, units), (steps, 3 * units)
    fold_outs = [rows, (slots, units, units), (slots, units), (units + 8, units), (8, units)]
    coefs = [rows] * 5
    own, in_rows, weight, bias, consts = call(
        fetch_kernel,
        [inputs.reshape(share, -1), h_start, in_weight, rec_weight, row(update_bias), row(reset_bias),
         row(cand_bias), row(rec_bias)],
        [(share, units), jax.ShapeDtypeStruct(in_weight.shape, BF16), rec_weight.shape, (1, 3 * units),
         (8, units)],
        [pltpu.VMEM((share, units), BF16), (1, units), (1, units), pltpu.SemaphoreType.DMA((8,))],
        space=pltpu.HBM,
    )
    shares = [own] + [exchanged(own, "tm", k) for k in range(1, SPAN)]
    gates, prev, mats, vecs, own_map, sent = call(
        first_kernel, [consts, in_rows, bias, weight, *shares], [wide] + fold_outs,
        [(SPAN, share, units)] + coefs,
    )
    sums = []
    for newton in range(ITERS):
        arrived = carry(consts, own_map, sent)
        args = [consts, gates, prev, mats, vecs, weight, *arrived, *sums]
        kernel = functools.partial(next_kernel, newton, len(arrived))
        if newton == ITERS - 1:
            states, total = call(kernel, args, [(share, units), (8, units)], [rows, rows])
        else:
            total, prev, mats, vecs, own_map, sent = call(
                kernel, args, [(8, units)] + fold_outs, [rows] + coefs
            )
        sums = [total]
    totals = summed(summed(total, "batch"), "tm", SPAN)[0, :ITERS]
    denom = lax.axis_size("batch") * sequences * units * (share * lax.axis_size("tm") + 1) / 2.0
    residual_norms = jnp.sqrt(totals / denom + 1e-06)
    return (states.reshape(share, sequences, units), residual_norms)


def solution(mesh):
    in_specs = (P("tm", "batch", None), P("batch", None), P(), P(), P(), P(), P(), P())
    out_specs = (P("tm", "batch", None), P())
    return jax.shard_map(
        per_device, mesh=mesh, in_specs=in_specs, out_specs=out_specs, check_vma=False
    )
```

time: 51.8 us -> 44.8 us (0.86)
  starting transfers between devices: 27 us -> 14.4 us
  Pallas kernels: 7.69 us -> 18 us
  waiting for transfers between devices: 15.5 us -> 11.1 us
    ppermute x16 -> x7, starting transfers between devices: 21.6 us -> 9.2 us  [exchanged(): lax.ppermute(value, axis, [(i, i ^ by) for i in range(lax.axis_size(axis))])]
    pallas_call x5 -> x4, Pallas kernels: 7.69 us -> 18 us  [call(): pl.pallas_call(kernel, out_shape=[jax.ShapeDtypeStruct(o, F32) if isinsta...]
    ppermute x16 -> x7, waiting for transfers between devices: 11.8 us -> 7.25 us  [exchanged(): lax.ppermute(value, axis, [(i, i ^ by) for i in range(lax.axis_size(axis))])]
  transfers between devices with their start and end apart: 18 -> 9, of which waited for: 13 -> 8; matrix products, arithmetic and copies ran while one was open for 0% -> 0% of each run, Pallas kernels for 0% -> 0%
where the time goes in v4:
time: 44.8 us; the launch traced here: 44.6 us
  Pallas kernels  18 us (40%)
  starting transfers between devices  14.4 us (32%)
  waiting for transfers between devices  11.1 us (25%)
  between operations  0.65 us (1%)
  other arithmetic  0.53 us (1%)
    pallas_call x4, Pallas kernels, call(): pl.pallas_call(kernel, out_shape=[jax.ShapeDtypeStruct(o, F32) if isinsta...  18 us
    ppermute x7, starting transfers between devices, exchanged(): lax.ppermute(value, axis, [(i, i ^ by) for i in range(lax.axis_size(axis))])  9.2 us
    ppermute x7, waiting for transfers between devices, exchanged(): lax.ppermute(value, axis, [(i, i ^ by) for i in range(lax.axis_size(axis))])  7.25 us
    ppermute x2, starting transfers between devices, carry(): arrived = [lax.ppermute(sent, 'tm', ring)]  5.17 us
    ppermute x2, waiting for transfers between devices, carry(): arrived = [lax.ppermute(sent, 'tm', ring)]  3.84 us
  transfers between devices with their start and end apart: 9, of which 8 were waited for; matrix products, arithmetic and copies ran while one was open for 0% of the time, Pallas kernels for 0%

profile of v4, /device:TPU:0, one launch (start us, length us, event | category | flops | bytes accessed | tf_op | source)
XLA Modules:
  0.0 44.6 jit_solution(11871292477256927540)
XLA Ops:
  0.6 1.1 %shard_map.95 = (f32[32,128]{1,0:T(8,128)S(1)}, bf16[128,384]{1,0:T(8,128)(2,1)S(1)}, f32[128,384]{1,0:T(8,128)S(1)}, f32[1,384]{1,0:T(1,128)S(1)}, f32[8,128]{1,0:T(8,128)S(1)}) custom-call(bf16[32,128]{1,0:T(8,128)(2,1)} %bitcast.10, f32[1,128]{1,0:T(1,128)} %start_hbm.1, bf16[128,384]{1,0:T(8,128)(2,1)} %in_weight_hbm.1, f32[128,384]{1,0:T(8,128)} %weight_hbm.1, ...), custom_call_target="tpu_custom_call" | custom-call | tf_op jit(solution)/shard_map/pallas_call | solution.py:254
  1.7 4.0 %collective-permute-start.2 = (f32[32,128]{1,0:T(8,128)S(1)}, f32[32,128]{1,0:T(8,128)S(1)}, u32[]{:S(2)}, u32[]{:S(2)}) collective-permute-start(f32[32,128]{1,0:T(8,128)S(1)} %get-tuple-element.23.refs_0_), channel_id=1, source_target_pairs={{0,12},{4,8},{8,4},{12,0},{16,28},{20,24},{24,20},{28,16},{1,13},{... | collective-permute-start | bytes 49160 | tf_op jit(solution)/shard_map/ppermute | solution.py:265
  5.8 0.4 %collective-permute-start.1 = (f32[32,128]{1,0:T(8,128)S(1)}, f32[32,128]{1,0:T(8,128)S(1)}, u32[]{:S(2)}, u32[]{:S(2)}) collective-permute-start(f32[32,128]{1,0:T(8,128)S(1)} %get-tuple-element.23.refs_0_), channel_id=1, source_target_pairs={{0,8},{4,12},{8,0},{12,4},{16,24},{20,28},{24,16},{28,20},{1,9},{5... | collective-permute-start | bytes 49160 | tf_op jit(solution)/shard_map/ppermute | solution.py:265
  6.2 0.2 collective-permute-start
  6.4 1.1 %collective-permute-done.2.refs_3_ = f32[32,128]{1,0:T(8,128)S(1)} collective-permute-done((f32[32,128]{1,0:T(8,128)S(1)}, f32[32,128]{1,0:T(8,128)S(1)}, u32[]{:S(2)}, u32[]{:S(2)}) %collective-permute-start.2) | collective-permute-done | bytes 16416 | tf_op jit(solution)/shard_map/ppermute | solution.py:265
  7.5 2.0 %collective-permute-done.1.refs_2_ = f32[32,128]{1,0:T(8,128)S(1)} collective-permute-done((f32[32,128]{1,0:T(8,128)S(1)}, f32[32,128]{1,0:T(8,128)S(1)}, u32[]{:S(2)}, u32[]{:S(2)}) %collective-permute-start.1) | collective-permute-done | bytes 16416 | tf_op jit(solution)/shard_map/ppermute | solution.py:265
  9.5 0.4 %collective-permute-done.refs_1_ = f32[32,128]{1,0:T(8,128)S(1)} collective-permute-done((f32[32,128]{1,0:T(8,128)S(1)}, f32[32,128]{1,0:T(8,128)S(1)}, u32[]{:S(2)}, u32[]{:S(2)}) %collective-permute-start) | collective-permute-done | bytes 16416 | tf_op jit(solution)/shard_map/ppermute | solution.py:265
  9.9 7.2 %shard_map.96 = (f32[128,384]{1,0:T(8,128)S(1)}, f32[128,128]{1,0:T(8,128)S(1)}, f32[144,128,128]{2,1,0:T(8,128)S(1)}, f32[144,128]{1,0:T(8,128)S(1)}, f32[136,128]{1,0:T(8,128)}, /*index=5*/f32[8,128]{1,0:T(8,128)S(1)}) custom-call(f32[8,128]{1,0:T(8,128)S(1)} %get-tuple-element.19.consts_ref.refs_0_, bf16[128,384]{1,0:T(8,128)(2,1)S(1)} %get-tuple-element.20.in_weight_ref, ...), custom_call_target="tpu_custom_call" | custom-call | tf_op jit(solution)/shard_map/pallas_call | solution.py:254
  17.1 2.6 %collective-permute-start.3 = (f32[8,128]{1,0:T(8,128)S(1)}, f32[8,128]{1,0:T(8,128)S(1)}, u32[]{:S(2)}, u32[]{:S(2)}) collective-permute-start(f32[8,128]{1,0:T(8,128)S(1)} %get-tuple-element.28), channel_id=1, source_target_pairs={{0,16},{4,20},{8,24},{12,28},{16,0},{20,4},{24,8},{28,12},{1,17},{... | collective-permute-start | bytes 12296 | tf_op jit(solution)/shard_map/ppermute | solution.py:287
  19.7 1.9 %collective-permute-done.3.refs_6_ = f32[8,128]{1,0:T(8,128)S(1)} collective-permute-done((f32[8,128]{1,0:T(8,128)S(1)}, f32[8,128]{1,0:T(8,128)S(1)}, u32[]{:S(2)}, u32[]{:S(2)}) %collective-permute-start.3) | collective-permute-done | bytes 4128 | tf_op jit(solution)/shard_map/ppermute | solution.py:287
  21.6 8.0 %shard_map.97 = (f32[8,128]{1,0:T(8,128)S(1)}, f32[128,128]{1,0:T(8,128)S(1)}, f32[144,128,128]{2,1,0:T(8,128)S(1)}, f32[144,128]{1,0:T(8,128)S(1)}, f32[136,128]{1,0:T(8,128)}, /*index=5*/f32[8,128]{1,0:T(8,128)S(1)}) custom-call(f32[8,128]{1,0:T(8,128)S(1)} %get-tuple-element.19.consts_ref.refs_0_, f32[128,384]{1,0:T(8,128)S(1)} %get-tuple-element.24.refs_1_, ...), custom_call_target="tpu_custom_call" | custom-call | tf_op jit(solution)/shard_map/pallas_call | solution.py:254
  29.6 2.6 %collective-permute-start.4 = (f32[8,128]{1,0:T(8,128)S(1)}, f32[8,128]{1,0:T(8,128)S(1)}, u32[]{:S(2)}, u32[]{:S(2)}) collective-permute-start(f32[8,128]{1,0:T(8,128)S(1)} %get-tuple-element.32), channel_id=1, source_target_pairs={{0,16},{4,20},{8,24},{12,28},{16,0},{20,4},{24,8},{28,12},{1,17},{... | collective-permute-start | bytes 12296 | tf_op jit(solution)/shard_map/ppermute | solution.py:287
  32.2 1.9 %collective-permute-done.4.refs_6_ = f32[8,128]{1,0:T(8,128)S(1)} collective-permute-done((f32[8,128]{1,0:T(8,128)S(1)}, f32[8,128]{1,0:T(8,128)S(1)}, u32[]{:S(2)}, u32[]{:S(2)}) %collective-permute-start.4) | collective-permute-done | bytes 4128 | tf_op jit(solution)/shard_map/ppermute | solution.py:287
  34.1 1.7 %shard_map.98 = (f32[32,128]{1,0:T(8,128)}, f32[8,128]{1,0:T(8,128)S(1)}) custom-call(f32[8,128]{1,0:T(8,128)S(1)} %get-tuple-element.19.consts_ref.refs_0_, f32[128,384]{1,0:T(8,128)S(1)} %get-tuple-element.24.refs_1_, f32[128,128]{1,0:T(8,128)S(1)} %get-tuple-element.29.refs_2_, f32[144,128,128]{2,1,0:T(8,128)S(1)} %get-tuple-element.30.refs_3_, ...), custom_call_target="tpu_custom_call" | custom-call | tf_op jit(solution)/shard_map/pallas_call | solution.py:254
  35.9 0.0 collective-permute-start.7
  35.9 1.5 %collective-permute-start.6 = (f32[8,128]{1,0:T(8,128)S(1)}, f32[8,128]{1,0:T(8,128)S(1)}, u32[]{:S(2)}, u32[]{:S(2)}) collective-permute-start(f32[8,128]{1,0:T(8,128)S(1)} %get-tuple-element.35), channel_id=1, source_target_pairs={{0,2},{1,3},{2,0},{3,1},{4,6},{5,7},{6,4},{7,5},{8,10},{9,11},{10,... | collective-permute-start | bytes 12296 | tf_op jit(solution)/shard_map/ppermute | solution.py:265
  37.4 0.3 collective-permute-start.5
  37.7 1.2 %collective-permute-done.7 = f32[8,128]{1,0:T(8,128)S(1)} collective-permute-done((f32[8,128]{1,0:T(8,128)S(1)}, f32[8,128]{1,0:T(8,128)S(1)}, u32[]{:S(2)}, u32[]{:S(2)}) %collective-permute-start.7) | collective-permute-done | bytes 4128 | tf_op jit(solution)/shard_map/ppermute | solution.py:265
  38.9 0.6 %collective-permute-done.6 = f32[8,128]{1,0:T(8,128)S(1)} collective-permute-done((f32[8,128]{1,0:T(8,128)S(1)}, f32[8,128]{1,0:T(8,128)S(1)}, u32[]{:S(2)}, u32[]{:S(2)}) %collective-permute-start.6) | collective-permute-done | bytes 4128 | tf_op jit(solution)/shard_map/ppermute | solution.py:265
  39.5 0.0 collective-permute-done.5
  39.5 2.6 %collective-permute-start.8 = (f32[8,128]{1,0:T(8,128)S(1)}, f32[8,128]{1,0:T(8,128)S(1)}, u32[]{:S(2)}, u32[]{:S(2)}) collective-permute-start(f32[8,128]{1,0:T(8,128)S(1)} %add_add_fusion), channel_id=1, source_target_pairs={{0,16},{4,20},{8,24},{12,28},{16,0},{20,4},{24,8},{28,12},{1,17},{... | collective-permute-start | bytes 12296 | tf_op jit(solution)/shard_map/ppermute | solution.py:265
  42.2 1.9 %collective-permute-done.8 = f32[8,128]{1,0:T(8,128)S(1)} collective-permute-done((f32[8,128]{1,0:T(8,128)S(1)}, f32[8,128]{1,0:T(8,128)S(1)}, u32[]{:S(2)}, u32[]{:S(2)}) %collective-permute-start.8) | collective-permute-done | bytes 4128 | tf_op jit(solution)/shard_map/ppermute | solution.py:265
  44.1 0.5 %sqrt_bitcast_fusion = f32[2]{0:T(128)} fusion(f32[8,128]{1,0:T(8,128)S(1)} %add.19), kind=kLoop, calls=%fused_computation.1 | loop fusion | flops 4 | bytes 16 | tf_op jit(solution)/shard_map/sqrt | solution.py:330
  (2 shorter events, 0.0 us)
Async XLA Ops:
  1.7 5.8 %collective-permute-start.2 = (f32[32,128]{1,0:T(8,128)S(1)}, f32[32,128]{1,0:T(8,128)S(1)}, u32[]{:S(2)}, u32[]{:S(2)}) collective-permute-start(f32[32,128]{1,0:T(8,128)S(1)} %get-tuple-element.23.refs_0_), channel_id=1, source_target_pairs={{0,12},{4,8},{8,4},{12,0},{16,28},{20,24},{24,20},{28,16},{1,13},{... | collective-permute-start | bytes 49160 | tf_op jit(solution)/shard_map/ppermute | solution.py:265
  5.8 3.7 %collective-permute-start.1 = (f32[32,128]{1,0:T(8,128)S(1)}, f32[32,128]{1,0:T(8,128)S(1)}, u32[]{:S(2)}, u32[]{:S(2)}) collective-permute-start(f32[32,128]{1,0:T(8,128)S(1)} %get-tuple-element.23.refs_0_), channel_id=1, source_target_pairs={{0,8},{4,12},{8,0},{12,4},{16,24},{20,28},{24,16},{28,20},{1,9},{5... | collective-permute-start | bytes 49160 | tf_op jit(solution)/shard_map/ppermute | solution.py:265
  6.2 3.7 %collective-permute-start = (f32[32,128]{1,0:T(8,128)S(1)}, f32[32,128]{1,0:T(8,128)S(1)}, u32[]{:S(2)}, u32[]{:S(2)}) collective-permute-start(f32[32,128]{1,0:T(8,128)S(1)} %get-tuple-element.23.refs_0_), channel_id=1, source_target_pairs={{0,4},{4,0},{8,12},{12,8},{16,20},{20,16},{24,28},{28,24},{1,5},{5... | collective-permute-start | bytes 49160 | tf_op jit(solution)/shard_map/ppermute | solution.py:265
  17.1 4.5 %collective-permute-start.3 = (f32[8,128]{1,0:T(8,128)S(1)}, f32[8,128]{1,0:T(8,128)S(1)}, u32[]{:S(2)}, u32[]{:S(2)}) collective-permute-start(f32[8,128]{1,0:T(8,128)S(1)} %get-tuple-element.28), channel_id=1, source_target_pairs={{0,16},{4,20},{8,24},{12,28},{16,0},{20,4},{24,8},{28,12},{1,17},{... | collective-permute-start | bytes 12296 | tf_op jit(solution)/shard_map/ppermute | solution.py:287
  29.6 4.5 %collective-permute-start.4 = (f32[8,128]{1,0:T(8,128)S(1)}, f32[8,128]{1,0:T(8,128)S(1)}, u32[]{:S(2)}, u32[]{:S(2)}) collective-permute-start(f32[8,128]{1,0:T(8,128)S(1)} %get-tuple-element.32), channel_id=1, source_target_pairs={{0,16},{4,20},{8,24},{12,28},{16,0},{20,4},{24,8},{28,12},{1,17},{... | collective-permute-start | bytes 12296 | tf_op jit(solution)/shard_map/ppermute | solution.py:287
  35.9 3.0 %collective-permute-start.7 = (f32[8,128]{1,0:T(8,128)S(1)}, f32[8,128]{1,0:T(8,128)S(1)}, u32[]{:S(2)}, u32[]{:S(2)}) collective-permute-start(f32[8,128]{1,0:T(8,128)S(1)} %get-tuple-element.35), channel_id=1, source_target_pairs={{0,3},{1,2},{2,1},{3,0},{4,7},{5,6},{6,5},{7,4},{8,11},{9,10},{10,... | collective-permute-start | bytes 12296 | tf_op jit(solution)/shard_map/ppermute | solution.py:265
  35.9 3.6 %collective-permute-start.6 = (f32[8,128]{1,0:T(8,128)S(1)}, f32[8,128]{1,0:T(8,128)S(1)}, u32[]{:S(2)}, u32[]{:S(2)}) collective-permute-start(f32[8,128]{1,0:T(8,128)S(1)} %get-tuple-element.35), channel_id=1, source_target_pairs={{0,2},{1,3},{2,0},{3,1},{4,6},{5,7},{6,4},{7,5},{8,10},{9,11},{10,... | collective-permute-start | bytes 12296 | tf_op jit(solution)/shard_map/ppermute | solution.py:265
  37.4 2.1 %collective-permute-start.5 = (f32[8,128]{1,0:T(8,128)S(1)}, f32[8,128]{1,0:T(8,128)S(1)}, u32[]{:S(2)}, u32[]{:S(2)}) collective-permute-start(f32[8,128]{1,0:T(8,128)S(1)} %get-tuple-element.35), channel_id=1, source_target_pairs={{0,1},{1,0},{2,3},{3,2},{4,5},{5,4},{6,7},{7,6},{8,9},{9,8},{10,11... | collective-permute-start | bytes 12296 | tf_op jit(solution)/shard_map/ppermute | solution.py:265
  39.5 4.6 %collective-permute-start.8 = (f32[8,128]{1,0:T(8,128)S(1)}, f32[8,128]{1,0:T(8,128)S(1)}, u32[]{:S(2)}, u32[]{:S(2)}) collective-permute-start(f32[8,128]{1,0:T(8,128)S(1)} %add_add_fusion), channel_id=1, source_target_pairs={{0,16},{4,20},{8,24},{12,28},{16,0},{20,4},{24,8},{28,12},{1,17},{... | collective-permute-start | bytes 12296 | tf_op jit(solution)/shard_map/ppermute | solution.py:265

commit v5 on v4

--- a/solution.py
+++ b/solution.py
@@ -55,11 +55,8 @@
     return update, reset, recur, cand, stepped
 
 
-def group_start(consts_ref, arrived_refs):
-    start = consts_ref[0:1, :]
-    if not arrived_refs:
-        return start
-    return jnp.where(lax.axis_index("tm") < SPAN, start, arrived_refs[0][0:1, :])
+def group():
+    return lax.axis_index("tm") // SPAN
 
 
 def through(state, one_map):
@@ -97,9 +94,9 @@
 
     def slope(t):
         return (
-            weight_ref[:, :units] * coef_update_ref[pl.ds(t, 1), :]
-            + weight_ref[:, units : 2 * units] * coef_reset_ref[pl.ds(t, 1), :]
-            + weight_ref[:, 2 * units :] * coef_cand_ref[pl.ds(t, 1), :]
+            weight_ref[:, :units] * coef_update_ref[t : t + 1, :]
+            + weight_ref[:, units : 2 * units] * coef_reset_ref[t : t + 1, :]
+            + weight_ref[:, 2 * units :] * coef_cand_ref[t : t + 1, :]
         )
 
     def stacked(mat, vec):
@@ -110,17 +107,13 @@
         mats_ref[t] = slope(t) + jnp.where(row == col, update_ref[t : t + 1, :], 0.0)
         vecs_ref[t : t + 1, :] = step_ref[t : t + 1, :]
 
-    def advance(inner, carried):
+    for inner in range(1, size):
         for block in range(CHAINS):
             t = block * size + inner
-            shifted = vecs_ref[pl.ds(t - 1, 1), :] - prev_ref[pl.ds(t, 1), :]
-            before = stacked(mats_ref[t - 1], shifted)
-            after = product(before, slope(t)) + before * update_ref[pl.ds(t, 1), :]
+            before = stacked(mats_ref[t - 1], vecs_ref[t - 1 : t, :] - prev_ref[t : t + 1, :])
+            after = product(before, slope(t)) + before * update_ref[t : t + 1, :]
             mats_ref[t] = after[:units]
-            vecs_ref[pl.ds(t, 1), :] = after[units : units + 1] + step_ref[pl.ds(t, 1), :]
-        return carried
-
-    lax.fori_loop(1, size, advance, 0)
+            vecs_ref[t : t + 1, :] = after[units : units + 1] + step_ref[t : t + 1, :]
 
     slots = joins(steps)
     for (first, span), slot in slots.items():
@@ -164,8 +157,8 @@
 
 def weighted_square(states, stepped):
     steps = states.shape[0]
-    group, count = lax.axis_index("tm") // SPAN, lax.axis_size("tm") // SPAN
-    position = group * steps + lax.broadcasted_iota(jnp.int32, states.shape, 0)
+    count = lax.axis_size("tm") // SPAN
+    position = group() * steps + lax.broadcasted_iota(jnp.int32, states.shape, 0)
     weights = (position.astype(F32) + 1.0) / (steps * count)
     return jnp.sum(weights * (states - stepped) ** 2, axis=(0, 1), keepdims=True)
 
@@ -201,7 +194,8 @@
 
 def first_kernel(consts_ref, in_weight_ref, bias_ref, weight_ref, *refs):
     shares, refs = refs[:SPAN], refs[SPAN:]
-    gates_ref, prev_ref, mats_ref, vecs_ref, map_ref, sent_ref, held_ref, *coef_refs = refs
+    gates_ref, sums_ref, prev_ref, mats_ref, vecs_ref, sent_ref, map_ref, held_ref, *coef_refs = refs
+    sums_ref[...] = jnp.zeros(sums_ref.shape, F32)
     steps, units = prev_ref.shape
     mine = lax.axis_index("tm")
     place = lax.rem(mine, SPAN)
@@ -219,34 +213,49 @@
     send_on(start, map_ref, sent_ref)
 
 
-def hop_kernel(consts_ref, map_ref, arrived_ref, sent_ref):
-    send_on(group_start(consts_ref, [arrived_ref]), map_ref, sent_ref)
-
-
-def next_kernel(newton, hops, *refs):
-    last = newton == ITERS - 1
-    consts_ref, gates_ref, old_prev_ref, old_mats_ref, old_vecs_ref, weight_ref = refs[:6]
-    arrived, refs = refs[6 : 6 + hops], refs[6 + hops :]
-    if newton > 0:
-        sums_ref, refs = refs[0], refs[1:]
-    if last:
-        out_ref, new_sums_ref, prev_ref, states_ref = refs
-    else:
-        new_sums_ref, prev_ref, mats_ref, vecs_ref, map_ref, sent_ref, states_ref, *coef_refs = refs
-    entering = group_start(consts_ref, arrived)
-    unfold(entering, old_prev_ref, old_mats_ref, old_vecs_ref, states_ref)
-    shift_in(entering, states_ref, prev_ref)
-    if last:
-        share = out_ref.shape[0]
-        first = pl.multiple_of(lax.rem(lax.axis_index("tm"), SPAN) * share, share)
-        out_ref[...] = states_ref[pl.ds(first, share), :]
-    parts = cell(gates_ref[...], prev_ref[...], weight_ref[...], consts_ref[1:2, :])
+def hop_kernel(sent_first_ref, map_ref, arrived_ref, sent_ref):
+    state = through(arrived_ref[0:1, :], map_ref)
+    sent_ref[...] = jnp.where(group() == 0, sent_first_ref[...], state)
+
+
+def middle_kernel(
+    newton, at_front, start_ref, consts_ref, gates_ref, weight_ref, old_prev_ref, old_mats_ref, old_vecs_ref,
+    sums_ref, new_sums_ref, new_prev_ref, mats_ref, vecs_ref, sent_ref, map_ref, states_ref, *coef_refs
+):
+    @pl.when((group() == 0) == at_front)
+    def _():
+        entering = start_ref[0:1, :]
+        unfold(entering, old_prev_ref, old_mats_ref, old_vecs_ref, states_ref)
+        shift_in(entering, states_ref, new_prev_ref)
+        parts = cell(gates_ref[...], new_prev_ref[...], weight_ref[...], consts_ref[1:2, :])
+        add_sum(newton, sums_ref, states_ref, parts, new_sums_ref)
+        fold(parts, new_prev_ref, weight_ref, coef_refs, mats_ref, vecs_ref, map_ref)
+        send_on(consts_ref[0:1, :], map_ref, sent_ref)
+
+
+def add_sum(newton, sums_ref, states_ref, parts, new_sums_ref):
     done = weighted_square(states_ref[...], parts[4])
     lane = lax.broadcasted_iota(jnp.int32, new_sums_ref.shape, 1)
-    new_sums_ref[...] = jnp.where(lane == newton, done, sums_ref[...] if newton > 0 else 0.0)
-    if not last:
-        fold(parts, prev_ref, weight_ref, coef_refs, mats_ref, vecs_ref, map_ref)
-        send_on(consts_ref[0:1, :], map_ref, sent_ref)
+    new_sums_ref[...] = jnp.where(lane == newton, done, sums_ref[...])
+
+
+def last_kernel(newton, sides, consts_ref, gates_ref, weight_ref, *refs):
+    sides_refs, refs = [refs[5 * i : 5 * i + 5] for i in range(sides)], refs[5 * sides :]
+    out_ref, new_sums_ref, prev_ref, states_ref, sums_ref = refs
+    for side, (start_ref, old_prev_ref, old_mats_ref, old_vecs_ref, old_sums_ref) in enumerate(sides_refs):
+
+        @pl.when((group() == 0) == (side == 0))
+        def _():
+            entering = start_ref[0:1, :]
+            unfold(entering, old_prev_ref, old_mats_ref, old_vecs_ref, states_ref)
+            shift_in(entering, states_ref, prev_ref)
+            sums_ref[...] = old_sums_ref[...]
+
+    share = out_ref.shape[0]
+    first = pl.multiple_of(lax.rem(lax.axis_index("tm"), SPAN) * share, share)
+    out_ref[...] = states_ref[pl.ds(first, share), :]
+    parts = cell(gates_ref[...], prev_ref[...], weight_ref[...], consts_ref[1:2, :])
+    add_sum(newton, sums_ref, states_ref, parts, new_sums_ref)
 
 
 def call(kernel, args, outs, scratch=(), space=pltpu.VMEM):
@@ -257,7 +266,7 @@
         in_specs=[pl.BlockSpec(memory_space=space)] * len(args),
         out_specs=[pl.BlockSpec(memory_space=pltpu.VMEM)] * len(outs),
         scratch_shapes=[pltpu.VMEM(one, F32) if isinstance(one, tuple) else one for one in scratch],
-        compiler_params=pltpu.CompilerParams(vmem_limit_bytes=24 * 1024 * 1024),
+        compiler_params=pltpu.CompilerParams(vmem_limit_bytes=16 * 1024 * 1024),
     )(*args)
 
 
@@ -277,14 +286,13 @@
     return value
 
 
-def carry(consts, own_map, sent):
+def carry(sent, own_map):
     count = lax.axis_size("tm")
-    ring = [(i, (i + SPAN) % count) for i in range(count)]
-    arrived = []
-    for hop in range(count // SPAN - 1):
-        if hop > 0:
-            (sent,) = call(hop_kernel, [consts, own_map, *arrived], [sent.shape])
-        arrived = [lax.ppermute(sent, "tm", ring)]
+    onward = [(i, i + SPAN) for i in range(count - SPAN)]
+    arrived = lax.ppermute(sent, "tm", onward)
+    for _ in range(count // SPAN - 2):
+        (further,) = call(hop_kernel, [sent, *own_map, arrived], [sent.shape])
+        arrived = lax.ppermute(further, "tm", onward)
     return arrived
 
 
@@ -297,8 +305,11 @@
     steps = share * SPAN
     slots = steps + CHAINS
     rows, wide = (steps, units), (steps, 3 * units)
-    fold_outs = [rows, (slots, units, units), (slots, units), (units + 8, units), (8, units)]
+    sides = min(2, lax.axis_size("tm") // SPAN)
+    fold_outs = [(8, units), rows, (slots, units, units), (slots, units), (8, units)]
     coefs = [rows] * 5
+    onward = lax.axis_size("tm") // SPAN > 2
+    map_out, map_scratch = [(units + 8, units)] * onward, [(units + 8, units)] * (not onward)
     own, in_rows, weight, bias, consts = call(
         fetch_kernel,
         [inputs.reshape(share, -1), h_start, in_weight, rec_weight, row(update_bias), row(reset_bias),
@@ -309,22 +320,29 @@
         space=pltpu.HBM,
     )
     shares = [own] + [exchanged(own, "tm", k) for k in range(1, SPAN)]
-    gates, prev, mats, vecs, own_map, sent = call(
-        first_kernel, [consts, in_rows, bias, weight, *shares], [wide] + fold_outs,
-        [(SPAN, share, units)] + coefs,
+    gates, *solved = call(
+        first_kernel, [consts, in_rows, bias, weight, *shares], [wide] + fold_outs + map_out,
+        map_scratch + [(SPAN, share, units)] + coefs,
     )
-    sums = []
+    held = [solved] * sides
     for newton in range(ITERS):
-        arrived = carry(consts, own_map, sent)
-        args = [consts, gates, prev, mats, vecs, weight, *arrived, *sums]
-        kernel = functools.partial(next_kernel, newton, len(arrived))
-        if newton == ITERS - 1:
-            states, total = call(kernel, args, [(share, units), (8, units)], [rows, rows])
+        starts = [consts] + [carry(held[0][4], held[-1][5:])] * (sides - 1)
+        if newton < ITERS - 1:
+            held = [
+                call(
+                    functools.partial(middle_kernel, newton, side == 0),
+                    [starts[side], consts, gates, weight, *held[side][1:4], held[side][0]],
+                    fold_outs + map_out,
+                    map_scratch + [rows] + coefs,
+                )
+                for side in range(sides)
+            ]
         else:
-            total, prev, mats, vecs, own_map, sent = call(
-                kernel, args, [(8, units)] + fold_outs, [rows] + coefs
+            args = [one for side in range(sides) for one in (starts[side], *held[side][1:4], held[side][0])]
+            states, total = call(
+                functools.partial(last_kernel, newton, sides), [consts, gates, weight, *args],
+                [(share, units), (8, units)], [rows, rows, (8, units)],
             )
-        sums = [total]
     totals = summed(summed(total, "batch"), "tm", SPAN)[0, :ITERS]
     denom = lax.axis_size("batch") * sequences * units * (share * lax.axis_size("tm") + 1) / 2.0
     residual_norms = jnp.sqrt(totals / denom + 1e-06)

time: 44.8 us -> 40.6 us (0.906)
  waiting for transfers between devices: 11.1 us -> 7.42 us
  Pallas kernels: 18 us -> 16.2 us
  starting transfers between devices: 14.4 us -> 15.6 us
    ppermute x2, waiting for transfers between devices: 3.84 us -> 0.51 us  [carry(): arrived = lax.ppermute(sent, 'tm', onward)]
    pallas_call x4 -> x5, Pallas kernels: 18 us -> 16.2 us  [call(): pl.pallas_call(kernel, out_shape=[jax.ShapeDtypeStruct(o, F32) if isinsta...]
    ppermute x2, starting transfers between devices: 5.17 us -> 5.79 us  [carry(): arrived = lax.ppermute(sent, 'tm', onward)]
    ppermute x7, starting transfers between devices: 9.2 us -> 9.8 us  [exchanged(): lax.ppermute(value, axis, [(i, i ^ by) for i in range(lax.axis_size(axis))])]
  transfers between devices with their start and end apart: 9 -> 9, of which waited for: 8 -> 7; matrix products, arithmetic and copies ran while one was open for 0% -> 0% of each run, Pallas kernels for 0% -> 19%
where the time goes in v5:
time: 40.6 us; the launch traced here: 40.4 us
  Pallas kernels  16.2 us (40%)
  starting transfers between devices  15.6 us (38%)
  waiting for transfers between devices  7.42 us (18%)
  between operations  0.68 us (2%)
  other arithmetic  0.53 us (1%)
    pallas_call x5, Pallas kernels, call(): pl.pallas_call(kernel, out_shape=[jax.ShapeDtypeStruct(o, F32) if isinsta...  16.2 us
    ppermute x7, starting transfers between devices, exchanged(): lax.ppermute(value, axis, [(i, i ^ by) for i in range(lax.axis_size(axis))])  9.8 us
    ppermute x7, waiting for transfers between devices, exchanged(): lax.ppermute(value, axis, [(i, i ^ by) for i in range(lax.axis_size(axis))])  6.91 us
    ppermute x2, starting transfers between devices, carry(): arrived = lax.ppermute(sent, 'tm', onward)  5.79 us
  transfers between devices with their start and end apart: 9, of which 7 were waited for; matrix products, arithmetic and copies ran while one was open for 0% of the time, Pallas kernels for 19%

profile of v5, /device:TPU:0, one launch (start us, length us, event | category | flops | bytes accessed | tf_op | source)
XLA Modules:
  0.0 40.4 jit_solution(11311361657533980753)
XLA Ops:
  0.6 1.1 %shard_map.95 = (f32[32,128]{1,0:T(8,128)S(1)}, bf16[128,384]{1,0:T(8,128)(2,1)S(1)}, f32[128,384]{1,0:T(8,128)S(1)}, f32[1,384]{1,0:T(1,128)S(1)}, f32[8,128]{1,0:T(8,128)S(1)}) custom-call(bf16[32,128]{1,0:T(8,128)(2,1)} %bitcast.10, f32[1,128]{1,0:T(1,128)} %start_hbm.1, bf16[128,384]{1,0:T(8,128)(2,1)} %in_weight_hbm.1, f32[128,384]{1,0:T(8,128)} %weight_hbm.1, ...), custom_call_target="tpu_custom_call" | custom-call | tf_op jit(solution)/shard_map/pallas_call | solution.py:263
  1.7 4.0 %collective-permute-start.2 = (f32[32,128]{1,0:T(8,128)S(1)}, f32[32,128]{1,0:T(8,128)S(1)}, u32[]{:S(2)}, u32[]{:S(2)}) collective-permute-start(f32[32,128]{1,0:T(8,128)S(1)} %get-tuple-element.28.refs_0_), channel_id=1, source_target_pairs={{0,12},{4,8},{8,4},{12,0},{16,28},{20,24},{24,20},{28,16},{1,13},{... | collective-permute-start | bytes 49160 | tf_op jit(solution)/shard_map/ppermute | solution.py:274
  5.8 0.4 %collective-permute-start.1 = (f32[32,128]{1,0:T(8,128)S(1)}, f32[32,128]{1,0:T(8,128)S(1)}, u32[]{:S(2)}, u32[]{:S(2)}) collective-permute-start(f32[32,128]{1,0:T(8,128)S(1)} %get-tuple-element.28.refs_0_), channel_id=1, source_target_pairs={{0,8},{4,12},{8,0},{12,4},{16,24},{20,28},{24,16},{28,20},{1,9},{5... | collective-permute-start | bytes 49160 | tf_op jit(solution)/shard_map/ppermute | solution.py:274
  6.2 0.2 collective-permute-start
  6.4 1.1 %collective-permute-done.2.refs_3_ = f32[32,128]{1,0:T(8,128)S(1)} collective-permute-done((f32[32,128]{1,0:T(8,128)S(1)}, f32[32,128]{1,0:T(8,128)S(1)}, u32[]{:S(2)}, u32[]{:S(2)}) %collective-permute-start.2) | collective-permute-done | bytes 16416 | tf_op jit(solution)/shard_map/ppermute | solution.py:274
  7.5 2.0 %collective-permute-done.1.refs_2_ = f32[32,128]{1,0:T(8,128)S(1)} collective-permute-done((f32[32,128]{1,0:T(8,128)S(1)}, f32[32,128]{1,0:T(8,128)S(1)}, u32[]{:S(2)}, u32[]{:S(2)}) %collective-permute-start.1) | collective-permute-done | bytes 16416 | tf_op jit(solution)/shard_map/ppermute | solution.py:274
  9.5 0.4 %collective-permute-done.refs_1_ = f32[32,128]{1,0:T(8,128)S(1)} collective-permute-done((f32[32,128]{1,0:T(8,128)S(1)}, f32[32,128]{1,0:T(8,128)S(1)}, u32[]{:S(2)}, u32[]{:S(2)}) %collective-permute-start) | collective-permute-done | bytes 16416 | tf_op jit(solution)/shard_map/ppermute | solution.py:274
  9.9 5.9 %shard_map.96 = (f32[128,384]{1,0:T(8,128)S(1)}, f32[8,128]{1,0:T(8,128)S(1)}, f32[128,128]{1,0:T(8,128)S(1)}, f32[144,128,128]{2,1,0:T(8,128)S(1)}, f32[144,128]{1,0:T(8,128)S(1)}, /*index=5*/f32[8,128]{1,0:T(8,128)S(1)}) custom-call(f32[8,128]{1,0:T(8,128)S(1)} %get-tuple-element.24.consts_ref.start_ref.refs_0_, ...), custom_call_target="tpu_custom_call" | custom-call | tf_op jit(solution)/shard_map/pallas_call | solution.py:263
  15.8 4.5 %collective-permute-start.4 = (f32[8,128]{1,0:T(8,128)S(1)}, f32[8,128]{1,0:T(8,128)S(1)}, u32[]{:S(2)}, u32[]{:S(2)}) collective-permute-start(f32[8,128]{1,0:T(8,128)S(1)} %get-tuple-element.39), channel_id=1, source_target_pairs={{0,16},{4,20},{8,24},{12,28},{1,17},{5,21},{9,25},{13,29},{2,18},{... | collective-permute-start | bytes 12296 | tf_op jit(solution)/shard_map/ppermute | solution.py:292
  20.3 6.7 %shard_map.97 = (f32[8,128]{1,0:T(8,128)S(1)}, f32[128,128]{1,0:T(8,128)S(1)}, f32[144,128,128]{2,1,0:T(8,128)S(1)}, f32[144,128]{1,0:T(8,128)S(1)}, f32[8,128]{1,0:T(8,128)S(1)}) custom-call(f32[8,128]{1,0:T(8,128)S(1)} %get-tuple-element.24.consts_ref.start_ref.refs_0_, f32[8,128]{1,0:T(8,128)S(1)} %get-tuple-element.24.consts_ref.start_ref.refs_0_, ...), custom_call_target="tpu_custom_call" | custom-call | tf_op jit(solution)/shard_map/pallas_call | solution.py:263
  27.0 1.3 %collective-permute-start.3 = (f32[8,128]{1,0:T(8,128)S(1)}, f32[8,128]{1,0:T(8,128)S(1)}, u32[]{:S(2)}, u32[]{:S(2)}) collective-permute-start(f32[8,128]{1,0:T(8,128)S(1)} %get-tuple-element.38), channel_id=1, source_target_pairs={{0,16},{4,20},{8,24},{12,28},{1,17},{5,21},{9,25},{13,29},{2,18},{... | collective-permute-start | bytes 12296 | tf_op jit(solution)/shard_map/ppermute | solution.py:292
  28.3 0.0 collective-permute-done.4.start_ref
  28.3 0.8 %shard_map.98 = (f32[8,128]{1,0:T(8,128)S(1)}, f32[128,128]{1,0:T(8,128)S(1)}, f32[144,128,128]{2,1,0:T(8,128)S(1)}, f32[144,128]{1,0:T(8,128)S(1)}, f32[8,128]{1,0:T(8,128)}) custom-call(f32[8,128]{1,0:T(8,128)S(1)} %collective-permute-done.4.start_ref, f32[8,128]{1,0:T(8,128)S(1)} %get-tuple-element.24.consts_ref.start_ref.refs_0_, ...), custom_call_target="tpu_custom_call" | custom-call | tf_op jit(solution)/shard_map/pallas_call | solution.py:263
  29.1 0.5 %collective-permute-done.3.refs_5_ = f32[8,128]{1,0:T(8,128)S(1)} collective-permute-done((f32[8,128]{1,0:T(8,128)S(1)}, f32[8,128]{1,0:T(8,128)S(1)}, u32[]{:S(2)}, u32[]{:S(2)}) %collective-permute-start.3) | collective-permute-done | bytes 4128 | tf_op jit(solution)/shard_map/ppermute | solution.py:292
  29.6 1.7 %shard_map.99 = (f32[32,128]{1,0:T(8,128)}, f32[8,128]{1,0:T(8,128)S(1)}) custom-call(f32[8,128]{1,0:T(8,128)S(1)} %get-tuple-element.24.consts_ref.start_ref.refs_0_, f32[128,384]{1,0:T(8,128)S(1)} %get-tuple-element.29.gates_ref, f32[128,384]{1,0:T(8,128)S(1)} %get-tuple-element.27.weight_ref, f32[8,128]{1,0:T(8,128)S(1)} %get-tuple-element.24.consts_ref.start_ref.refs_0_, ...), custom_call_target="tpu_custom_call" | custom-call | tf_op jit(solution)/shard_map/pallas_call | solution.py:263
  31.3 0.0 collective-permute-start.7
  31.4 1.5 %collective-permute-start.6 = (f32[8,128]{1,0:T(8,128)S(1)}, f32[8,128]{1,0:T(8,128)S(1)}, u32[]{:S(2)}, u32[]{:S(2)}) collective-permute-start(f32[8,128]{1,0:T(8,128)S(1)} %get-tuple-element.45), channel_id=1, source_target_pairs={{0,2},{1,3},{2,0},{3,1},{4,6},{5,7},{6,4},{7,5},{8,10},{9,11},{10,... | collective-permute-start | bytes 12296 | tf_op jit(solution)/shard_map/ppermute | solution.py:274
  32.9 0.3 collective-permute-start.5
  33.2 1.2 %collective-permute-done.7 = f32[8,128]{1,0:T(8,128)S(1)} collective-permute-done((f32[8,128]{1,0:T(8,128)S(1)}, f32[8,128]{1,0:T(8,128)S(1)}, u32[]{:S(2)}, u32[]{:S(2)}) %collective-permute-start.7) | collective-permute-done | bytes 4128 | tf_op jit(solution)/shard_map/ppermute | solution.py:274
  34.4 0.6 %collective-permute-done.6 = f32[8,128]{1,0:T(8,128)S(1)} collective-permute-done((f32[8,128]{1,0:T(8,128)S(1)}, f32[8,128]{1,0:T(8,128)S(1)}, u32[]{:S(2)}, u32[]{:S(2)}) %collective-permute-start.6) | collective-permute-done | bytes 4128 | tf_op jit(solution)/shard_map/ppermute | solution.py:274
  35.0 0.0 collective-permute-done.5
  35.0 3.2 %collective-permute-start.8 = (f32[8,128]{1,0:T(8,128)S(1)}, f32[8,128]{1,0:T(8,128)S(1)}, u32[]{:S(2)}, u32[]{:S(2)}) collective-permute-start(f32[8,128]{1,0:T(8,128)S(1)} %add_add_fusion), channel_id=1, source_target_pairs={{0,16},{4,20},{8,24},{12,28},{16,0},{20,4},{24,8},{28,12},{1,17},{... | collective-permute-start | bytes 12296 | tf_op jit(solution)/shard_map/ppermute | solution.py:274
  38.3 1.6 %collective-permute-done.8 = f32[8,128]{1,0:T(8,128)S(1)} collective-permute-done((f32[8,128]{1,0:T(8,128)S(1)}, f32[8,128]{1,0:T(8,128)S(1)}, u32[]{:S(2)}, u32[]{:S(2)}) %collective-permute-start.8) | collective-permute-done | bytes 4128 | tf_op jit(solution)/shard_map/ppermute | solution.py:274
  39.8 0.5 %sqrt_bitcast_fusion = f32[2]{0:T(128)} fusion(f32[8,128]{1,0:T(8,128)S(1)} %add.19), kind=kLoop, calls=%fused_computation.1 | loop fusion | flops 4 | bytes 16 | tf_op jit(solution)/shard_map/sqrt | solution.py:348
  (2 shorter events, 0.0 us)
Async XLA Ops:
  1.7 5.8 %collective-permute-start.2 = (f32[32,128]{1,0:T(8,128)S(1)}, f32[32,128]{1,0:T(8,128)S(1)}, u32[]{:S(2)}, u32[]{:S(2)}) collective-permute-start(f32[32,128]{1,0:T(8,128)S(1)} %get-tuple-element.28.refs_0_), channel_id=1, source_target_pairs={{0,12},{4,8},{8,4},{12,0},{16,28},{20,24},{24,20},{28,16},{1,13},{... | collective-permute-start | bytes 49160 | tf_op jit(solution)/shard_map/ppermute | solution.py:274
  5.8 3.7 %collective-permute-start.1 = (f32[32,128]{1,0:T(8,128)S(1)}, f32[32,128]{1,0:T(8,128)S(1)}, u32[]{:S(2)}, u32[]{:S(2)}) collective-permute-start(f32[32,128]{1,0:T(8,128)S(1)} %get-tuple-element.28.refs_0_), channel_id=1, source_target_pairs={{0,8},{4,12},{8,0},{12,4},{16,24},{20,28},{24,16},{28,20},{1,9},{5... | collective-permute-start | bytes 49160 | tf_op jit(solution)/shard_map/ppermute | solution.py:274
  6.2 3.7 %collective-permute-start = (f32[32,128]{1,0:T(8,128)S(1)}, f32[32,128]{1,0:T(8,128)S(1)}, u32[]{:S(2)}, u32[]{:S(2)}) collective-permute-start(f32[32,128]{1,0:T(8,128)S(1)} %get-tuple-element.28.refs_0_), channel_id=1, source_target_pairs={{0,4},{4,0},{8,12},{12,8},{16,20},{20,16},{24,28},{28,24},{1,5},{5... | collective-permute-start | bytes 49160 | tf_op jit(solution)/shard_map/ppermute | solution.py:274
  15.8 12.5 %collective-permute-start.4 = (f32[8,128]{1,0:T(8,128)S(1)}, f32[8,128]{1,0:T(8,128)S(1)}, u32[]{:S(2)}, u32[]{:S(2)}) collective-permute-start(f32[8,128]{1,0:T(8,128)S(1)} %get-tuple-element.39), channel_id=1, source_target_pairs={{0,16},{4,20},{8,24},{12,28},{1,17},{5,21},{9,25},{13,29},{2,18},{... | collective-permute-start | bytes 12296 | tf_op jit(solution)/shard_map/ppermute | solution.py:292
  27.0 2.6 %collective-permute-start.3 = (f32[8,128]{1,0:T(8,128)S(1)}, f32[8,128]{1,0:T(8,128)S(1)}, u32[]{:S(2)}, u32[]{:S(2)}) collective-permute-start(f32[8,128]{1,0:T(8,128)S(1)} %get-tuple-element.38), channel_id=1, source_target_pairs={{0,16},{4,20},{8,24},{12,28},{1,17},{5,21},{9,25},{13,29},{2,18},{... | collective-permute-start | bytes 12296 | tf_op jit(solution)/shard_map/ppermute | solution.py:292
  31.3 3.0 %collective-permute-start.7 = (f32[8,128]{1,0:T(8,128)S(1)}, f32[8,128]{1,0:T(8,128)S(1)}, u32[]{:S(2)}, u32[]{:S(2)}) collective-permute-start(f32[8,128]{1,0:T(8,128)S(1)} %get-tuple-element.45), channel_id=1, source_target_pairs={{0,3},{1,2},{2,1},{3,0},{4,7},{5,6},{6,5},{7,4},{8,11},{9,10},{10,... | collective-permute-start | bytes 12296 | tf_op jit(solution)/shard_map/ppermute | solution.py:274
  31.4 3.6 %collective-permute-start.6 = (f32[8,128]{1,0:T(8,128)S(1)}, f32[8,128]{1,0:T(8,128)S(1)}, u32[]{:S(2)}, u32[]{:S(2)}) collective-permute-start(f32[8,128]{1,0:T(8,128)S(1)} %get-tuple-element.45), channel_id=1, source_target_pairs={{0,2},{1,3},{2,0},{3,1},{4,6},{5,7},{6,4},{7,5},{8,10},{9,11},{10,... | collective-permute-start | bytes 12296 | tf_op jit(solution)/shard_map/ppermute | solution.py:274
  32.9 2.1 %collective-permute-start.5 = (f32[8,128]{1,0:T(8,128)S(1)}, f32[8,128]{1,0:T(8,128)S(1)}, u32[]{:S(2)}, u32[]{:S(2)}) collective-permute-start(f32[8,128]{1,0:T(8,128)S(1)} %get-tuple-element.45), channel_id=1, source_target_pairs={{0,1},{1,0},{2,3},{3,2},{4,5},{5,4},{6,7},{7,6},{8,9},{9,8},{10,11... | collective-permute-start | bytes 12296 | tf_op jit(solution)/shard_map/ppermute | solution.py:274
  35.0 4.8 %collective-permute-start.8 = (f32[8,128]{1,0:T(8,128)S(1)}, f32[8,128]{1,0:T(8,128)S(1)}, u32[]{:S(2)}, u32[]{:S(2)}) collective-permute-start(f32[8,128]{1,0:T(8,128)S(1)} %add_add_fusion), channel_id=1, source_target_pairs={{0,16},{4,20},{8,24},{12,28},{16,0},{20,4},{24,8},{28,12},{1,17},{... | collective-permute-start | bytes 12296 | tf_op jit(solution)/shard_map/ppermute | solution.py:274

commit v6 on v5

--- a/solution.py
+++ b/solution.py
@@ -192,25 +192,30 @@
     consts_ref[2:, :] = jnp.zeros((6, units), F32)
 
 
-def first_kernel(consts_ref, in_weight_ref, bias_ref, weight_ref, *refs):
+def first_kernel(at_front, consts_ref, in_weight_ref, bias_ref, weight_ref, *refs):
     shares, refs = refs[:SPAN], refs[SPAN:]
     gates_ref, sums_ref, prev_ref, mats_ref, vecs_ref, sent_ref, map_ref, held_ref, *coef_refs = refs
-    sums_ref[...] = jnp.zeros(sums_ref.shape, F32)
     steps, units = prev_ref.shape
-    mine = lax.axis_index("tm")
-    place = lax.rem(mine, SPAN)
-    for k in range(SPAN):
-        held_ref[k] = shares[k][...]
-    inputs = jnp.concatenate([held_ref[place ^ j] for j in range(SPAN)], axis=0).astype(BF16)
-    gates = jnp.dot(inputs, in_weight_ref[...], preferred_element_type=F32) + bias_ref[...]
-    gates_ref[...] = gates
-    start = consts_ref[0:1, :]
-    at_start = (mine < SPAN) & (lax.broadcasted_iota(jnp.int32, (steps, units), 0) == 0)
-    previous = jnp.where(at_start, start, 0.0)
-    prev_ref[...] = previous
-    parts = cell(gates, previous, weight_ref[...], consts_ref[1:2, :])
-    fold(parts, prev_ref, weight_ref, coef_refs, mats_ref, vecs_ref, map_ref)
-    send_on(start, map_ref, sent_ref)
+    place = lax.rem(lax.axis_index("tm"), SPAN)
+
+    @pl.when((group() == 0) == at_front)
+    def _():
+        sums_ref[...] = jnp.zeros(sums_ref.shape, F32)
+        for k in range(SPAN):
+            held_ref[k] = shares[k][...]
+        inputs = jnp.concatenate([held_ref[place ^ j] for j in range(SPAN)], axis=0).astype(BF16)
+        gates = jnp.dot(inputs, in_weight_ref[...], preferred_element_type=F32) + bias_ref[...]
+        gates_ref[...] = gates
+        start = consts_ref[0:1, :]
+        previous = jnp.zeros((steps, units), F32)
+        if at_front:
+            row = lax.broadcasted_iota(jnp.int32, (steps, units), 0)
+            previous = jnp.where(row == 0, start, 0.0)
+        prev_ref[...] = previous
+        parts = cell(gates, previous, weight_ref[...], consts_ref[1:2, :])
+        fold(parts, prev_ref, weight_ref, coef_refs, mats_ref, vecs_ref, map_ref)
+        if at_front:
+            send_on(start, map_ref, sent_ref)
 
 
 def hop_kernel(sent_first_ref, map_ref, arrived_ref, sent_ref):
@@ -230,7 +235,8 @@
         parts = cell(gates_ref[...], new_prev_ref[...], weight_ref[...], consts_ref[1:2, :])
         add_sum(newton, sums_ref, states_ref, parts, new_sums_ref)
         fold(parts, new_prev_ref, weight_ref, coef_refs, mats_ref, vecs_ref, map_ref)
-        send_on(consts_ref[0:1, :], map_ref, sent_ref)
+        if at_front:
+            send_on(entering, map_ref, sent_ref)
 
 
 def add_sum(newton, sums_ref, states_ref, parts, new_sums_ref):
@@ -239,23 +245,22 @@
     new_sums_ref[...] = jnp.where(lane == newton, done, sums_ref[...])
 
 
-def last_kernel(newton, sides, consts_ref, gates_ref, weight_ref, *refs):
-    sides_refs, refs = [refs[5 * i : 5 * i + 5] for i in range(sides)], refs[5 * sides :]
-    out_ref, new_sums_ref, prev_ref, states_ref, sums_ref = refs
-    for side, (start_ref, old_prev_ref, old_mats_ref, old_vecs_ref, old_sums_ref) in enumerate(sides_refs):
+def last_kernel(newton, sides, consts_ref, weight_ref, *refs):
+    sides_refs, refs = [refs[6 * i : 6 * i + 6] for i in range(sides)], refs[6 * sides :]
+    out_ref, new_sums_ref, prev_ref, states_ref = refs
+    for side, (start_ref, gates_ref, sums_ref, old_prev_ref, old_mats_ref, old_vecs_ref) in enumerate(sides_refs):
 
         @pl.when((group() == 0) == (side == 0))
         def _():
             entering = start_ref[0:1, :]
             unfold(entering, old_prev_ref, old_mats_ref, old_vecs_ref, states_ref)
             shift_in(entering, states_ref, prev_ref)
-            sums_ref[...] = old_sums_ref[...]
+            parts = cell(gates_ref[...], prev_ref[...], weight_ref[...], consts_ref[1:2, :])
+            add_sum(newton, sums_ref, states_ref, parts, new_sums_ref)
 
     share = out_ref.shape[0]
     first = pl.multiple_of(lax.rem(lax.axis_index("tm"), SPAN) * share, share)
     out_ref[...] = states_ref[pl.ds(first, share), :]
-    parts = cell(gates_ref[...], prev_ref[...], weight_ref[...], consts_ref[1:2, :])
-    add_sum(newton, sums_ref, states_ref, parts, new_sums_ref)
 
 
 def call(kernel, args, outs, scratch=(), space=pltpu.VMEM):
@@ -306,10 +311,13 @@
     slots = steps + CHAINS
     rows, wide = (steps, units), (steps, 3 * units)
     sides = min(2, lax.axis_size("tm") // SPAN)
-    fold_outs = [(8, units), rows, (slots, units, units), (slots, units), (8, units)]
+    fold_outs = [(8, units), rows, (slots, units, units), (slots, units)]
     coefs = [rows] * 5
-    onward = lax.axis_size("tm") // SPAN > 2
-    map_out, map_scratch = [(units + 8, units)] * onward, [(units + 8, units)] * (not onward)
+    state_row, map_rows = (8, units), (units + 8, units)
+    further = lax.axis_size("tm") // SPAN > 2
+    ends = [([state_row], [map_rows])]
+    if sides > 1:
+        ends.append(([state_row, map_rows], []) if further else ([], [state_row, map_rows]))
     own, in_rows, weight, bias, consts = call(
         fetch_kernel,
         [inputs.reshape(share, -1), h_start, in_weight, rec_weight, row(update_bias), row(reset_bias),
@@ -320,28 +328,28 @@
         space=pltpu.HBM,
     )
     shares = [own] + [exchanged(own, "tm", k) for k in range(1, SPAN)]
-    gates, *solved = call(
-        first_kernel, [consts, in_rows, bias, weight, *shares], [wide] + fold_outs + map_out,
-        map_scratch + [(SPAN, share, units)] + coefs,
-    )
-    held = [solved] * sides
+    held = []
+    for side, (out, kept) in enumerate(ends):
+        held.append(call(
+            functools.partial(first_kernel, side == 0), [consts, in_rows, bias, weight, *shares],
+            [wide] + fold_outs + out, kept + [(SPAN, share, units)] + coefs,
+        ))
     for newton in range(ITERS):
-        starts = [consts] + [carry(held[0][4], held[-1][5:])] * (sides - 1)
+        starts = [consts] + [carry(held[0][5], held[-1][6:])] * (sides - 1)
         if newton < ITERS - 1:
             held = [
-                call(
+                held[side][:1] + call(
                     functools.partial(middle_kernel, newton, side == 0),
-                    [starts[side], consts, gates, weight, *held[side][1:4], held[side][0]],
-                    fold_outs + map_out,
-                    map_scratch + [rows] + coefs,
+                    [starts[side], consts, held[side][0], weight, *held[side][2:5], held[side][1]],
+                    fold_outs + out, kept + [rows] + coefs,
                 )
-                for side in range(sides)
+                for side, (out, kept) in enumerate(ends)
             ]
         else:
-            args = [one for side in range(sides) for one in (starts[side], *held[side][1:4], held[side][0])]
+            args = [one for side in range(sides) for one in (starts[side], *held[side][:5])]
             states, total = call(
-                functools.partial(last_kernel, newton, sides), [consts, gates, weight, *args],
-                [(share, units), (8, units)], [rows, rows, (8, units)],
+                functools.partial(last_kernel, newton, sides), [consts, weight, *args],
+                [(share, units), (8, units)], [rows, rows],
             )
     totals = summed(summed(total, "batch"), "tm", SPAN)[0, :ITERS]
     denom = lax.axis_size("batch") * sequences * units * (share * lax.axis_size("tm") + 1) / 2.0

time: 40.6 us -> 39 us (0.961)
  starting transfers between devices: 15.6 us -> 12.2 us
  waiting for transfers between devices: 7.42 us -> 9.94 us
  Pallas kernels: 16.2 us -> 15.4 us
    ppermute x2, starting transfers between devices: 5.79 us -> 2.58 us  [carry(): arrived = lax.ppermute(sent, 'tm', onward)]
    ppermute x7, waiting for transfers between devices: 6.91 us -> 8.88 us  [exchanged(): lax.ppermute(value, axis, [(i, i ^ by) for i in range(lax.axis_size(axis))])]
    pallas_call x5 -> x6, Pallas kernels: 16.2 us -> 15.4 us  [call(): pl.pallas_call(kernel, out_shape=[jax.ShapeDtypeStruct(o, F32) if isinsta...]
    ppermute x2, waiting for transfers between devices: 0.51 us -> 1.06 us  [carry(): arrived = lax.ppermute(sent, 'tm', onward)]
  transfers between devices with their start and end apart: 9 -> 9, of which waited for: 7 -> 7; matrix products, arithmetic and copies ran while one was open for 0% -> 0% of each run, Pallas kernels for 19% -> 18%
where the time goes in v6:
time: 39 us; the launch traced here: 38.8 us
  Pallas kernels  15.4 us (39%)
  starting transfers between devices  12.2 us (31%)
  waiting for transfers between devices  9.94 us (25%)
  between operations  0.69 us (2%)
  other arithmetic  0.53 us (1%)
    pallas_call x6, Pallas kernels, call(): pl.pallas_call(kernel, out_shape=[jax.ShapeDtypeStruct(o, F32) if isinsta...  15.4 us
    ppermute x7, starting transfers between devices, exchanged(): lax.ppermute(value, axis, [(i, i ^ by) for i in range(lax.axis_size(axis))])  9.64 us
    ppermute x7, waiting for transfers between devices, exchanged(): lax.ppermute(value, axis, [(i, i ^ by) for i in range(lax.axis_size(axis))])  8.88 us
    ppermute x2, starting transfers between devices, carry(): arrived = lax.ppermute(sent, 'tm', onward)  2.58 us
    ppermute x2, waiting for transfers between devices, carry(): arrived = lax.ppermute(sent, 'tm', onward)  1.06 us
  transfers between devices with their start and end apart: 9, of which 7 were waited for; matrix products, arithmetic and copies ran while one was open for 0% of the time, Pallas kernels for 18%

profile of v6, /device:TPU:0, one launch (start us, length us, event | category | flops | bytes accessed | tf_op | source)
XLA Modules:
  0.0 38.8 jit_solution(2182471083513642181)
XLA Ops:
  0.6 1.1 %shard_map.95 = (f32[32,128]{1,0:T(8,128)S(1)}, bf16[128,384]{1,0:T(8,128)(2,1)S(1)}, f32[128,384]{1,0:T(8,128)S(1)}, f32[1,384]{1,0:T(1,128)S(1)}, f32[8,128]{1,0:T(8,128)S(1)}) custom-call(bf16[32,128]{1,0:T(8,128)(2,1)} %bitcast.10, f32[1,128]{1,0:T(1,128)} %start_hbm.1, bf16[128,384]{1,0:T(8,128)(2,1)} %in_weight_hbm.1, f32[128,384]{1,0:T(8,128)} %weight_hbm.1, ...), custom_call_target="tpu_custom_call" | custom-call | tf_op jit(solution)/shard_map/pallas_call | solution.py:268
  1.7 3.0 %collective-permute-start = (f32[32,128]{1,0:T(8,128)S(1)}, f32[32,128]{1,0:T(8,128)S(1)}, u32[]{:S(2)}, u32[]{:S(2)}) collective-permute-start(f32[32,128]{1,0:T(8,128)S(1)} %get-tuple-element.33.refs_0_), channel_id=1, source_target_pairs={{0,4},{4,0},{8,12},{12,8},{16,20},{20,16},{24,28},{28,24},{1,5},{5... | collective-permute-start | bytes 49160 | tf_op jit(solution)/shard_map/ppermute | solution.py:279
  4.7 1.6 %collective-permute-start.1 = (f32[32,128]{1,0:T(8,128)S(1)}, f32[32,128]{1,0:T(8,128)S(1)}, u32[]{:S(2)}, u32[]{:S(2)}) collective-permute-start(f32[32,128]{1,0:T(8,128)S(1)} %get-tuple-element.33.refs_0_), channel_id=1, source_target_pairs={{0,8},{4,12},{8,0},{12,4},{16,24},{20,28},{24,16},{28,20},{1,9},{5... | collective-permute-start | bytes 49160 | tf_op jit(solution)/shard_map/ppermute | solution.py:279
  6.3 0.0 collective-permute-start.2
  6.3 0.1 collective-permute-done.refs_1_
  6.5 2.0 %collective-permute-done.1.refs_2_ = f32[32,128]{1,0:T(8,128)S(1)} collective-permute-done((f32[32,128]{1,0:T(8,128)S(1)}, f32[32,128]{1,0:T(8,128)S(1)}, u32[]{:S(2)}, u32[]{:S(2)}) %collective-permute-start.1) | collective-permute-done | bytes 16416 | tf_op jit(solution)/shard_map/ppermute | solution.py:279
  8.5 2.5 %collective-permute-done.2.refs_3_ = f32[32,128]{1,0:T(8,128)S(1)} collective-permute-done((f32[32,128]{1,0:T(8,128)S(1)}, f32[32,128]{1,0:T(8,128)S(1)}, u32[]{:S(2)}, u32[]{:S(2)}) %collective-permute-start.2) | collective-permute-done | bytes 16416 | tf_op jit(solution)/shard_map/ppermute | solution.py:279
  11.0 5.7 %shard_map.96 = (f32[128,384]{1,0:T(8,128)S(1)}, f32[8,128]{1,0:T(8,128)S(1)}, f32[128,128]{1,0:T(8,128)S(1)}, f32[144,128,128]{2,1,0:T(8,128)S(1)}, f32[144,128]{1,0:T(8,128)S(1)}, /*index=5*/f32[8,128]{1,0:T(8,128)S(1)}) custom-call(f32[8,128]{1,0:T(8,128)S(1)} %get-tuple-element.29.consts_ref.start_ref.refs_0_, ...), custom_call_target="tpu_custom_call" | custom-call | tf_op jit(solution)/shard_map/pallas_call | solution.py:268
  16.6 1.3 %collective-permute-start.4 = (f32[8,128]{1,0:T(8,128)S(1)}, f32[8,128]{1,0:T(8,128)S(1)}, u32[]{:S(2)}, u32[]{:S(2)}) collective-permute-start(f32[8,128]{1,0:T(8,128)S(1)} %get-tuple-element.45), channel_id=1, source_target_pairs={{0,16},{4,20},{8,24},{12,28},{1,17},{5,21},{9,25},{13,29},{2,18},{... | collective-permute-start | bytes 12296 | tf_op jit(solution)/shard_map/ppermute | solution.py:297
  17.9 6.6 %shard_map.97 = (f32[8,128]{1,0:T(8,128)S(1)}, f32[128,128]{1,0:T(8,128)S(1)}, f32[144,128,128]{2,1,0:T(8,128)S(1)}, f32[144,128]{1,0:T(8,128)S(1)}, f32[8,128]{1,0:T(8,128)S(1)}) custom-call(f32[8,128]{1,0:T(8,128)S(1)} %get-tuple-element.29.consts_ref.start_ref.refs_0_, f32[8,128]{1,0:T(8,128)S(1)} %get-tuple-element.29.consts_ref.start_ref.refs_0_, ...), custom_call_target="tpu_custom_call" | custom-call | tf_op jit(solution)/shard_map/pallas_call | solution.py:268
  24.5 1.3 %collective-permute-start.3 = (f32[8,128]{1,0:T(8,128)S(1)}, f32[8,128]{1,0:T(8,128)S(1)}, u32[]{:S(2)}, u32[]{:S(2)}) collective-permute-start(f32[8,128]{1,0:T(8,128)S(1)} %get-tuple-element.43), channel_id=1, source_target_pairs={{0,16},{4,20},{8,24},{12,28},{1,17},{5,21},{9,25},{13,29},{2,18},{... | collective-permute-start | bytes 12296 | tf_op jit(solution)/shard_map/ppermute | solution.py:297
  25.8 0.2 shard_map.98
  26.0 0.0 collective-permute-done.4.start_ref
  26.1 1.1 %collective-permute-done.3.refs_6_ = f32[8,128]{1,0:T(8,128)S(1)} collective-permute-done((f32[8,128]{1,0:T(8,128)S(1)}, f32[8,128]{1,0:T(8,128)S(1)}, u32[]{:S(2)}, u32[]{:S(2)}) %collective-permute-start.3) | collective-permute-done | bytes 4128 | tf_op jit(solution)/shard_map/ppermute | solution.py:297
  27.1 1.8 %shard_map.100 = (f32[32,128]{1,0:T(8,128)}, f32[8,128]{1,0:T(8,128)S(1)}) custom-call(f32[8,128]{1,0:T(8,128)S(1)} %get-tuple-element.29.consts_ref.start_ref.refs_0_, f32[128,384]{1,0:T(8,128)S(1)} %get-tuple-element.30.weight_ref, f32[8,128]{1,0:T(8,128)S(1)} %get-tuple-element.29.consts_ref.start_ref.refs_0_, ...), custom_call_target="tpu_custom_call" | custom-call | tf_op jit(solution)/shard_map/pallas_call | solution.py:268
  29.0 0.0 collective-permute-start.5
  29.0 1.5 %collective-permute-start.6 = (f32[8,128]{1,0:T(8,128)S(1)}, f32[8,128]{1,0:T(8,128)S(1)}, u32[]{:S(2)}, u32[]{:S(2)}) collective-permute-start(f32[8,128]{1,0:T(8,128)S(1)} %get-tuple-element.55), channel_id=1, source_target_pairs={{0,2},{1,3},{2,0},{3,1},{4,6},{5,7},{6,4},{7,5},{8,10},{9,11},{10,... | collective-permute-start | bytes 12296 | tf_op jit(solution)/shard_map/ppermute | solution.py:279
  30.5 0.4 collective-permute-start.7
  30.8 0.0 collective-permute-done.5
  30.9 1.7 %collective-permute-done.6 = f32[8,128]{1,0:T(8,128)S(1)} collective-permute-done((f32[8,128]{1,0:T(8,128)S(1)}, f32[8,128]{1,0:T(8,128)S(1)}, u32[]{:S(2)}, u32[]{:S(2)}) %collective-permute-start.6) | collective-permute-done | bytes 4128 | tf_op jit(solution)/shard_map/ppermute | solution.py:279
  32.6 0.9 %collective-permute-done.7 = f32[8,128]{1,0:T(8,128)S(1)} collective-permute-done((f32[8,128]{1,0:T(8,128)S(1)}, f32[8,128]{1,0:T(8,128)S(1)}, u32[]{:S(2)}, u32[]{:S(2)}) %collective-permute-start.7) | collective-permute-done | bytes 4128 | tf_op jit(solution)/shard_map/ppermute | solution.py:279
  33.5 3.2 %collective-permute-start.8 = (f32[8,128]{1,0:T(8,128)S(1)}, f32[8,128]{1,0:T(8,128)S(1)}, u32[]{:S(2)}, u32[]{:S(2)}) collective-permute-start(f32[8,128]{1,0:T(8,128)S(1)} %add_add_fusion), channel_id=1, source_target_pairs={{0,16},{4,20},{8,24},{12,28},{16,0},{20,4},{24,8},{28,12},{1,17},{... | collective-permute-start | bytes 12296 | tf_op jit(solution)/shard_map/ppermute | solution.py:279
  36.7 1.6 %collective-permute-done.8 = f32[8,128]{1,0:T(8,128)S(1)} collective-permute-done((f32[8,128]{1,0:T(8,128)S(1)}, f32[8,128]{1,0:T(8,128)S(1)}, u32[]{:S(2)}, u32[]{:S(2)}) %collective-permute-start.8) | collective-permute-done | bytes 4128 | tf_op jit(solution)/shard_map/ppermute | solution.py:279
  38.3 0.5 %sqrt_bitcast_fusion = f32[2]{0:T(128)} fusion(f32[8,128]{1,0:T(8,128)S(1)} %add.19), kind=kLoop, calls=%fused_computation.1 | loop fusion | flops 4 | bytes 16 | tf_op jit(solution)/shard_map/sqrt | solution.py:356
  (3 shorter events, 0.0 us)
Async XLA Ops:
  1.7 4.8 %collective-permute-start = (f32[32,128]{1,0:T(8,128)S(1)}, f32[32,128]{1,0:T(8,128)S(1)}, u32[]{:S(2)}, u32[]{:S(2)}) collective-permute-start(f32[32,128]{1,0:T(8,128)S(1)} %get-tuple-element.33.refs_0_), channel_id=1, source_target_pairs={{0,4},{4,0},{8,12},{12,8},{16,20},{20,16},{24,28},{28,24},{1,5},{5... | collective-permute-start | bytes 49160 | tf_op jit(solution)/shard_map/ppermute | solution.py:279
  4.7 3.7 %collective-permute-start.1 = (f32[32,128]{1,0:T(8,128)S(1)}, f32[32,128]{1,0:T(8,128)S(1)}, u32[]{:S(2)}, u32[]{:S(2)}) collective-permute-start(f32[32,128]{1,0:T(8,128)S(1)} %get-tuple-element.33.refs_0_), channel_id=1, source_target_pairs={{0,8},{4,12},{8,0},{12,4},{16,24},{20,28},{24,16},{28,20},{1,9},{5... | collective-permute-start | bytes 49160 | tf_op jit(solution)/shard_map/ppermute | solution.py:279
  6.3 4.6 %collective-permute-start.2 = (f32[32,128]{1,0:T(8,128)S(1)}, f32[32,128]{1,0:T(8,128)S(1)}, u32[]{:S(2)}, u32[]{:S(2)}) collective-permute-start(f32[32,128]{1,0:T(8,128)S(1)} %get-tuple-element.33.refs_0_), channel_id=1, source_target_pairs={{0,12},{4,8},{8,4},{12,0},{16,28},{20,24},{24,20},{28,16},{1,13},{... | collective-permute-start | bytes 49160 | tf_op jit(solution)/shard_map/ppermute | solution.py:279
  16.6 9.4 %collective-permute-start.4 = (f32[8,128]{1,0:T(8,128)S(1)}, f32[8,128]{1,0:T(8,128)S(1)}, u32[]{:S(2)}, u32[]{:S(2)}) collective-permute-start(f32[8,128]{1,0:T(8,128)S(1)} %get-tuple-element.45), channel_id=1, source_target_pairs={{0,16},{4,20},{8,24},{12,28},{1,17},{5,21},{9,25},{13,29},{2,18},{... | collective-permute-start | bytes 12296 | tf_op jit(solution)/shard_map/ppermute | solution.py:297
  24.5 2.6 %collective-permute-start.3 = (f32[8,128]{1,0:T(8,128)S(1)}, f32[8,128]{1,0:T(8,128)S(1)}, u32[]{:S(2)}, u32[]{:S(2)}) collective-permute-start(f32[8,128]{1,0:T(8,128)S(1)} %get-tuple-element.43), channel_id=1, source_target_pairs={{0,16},{4,20},{8,24},{12,28},{1,17},{5,21},{9,25},{13,29},{2,18},{... | collective-permute-start | bytes 12296 | tf_op jit(solution)/shard_map/ppermute | solution.py:297
  29.0 1.9 %collective-permute-start.5 = (f32[8,128]{1,0:T(8,128)S(1)}, f32[8,128]{1,0:T(8,128)S(1)}, u32[]{:S(2)}, u32[]{:S(2)}) collective-permute-start(f32[8,128]{1,0:T(8,128)S(1)} %get-tuple-element.55), channel_id=1, source_target_pairs={{0,1},{1,0},{2,3},{3,2},{4,5},{5,4},{6,7},{7,6},{8,9},{9,8},{10,11... | collective-permute-start | bytes 12296 | tf_op jit(solution)/shard_map/ppermute | solution.py:279
  29.0 3.6 %collective-permute-start.6 = (f32[8,128]{1,0:T(8,128)S(1)}, f32[8,128]{1,0:T(8,128)S(1)}, u32[]{:S(2)}, u32[]{:S(2)}) collective-permute-start(f32[8,128]{1,0:T(8,128)S(1)} %get-tuple-element.55), channel_id=1, source_target_pairs={{0,2},{1,3},{2,0},{3,1},{4,6},{5,7},{6,4},{7,5},{8,10},{9,11},{10,... | collective-permute-start | bytes 12296 | tf_op jit(solution)/shard_map/ppermute | solution.py:279
  30.5 3.0 %collective-permute-start.7 = (f32[8,128]{1,0:T(8,128)S(1)}, f32[8,128]{1,0:T(8,128)S(1)}, u32[]{:S(2)}, u32[]{:S(2)}) collective-permute-start(f32[8,128]{1,0:T(8,128)S(1)} %get-tuple-element.55), channel_id=1, source_target_pairs={{0,3},{1,2},{2,1},{3,0},{4,7},{5,6},{6,5},{7,4},{8,11},{9,10},{10,... | collective-permute-start | bytes 12296 | tf_op jit(solution)/shard_map/ppermute | solution.py:279
  33.5 4.8 %collective-permute-start.8 = (f32[8,128]{1,0:T(8,128)S(1)}, f32[8,128]{1,0:T(8,128)S(1)}, u32[]{:S(2)}, u32[]{:S(2)}) collective-permute-start(f32[8,128]{1,0:T(8,128)S(1)} %add_add_fusion), channel_id=1, source_target_pairs={{0,16},{4,20},{8,24},{12,28},{16,0},{20,4},{24,8},{28,12},{1,17},{... | collective-permute-start | bytes 12296 | tf_op jit(solution)/shard_map/ppermute | solution.py:279

commit v7 on v6

--- a/solution.py
+++ b/solution.py
@@ -9,7 +9,7 @@
 
 ITERS = 2
 SPAN = 4
-CHAINS = 16
+CHAINS = 8
 PAD = 16
 F32 = jnp.float32
 BF16 = jnp.bfloat16
@@ -202,7 +202,7 @@
     def _():
         sums_ref[...] = jnp.zeros(sums_ref.shape, F32)
         for k in range(SPAN):
-            held_ref[k] = shares[k][...]
+            held_ref[k] = shares[SPAN - 1 - k][...]
         inputs = jnp.concatenate([held_ref[place ^ j] for j in range(SPAN)], axis=0).astype(BF16)
         gates = jnp.dot(inputs, in_weight_ref[...], preferred_element_type=F32) + bias_ref[...]
         gates_ref[...] = gates
@@ -283,7 +283,7 @@
     count = lax.axis_size(axis)
     while by < count:
         radix = min(4, count // by)
-        terms = [value] + [exchanged(value, axis, k * by) for k in range(1, radix)]
+        terms = [exchanged(value, axis, k * by) for k in range(radix - 1, 0, -1)] + [value]
         while len(terms) > 1:
             terms = [a + b for a, b in zip(terms[0::2], terms[1::2])]
         value = terms[0]
@@ -327,7 +327,7 @@
         [pltpu.VMEM((share, units), BF16), (1, units), (1, units), pltpu.SemaphoreType.DMA((8,))],
         space=pltpu.HBM,
     )
-    shares = [own] + [exchanged(own, "tm", k) for k in range(1, SPAN)]
+    shares = [exchanged(own, "tm", k) for k in range(SPAN - 1, 0, -1)] + [own]
     held = []
     for side, (out, kept) in enumerate(ends):
         held.append(call(

time: 39 us -> 37.7 us (0.967)
  waiting for transfers between devices: 9.94 us -> 7.97 us
  Pallas kernels: 15.4 us -> 15.9 us
    ppermute x7, waiting for transfers between devices: 8.88 us -> 6.91 us  [exchanged(): lax.ppermute(value, axis, [(i, i ^ by) for i in range(lax.axis_size(axis))])]
    pallas_call x6, Pallas kernels: 15.4 us -> 15.9 us  [call(): pl.pallas_call(kernel, out_shape=[jax.ShapeDtypeStruct(o, F32) if isinsta...]
  transfers between devices with their start and end apart: 9 -> 9, of which waited for: 7 -> 7; matrix products, arithmetic and copies ran while one was open for 0% -> 0% of each run, Pallas kernels for 18% -> 19%
where the time goes in v7:
time: 37.7 us; the launch traced here: 37.5 us
  Pallas kernels  15.9 us (42%)
  starting transfers between devices  12.4 us (33%)
  waiting for transfers between devices  7.97 us (21%)
  between operations  0.69 us (2%)
  other arithmetic  0.53 us (1%)
    pallas_call x6, Pallas kernels, call(): pl.pallas_call(kernel, out_shape=[jax.ShapeDtypeStruct(o, F32) if isinsta...  15.9 us
    ppermute x7, starting transfers between devices, exchanged(): lax.ppermute(value, axis, [(i, i ^ by) for i in range(lax.axis_size(axis))])  9.78 us
    ppermute x7, waiting for transfers between devices, exchanged(): lax.ppermute(value, axis, [(i, i ^ by) for i in range(lax.axis_size(axis))])  6.91 us
    ppermute x2, starting transfers between devices, carry(): arrived = lax.ppermute(sent, 'tm', onward)  2.58 us
    ppermute x2, waiting for transfers between devices, carry(): arrived = lax.ppermute(sent, 'tm', onward)  1.06 us
  transfers between devices with their start and end apart: 9, of which 7 were waited for; matrix products, arithmetic and copies ran while one was open for 0% of the time, Pallas kernels for 19%

profile of v7, /device:TPU:0, one launch (start us, length us, event | category | flops | bytes accessed | tf_op | source)
XLA Modules:
  0.0 37.5 jit_solution(18235069874709301395)
XLA Ops:
  0.6 1.1 %shard_map.95 = (f32[32,128]{1,0:T(8,128)S(1)}, bf16[128,384]{1,0:T(8,128)(2,1)S(1)}, f32[128,384]{1,0:T(8,128)S(1)}, f32[1,384]{1,0:T(1,128)S(1)}, f32[8,128]{1,0:T(8,128)S(1)}) custom-call(bf16[32,128]{1,0:T(8,128)(2,1)} %bitcast.10, f32[1,128]{1,0:T(1,128)} %start_hbm.1, bf16[128,384]{1,0:T(8,128)(2,1)} %in_weight_hbm.1, f32[128,384]{1,0:T(8,128)} %weight_hbm.1, ...), custom_call_target="tpu_custom_call" | custom-call | tf_op jit(solution)/shard_map/pallas_call | solution.py:268
  1.7 4.0 %collective-permute-start = (f32[32,128]{1,0:T(8,128)S(1)}, f32[32,128]{1,0:T(8,128)S(1)}, u32[]{:S(2)}, u32[]{:S(2)}) collective-permute-start(f32[32,128]{1,0:T(8,128)S(1)} %get-tuple-element.33.refs_3_), channel_id=1, source_target_pairs={{0,12},{4,8},{8,4},{12,0},{16,28},{20,24},{24,20},{28,16},{1,13},{... | collective-permute-start | bytes 49160 | tf_op jit(solution)/shard_map/ppermute | solution.py:279
  5.8 0.4 %collective-permute-start.1 = (f32[32,128]{1,0:T(8,128)S(1)}, f32[32,128]{1,0:T(8,128)S(1)}, u32[]{:S(2)}, u32[]{:S(2)}) collective-permute-start(f32[32,128]{1,0:T(8,128)S(1)} %get-tuple-element.33.refs_3_), channel_id=1, source_target_pairs={{0,8},{4,12},{8,0},{12,4},{16,24},{20,28},{24,16},{28,20},{1,9},{5... | collective-permute-start | bytes 49160 | tf_op jit(solution)/shard_map/ppermute | solution.py:279
  6.2 0.2 collective-permute-start.2
  6.4 1.1 %collective-permute-done.refs_0_ = f32[32,128]{1,0:T(8,128)S(1)} collective-permute-done((f32[32,128]{1,0:T(8,128)S(1)}, f32[32,128]{1,0:T(8,128)S(1)}, u32[]{:S(2)}, u32[]{:S(2)}) %collective-permute-start) | collective-permute-done | bytes 16416 | tf_op jit(solution)/shard_map/ppermute | solution.py:279
  7.5 2.0 %collective-permute-done.1.refs_1_ = f32[32,128]{1,0:T(8,128)S(1)} collective-permute-done((f32[32,128]{1,0:T(8,128)S(1)}, f32[32,128]{1,0:T(8,128)S(1)}, u32[]{:S(2)}, u32[]{:S(2)}) %collective-permute-start.1) | collective-permute-done | bytes 16416 | tf_op jit(solution)/shard_map/ppermute | solution.py:279
  9.5 0.4 %collective-permute-done.2.refs_2_ = f32[32,128]{1,0:T(8,128)S(1)} collective-permute-done((f32[32,128]{1,0:T(8,128)S(1)}, f32[32,128]{1,0:T(8,128)S(1)}, u32[]{:S(2)}, u32[]{:S(2)}) %collective-permute-start.2) | collective-permute-done | bytes 16416 | tf_op jit(solution)/shard_map/ppermute | solution.py:279
  9.9 6.0 %shard_map.96 = (f32[128,384]{1,0:T(8,128)S(1)}, f32[8,128]{1,0:T(8,128)S(1)}, f32[128,128]{1,0:T(8,128)S(1)}, f32[136,128,128]{2,1,0:T(8,128)S(1)}, f32[136,128]{1,0:T(8,128)S(1)}, /*index=5*/f32[8,128]{1,0:T(8,128)S(1)}) custom-call(f32[8,128]{1,0:T(8,128)S(1)} %get-tuple-element.29.consts_ref.start_ref.refs_0_, ...), custom_call_target="tpu_custom_call" | custom-call | tf_op jit(solution)/shard_map/pallas_call | solution.py:268
  15.9 1.3 %collective-permute-start.4 = (f32[8,128]{1,0:T(8,128)S(1)}, f32[8,128]{1,0:T(8,128)S(1)}, u32[]{:S(2)}, u32[]{:S(2)}) collective-permute-start(f32[8,128]{1,0:T(8,128)S(1)} %get-tuple-element.45), channel_id=1, source_target_pairs={{0,16},{4,20},{8,24},{12,28},{1,17},{5,21},{9,25},{13,29},{2,18},{... | collective-permute-start | bytes 12296 | tf_op jit(solution)/shard_map/ppermute | solution.py:297
  17.2 6.8 %shard_map.97 = (f32[8,128]{1,0:T(8,128)S(1)}, f32[128,128]{1,0:T(8,128)S(1)}, f32[136,128,128]{2,1,0:T(8,128)S(1)}, f32[136,128]{1,0:T(8,128)S(1)}, f32[8,128]{1,0:T(8,128)S(1)}) custom-call(f32[8,128]{1,0:T(8,128)S(1)} %get-tuple-element.29.consts_ref.start_ref.refs_0_, f32[8,128]{1,0:T(8,128)S(1)} %get-tuple-element.29.consts_ref.start_ref.refs_0_, ...), custom_call_target="tpu_custom_call" | custom-call | tf_op jit(solution)/shard_map/pallas_call | solution.py:268
  24.0 1.3 %collective-permute-start.3 = (f32[8,128]{1,0:T(8,128)S(1)}, f32[8,128]{1,0:T(8,128)S(1)}, u32[]{:S(2)}, u32[]{:S(2)}) collective-permute-start(f32[8,128]{1,0:T(8,128)S(1)} %get-tuple-element.43), channel_id=1, source_target_pairs={{0,16},{4,20},{8,24},{12,28},{1,17},{5,21},{9,25},{13,29},{2,18},{... | collective-permute-start | bytes 12296 | tf_op jit(solution)/shard_map/ppermute | solution.py:297
  25.3 0.2 shard_map.98
  25.5 0.0 collective-permute-done.4.start_ref
  25.6 1.1 %collective-permute-done.3.refs_6_ = f32[8,128]{1,0:T(8,128)S(1)} collective-permute-done((f32[8,128]{1,0:T(8,128)S(1)}, f32[8,128]{1,0:T(8,128)S(1)}, u32[]{:S(2)}, u32[]{:S(2)}) %collective-permute-start.3) | collective-permute-done | bytes 4128 | tf_op jit(solution)/shard_map/ppermute | solution.py:297
  26.6 1.8 %shard_map.100 = (f32[32,128]{1,0:T(8,128)}, f32[8,128]{1,0:T(8,128)S(1)}) custom-call(f32[8,128]{1,0:T(8,128)S(1)} %get-tuple-element.29.consts_ref.start_ref.refs_0_, f32[128,384]{1,0:T(8,128)S(1)} %get-tuple-element.30.weight_ref, f32[8,128]{1,0:T(8,128)S(1)} %get-tuple-element.29.consts_ref.start_ref.refs_0_, ...), custom_call_target="tpu_custom_call" | custom-call | tf_op jit(solution)/shard_map/pallas_call | solution.py:268
  28.4 0.0 collective-permute-start.5
  28.4 1.5 %collective-permute-start.6 = (f32[8,128]{1,0:T(8,128)S(1)}, f32[8,128]{1,0:T(8,128)S(1)}, u32[]{:S(2)}, u32[]{:S(2)}) collective-permute-start(f32[8,128]{1,0:T(8,128)S(1)} %get-tuple-element.55), channel_id=1, source_target_pairs={{0,2},{1,3},{2,0},{3,1},{4,6},{5,7},{6,4},{7,5},{8,10},{9,11},{10,... | collective-permute-start | bytes 12296 | tf_op jit(solution)/shard_map/ppermute | solution.py:279
  30.0 0.3 collective-permute-start.7
  30.3 1.2 %collective-permute-done.5 = f32[8,128]{1,0:T(8,128)S(1)} collective-permute-done((f32[8,128]{1,0:T(8,128)S(1)}, f32[8,128]{1,0:T(8,128)S(1)}, u32[]{:S(2)}, u32[]{:S(2)}) %collective-permute-start.5) | collective-permute-done | bytes 4128 | tf_op jit(solution)/shard_map/ppermute | solution.py:279
  31.5 0.6 %collective-permute-done.6 = f32[8,128]{1,0:T(8,128)S(1)} collective-permute-done((f32[8,128]{1,0:T(8,128)S(1)}, f32[8,128]{1,0:T(8,128)S(1)}, u32[]{:S(2)}, u32[]{:S(2)}) %collective-permute-start.6) | collective-permute-done | bytes 4128 | tf_op jit(solution)/shard_map/ppermute | solution.py:279
  32.1 0.0 collective-permute-done.7
  32.1 3.2 %collective-permute-start.8 = (f32[8,128]{1,0:T(8,128)S(1)}, f32[8,128]{1,0:T(8,128)S(1)}, u32[]{:S(2)}, u32[]{:S(2)}) collective-permute-start(f32[8,128]{1,0:T(8,128)S(1)} %add_add_fusion), channel_id=1, source_target_pairs={{0,16},{4,20},{8,24},{12,28},{16,0},{20,4},{24,8},{28,12},{1,17},{... | collective-permute-start | bytes 12296 | tf_op jit(solution)/shard_map/ppermute | solution.py:279
  35.3 1.6 %collective-permute-done.8 = f32[8,128]{1,0:T(8,128)S(1)} collective-permute-done((f32[8,128]{1,0:T(8,128)S(1)}, f32[8,128]{1,0:T(8,128)S(1)}, u32[]{:S(2)}, u32[]{:S(2)}) %collective-permute-start.8) | collective-permute-done | bytes 4128 | tf_op jit(solution)/shard_map/ppermute | solution.py:279
  36.9 0.5 %sqrt_bitcast_fusion = f32[2]{0:T(128)} fusion(f32[8,128]{1,0:T(8,128)S(1)} %add.19), kind=kLoop, calls=%fused_computation.1 | loop fusion | flops 4 | bytes 16 | tf_op jit(solution)/shard_map/sqrt | solution.py:356
  (3 shorter events, 0.0 us)
Async XLA Ops:
  1.7 5.8 %collective-permute-start = (f32[32,128]{1,0:T(8,128)S(1)}, f32[32,128]{1,0:T(8,128)S(1)}, u32[]{:S(2)}, u32[]{:S(2)}) collective-permute-start(f32[32,128]{1,0:T(8,128)S(1)} %get-tuple-element.33.refs_3_), channel_id=1, source_target_pairs={{0,12},{4,8},{8,4},{12,0},{16,28},{20,24},{24,20},{28,16},{1,13},{... | collective-permute-start | bytes 49160 | tf_op jit(solution)/shard_map/ppermute | solution.py:279
  5.8 3.7 %collective-permute-start.1 = (f32[32,128]{1,0:T(8,128)S(1)}, f32[32,128]{1,0:T(8,128)S(1)}, u32[]{:S(2)}, u32[]{:S(2)}) collective-permute-start(f32[32,128]{1,0:T(8,128)S(1)} %get-tuple-element.33.refs_3_), channel_id=1, source_target_pairs={{0,8},{4,12},{8,0},{12,4},{16,24},{20,28},{24,16},{28,20},{1,9},{5... | collective-permute-start | bytes 49160 | tf_op jit(solution)/shard_map/ppermute | solution.py:279
  6.2 3.7 %collective-permute-start.2 = (f32[32,128]{1,0:T(8,128)S(1)}, f32[32,128]{1,0:T(8,128)S(1)}, u32[]{:S(2)}, u32[]{:S(2)}) collective-permute-start(f32[32,128]{1,0:T(8,128)S(1)} %get-tuple-element.33.refs_3_), channel_id=1, source_target_pairs={{0,4},{4,0},{8,12},{12,8},{16,20},{20,16},{24,28},{28,24},{1,5},{5... | collective-permute-start | bytes 49160 | tf_op jit(solution)/shard_map/ppermute | solution.py:279
  15.9 9.6 %collective-permute-start.4 = (f32[8,128]{1,0:T(8,128)S(1)}, f32[8,128]{1,0:T(8,128)S(1)}, u32[]{:S(2)}, u32[]{:S(2)}) collective-permute-start(f32[8,128]{1,0:T(8,128)S(1)} %get-tuple-element.45), channel_id=1, source_target_pairs={{0,16},{4,20},{8,24},{12,28},{1,17},{5,21},{9,25},{13,29},{2,18},{... | collective-permute-start | bytes 12296 | tf_op jit(solution)/shard_map/ppermute | solution.py:297
  24.0 2.6 %collective-permute-start.3 = (f32[8,128]{1,0:T(8,128)S(1)}, f32[8,128]{1,0:T(8,128)S(1)}, u32[]{:S(2)}, u32[]{:S(2)}) collective-permute-start(f32[8,128]{1,0:T(8,128)S(1)} %get-tuple-element.43), channel_id=1, source_target_pairs={{0,16},{4,20},{8,24},{12,28},{1,17},{5,21},{9,25},{13,29},{2,18},{... | collective-permute-start | bytes 12296 | tf_op jit(solution)/shard_map/ppermute | solution.py:297
  28.4 3.0 %collective-permute-start.5 = (f32[8,128]{1,0:T(8,128)S(1)}, f32[8,128]{1,0:T(8,128)S(1)}, u32[]{:S(2)}, u32[]{:S(2)}) collective-permute-start(f32[8,128]{1,0:T(8,128)S(1)} %get-tuple-element.55), channel_id=1, source_target_pairs={{0,3},{1,2},{2,1},{3,0},{4,7},{5,6},{6,5},{7,4},{8,11},{9,10},{10,... | collective-permute-start | bytes 12296 | tf_op jit(solution)/shard_map/ppermute | solution.py:279
  28.4 3.6 %collective-permute-start.6 = (f32[8,128]{1,0:T(8,128)S(1)}, f32[8,128]{1,0:T(8,128)S(1)}, u32[]{:S(2)}, u32[]{:S(2)}) collective-permute-start(f32[8,128]{1,0:T(8,128)S(1)} %get-tuple-element.55), channel_id=1, source_target_pairs={{0,2},{1,3},{2,0},{3,1},{4,6},{5,7},{6,4},{7,5},{8,10},{9,11},{10,... | collective-permute-start | bytes 12296 | tf_op jit(solution)/shard_map/ppermute | solution.py:279
  30.0 2.1 %collective-permute-start.7 = (f32[8,128]{1,0:T(8,128)S(1)}, f32[8,128]{1,0:T(8,128)S(1)}, u32[]{:S(2)}, u32[]{:S(2)}) collective-permute-start(f32[8,128]{1,0:T(8,128)S(1)} %get-tuple-element.55), channel_id=1, source_target_pairs={{0,1},{1,0},{2,3},{3,2},{4,5},{5,4},{6,7},{7,6},{8,9},{9,8},{10,11... | collective-permute-start | bytes 12296 | tf_op jit(solution)/shard_map/ppermute | solution.py:279
  32.1 4.8 %collective-permute-start.8 = (f32[8,128]{1,0:T(8,128)S(1)}, f32[8,128]{1,0:T(8,128)S(1)}, u32[]{:S(2)}, u32[]{:S(2)}) collective-permute-start(f32[8,128]{1,0:T(8,128)S(1)} %add_add_fusion), channel_id=1, source_target_pairs={{0,16},{4,20},{8,24},{12,28},{16,0},{20,4},{24,8},{28,12},{1,17},{... | collective-permute-start | bytes 12296 | tf_op jit(solution)/shard_map/ppermute | solution.py:279

commit v8 on v7

--- a/solution.py
+++ b/solution.py
@@ -241,8 +241,9 @@
 
 def add_sum(newton, sums_ref, states_ref, parts, new_sums_ref):
     done = weighted_square(states_ref[...], parts[4])
-    lane = lax.broadcasted_iota(jnp.int32, new_sums_ref.shape, 1)
-    new_sums_ref[...] = jnp.where(lane == newton, done, sums_ref[...])
+    lane = lax.broadcasted_iota(jnp.int32, (1, states_ref.shape[1]), 1)
+    sums = jnp.where(lane == newton, done, sums_ref[0:1, :])
+    new_sums_ref[...] = jnp.broadcast_to(sums.reshape((1,) * len(new_sums_ref.shape[:-1]) + sums.shape[1:]), new_sums_ref.shape)
 
 
 def last_kernel(newton, sides, consts_ref, weight_ref, *refs):
@@ -279,16 +280,10 @@
     return lax.ppermute(value, axis, [(i, i ^ by) for i in range(lax.axis_size(axis))])
 
 
-def summed(value, axis, by=1):
-    count = lax.axis_size(axis)
-    while by < count:
-        radix = min(4, count // by)
-        terms = [exchanged(value, axis, k * by) for k in range(radix - 1, 0, -1)] + [value]
-        while len(terms) > 1:
-            terms = [a + b for a, b in zip(terms[0::2], terms[1::2])]
-        value = terms[0]
-        by *= radix
-    return value
+def summed(rows, by):
+    count, batch = lax.axis_size("tm"), lax.axis_size("batch")
+    groups = [[i * batch + j for i in range(place, count, by) for j in range(batch)] for place in range(by)]
+    return jnp.sum(lax.all_to_all(rows, ("tm", "batch"), 0, 0, axis_index_groups=groups), axis=0)
 
 
 def carry(sent, own_map):
@@ -349,9 +344,9 @@
             args = [one for side in range(sides) for one in (starts[side], *held[side][:5])]
             states, total = call(
                 functools.partial(last_kernel, newton, sides), [consts, weight, *args],
-                [(share, units), (8, units)], [rows, rows],
+                [(share, units), (lax.axis_size("batch") * lax.axis_size("tm") // SPAN, 1, units)], [rows, rows],
             )
-    totals = summed(summed(total, "batch"), "tm", SPAN)[0, :ITERS]
+    totals = summed(total, SPAN)[0, :ITERS]
     denom = lax.axis_size("batch") * sequences * units * (share * lax.axis_size("tm") + 1) / 2.0
     residual_norms = jnp.sqrt(totals / denom + 1e-06)
     return (states.reshape(share, sequences, units), residual_norms)

time: 37.7 us -> 40 us (1.061)
  blocking collectives: 0 us -> 10.7 us
  starting transfers between devices: 12.4 us -> 7.27 us
  waiting for transfers between devices: 7.97 us -> 4.6 us
    all_to_all x0 -> x1, blocking collectives: none -> 10.7 us  [summed(): lax.all_to_all(rows, ('tm', 'batch'), 0, 0, axis_index_groups=groups)]
    ppermute x7 -> x3, starting transfers between devices: 9.78 us -> 4.69 us  [exchanged(): lax.ppermute(value, axis, [(i, i ^ by) for i in range(lax.axis_size(axis))])]
    ppermute x7 -> x3, waiting for transfers between devices: 6.91 us -> 3.54 us  [exchanged(): lax.ppermute(value, axis, [(i, i ^ by) for i in range(lax.axis_size(axis))])]
  transfers between devices with their start and end apart: 9 -> 5, of which waited for: 7 -> 4; matrix products, arithmetic and copies ran while one was open for 0% -> 0% of each run, Pallas kernels for 19% -> 18%
where the time goes in v8:
time: 40 us; the launch traced here: 39.7 us
  Pallas kernels  15.9 us (40%)
  blocking collectives  10.7 us (27%)
  starting transfers between devices  7.27 us (18%)
  waiting for transfers between devices  4.6 us (11%)
  between operations  0.69 us (2%)
  other arithmetic  0.55 us (1%)
    pallas_call x6, Pallas kernels, call(): pl.pallas_call(kernel, out_shape=[jax.ShapeDtypeStruct(o, F32) if isinsta...  15.9 us
    all_to_all x1, blocking collectives, summed(): lax.all_to_all(rows, ('tm', 'batch'), 0, 0, axis_index_groups=groups)  10.7 us
    ppermute x3, starting transfers between devices, exchanged(): lax.ppermute(value, axis, [(i, i ^ by) for i in range(lax.axis_size(axis))])  4.69 us
    ppermute x3, waiting for transfers between devices, exchanged(): lax.ppermute(value, axis, [(i, i ^ by) for i in range(lax.axis_size(axis))])  3.54 us
    ppermute x2, starting transfers between devices, carry(): arrived = lax.ppermute(sent, 'tm', onward)  2.58 us
    ppermute x2, waiting for transfers between devices, carry(): arrived = lax.ppermute(sent, 'tm', onward)  1.06 us
  transfers between devices with their start and end apart: 5, of which 4 were waited for; matrix products, arithmetic and copies ran while one was open for 0% of the time, Pallas kernels for 18%

profile of v8, /device:TPU:0, one launch (start us, length us, event | category | flops | bytes accessed | tf_op | source)
XLA Modules:
  0.0 39.7 jit_solution(2197799540770550442)
XLA Ops:
  0.6 1.1 %shard_map.95 = (f32[32,128]{1,0:T(8,128)S(1)}, bf16[128,384]{1,0:T(8,128)(2,1)S(1)}, f32[128,384]{1,0:T(8,128)S(1)}, f32[1,384]{1,0:T(1,128)S(1)}, f32[8,128]{1,0:T(8,128)S(1)}) custom-call(bf16[32,128]{1,0:T(8,128)(2,1)} %bitcast.11, f32[1,128]{1,0:T(1,128)} %start_hbm.1, bf16[128,384]{1,0:T(8,128)(2,1)} %in_weight_hbm.1, f32[128,384]{1,0:T(8,128)} %weight_hbm.1, ...), custom_call_target="tpu_custom_call" | custom-call | tf_op jit(solution)/shard_map/pallas_call | solution.py:269
  1.7 4.0 %collective-permute-start = (f32[32,128]{1,0:T(8,128)S(1)}, f32[32,128]{1,0:T(8,128)S(1)}, u32[]{:S(2)}, u32[]{:S(2)}) collective-permute-start(f32[32,128]{1,0:T(8,128)S(1)} %get-tuple-element.33.refs_3_), channel_id=1, source_target_pairs={{0,12},{4,8},{8,4},{12,0},{16,28},{20,24},{24,20},{28,16},{1,13},{... | collective-permute-start | bytes 49160 | tf_op jit(solution)/shard_map/ppermute | solution.py:280
  5.8 0.4 %collective-permute-start.1 = (f32[32,128]{1,0:T(8,128)S(1)}, f32[32,128]{1,0:T(8,128)S(1)}, u32[]{:S(2)}, u32[]{:S(2)}) collective-permute-start(f32[32,128]{1,0:T(8,128)S(1)} %get-tuple-element.33.refs_3_), channel_id=1, source_target_pairs={{0,8},{4,12},{8,0},{12,4},{16,24},{20,28},{24,16},{28,20},{1,9},{5... | collective-permute-start | bytes 49160 | tf_op jit(solution)/shard_map/ppermute | solution.py:280
  6.2 0.2 collective-permute-start.2
  6.4 1.1 %collective-permute-done.refs_0_ = f32[32,128]{1,0:T(8,128)S(1)} collective-permute-done((f32[32,128]{1,0:T(8,128)S(1)}, f32[32,128]{1,0:T(8,128)S(1)}, u32[]{:S(2)}, u32[]{:S(2)}) %collective-permute-start) | collective-permute-done | bytes 16416 | tf_op jit(solution)/shard_map/ppermute | solution.py:280
  7.5 2.0 %collective-permute-done.1.refs_1_ = f32[32,128]{1,0:T(8,128)S(1)} collective-permute-done((f32[32,128]{1,0:T(8,128)S(1)}, f32[32,128]{1,0:T(8,128)S(1)}, u32[]{:S(2)}, u32[]{:S(2)}) %collective-permute-start.1) | collective-permute-done | bytes 16416 | tf_op jit(solution)/shard_map/ppermute | solution.py:280
  9.5 0.4 %collective-permute-done.2.refs_2_ = f32[32,128]{1,0:T(8,128)S(1)} collective-permute-done((f32[32,128]{1,0:T(8,128)S(1)}, f32[32,128]{1,0:T(8,128)S(1)}, u32[]{:S(2)}, u32[]{:S(2)}) %collective-permute-start.2) | collective-permute-done | bytes 16416 | tf_op jit(solution)/shard_map/ppermute | solution.py:280
  9.9 6.0 %shard_map.96 = (f32[128,384]{1,0:T(8,128)S(1)}, f32[8,128]{1,0:T(8,128)S(1)}, f32[128,128]{1,0:T(8,128)S(1)}, f32[136,128,128]{2,1,0:T(8,128)S(1)}, f32[136,128]{1,0:T(8,128)S(1)}, /*index=5*/f32[8,128]{1,0:T(8,128)S(1)}) custom-call(f32[8,128]{1,0:T(8,128)S(1)} %get-tuple-element.29.consts_ref.start_ref.refs_0_, ...), custom_call_target="tpu_custom_call" | custom-call | tf_op jit(solution)/shard_map/pallas_call | solution.py:269
  15.9 1.3 %collective-permute-start.4 = (f32[8,128]{1,0:T(8,128)S(1)}, f32[8,128]{1,0:T(8,128)S(1)}, u32[]{:S(2)}, u32[]{:S(2)}) collective-permute-start(f32[8,128]{1,0:T(8,128)S(1)} %get-tuple-element.45), channel_id=1, source_target_pairs={{0,16},{4,20},{8,24},{12,28},{1,17},{5,21},{9,25},{13,29},{2,18},{... | collective-permute-start | bytes 12296 | tf_op jit(solution)/shard_map/ppermute | solution.py:292
  17.2 6.8 %shard_map.97 = (f32[8,128]{1,0:T(8,128)S(1)}, f32[128,128]{1,0:T(8,128)S(1)}, f32[136,128,128]{2,1,0:T(8,128)S(1)}, f32[136,128]{1,0:T(8,128)S(1)}, f32[8,128]{1,0:T(8,128)S(1)}) custom-call(f32[8,128]{1,0:T(8,128)S(1)} %get-tuple-element.29.consts_ref.start_ref.refs_0_, f32[8,128]{1,0:T(8,128)S(1)} %get-tuple-element.29.consts_ref.start_ref.refs_0_, ...), custom_call_target="tpu_custom_call" | custom-call | tf_op jit(solution)/shard_map/pallas_call | solution.py:269
  24.0 1.3 %collective-permute-start.3 = (f32[8,128]{1,0:T(8,128)S(1)}, f32[8,128]{1,0:T(8,128)S(1)}, u32[]{:S(2)}, u32[]{:S(2)}) collective-permute-start(f32[8,128]{1,0:T(8,128)S(1)} %get-tuple-element.43), channel_id=1, source_target_pairs={{0,16},{4,20},{8,24},{12,28},{1,17},{5,21},{9,25},{13,29},{2,18},{... | collective-permute-start | bytes 12296 | tf_op jit(solution)/shard_map/ppermute | solution.py:292
  25.3 0.2 shard_map.98
  25.6 0.0 collective-permute-done.4.start_ref
  25.6 1.1 %collective-permute-done.3.refs_6_ = f32[8,128]{1,0:T(8,128)S(1)} collective-permute-done((f32[8,128]{1,0:T(8,128)S(1)}, f32[8,128]{1,0:T(8,128)S(1)}, u32[]{:S(2)}, u32[]{:S(2)}) %collective-permute-start.3) | collective-permute-done | bytes 4128 | tf_op jit(solution)/shard_map/ppermute | solution.py:292
  26.6 1.8 %shard_map.100 = (f32[32,128]{1,0:T(8,128)}, f32[8,1,128]{2,1,0:T(1,128)S(1)}) custom-call(f32[8,128]{1,0:T(8,128)S(1)} %get-tuple-element.29.consts_ref.start_ref.refs_0_, f32[128,384]{1,0:T(8,128)S(1)} %get-tuple-element.30.weight_ref, f32[8,128]{1,0:T(8,128)S(1)} %get-tuple-element.29.consts_ref.start_ref.refs_0_, ...), custom_call_target="tpu_custom_call" | custom-call | tf_op jit(solution)/shard_map/pallas_call | solution.py:269
  28.5 10.7 %all_to_all.5 = f32[8,1,128]{2,1,0:T(1,128)S(1)} all-to-all(f32[8,1,128]{2,1,0:T(1,128)S(1)} %get-tuple-element.55), channel_id=1, replica_groups={{0,1,2,3,16,17,18,19},{4,5,6,7,20,21,22,23},{8,9,10,11,24,25,26,27},{12..., dimensions={0} | all-to-all | bytes 8192 | tf_op jit(solution)/shard_map/all_to_all | solution.py:286
  39.2 0.5 %sqrt_bitcast_fusion = f32[2]{0:T(128)} fusion(f32[1,128]{1,0:T(1,128)S(1)} %bitcast.16), kind=kLoop, calls=%fused_computation | loop fusion | flops 4 | bytes 16 | tf_op jit(solution)/shard_map/sqrt | solution.py:351
  (2 shorter events, 0.1 us)
Async XLA Ops:
  1.7 5.8 %collective-permute-start = (f32[32,128]{1,0:T(8,128)S(1)}, f32[32,128]{1,0:T(8,128)S(1)}, u32[]{:S(2)}, u32[]{:S(2)}) collective-permute-start(f32[32,128]{1,0:T(8,128)S(1)} %get-tuple-element.33.refs_3_), channel_id=1, source_target_pairs={{0,12},{4,8},{8,4},{12,0},{16,28},{20,24},{24,20},{28,16},{1,13},{... | collective-permute-start | bytes 49160 | tf_op jit(solution)/shard_map/ppermute | solution.py:280
  5.8 3.7 %collective-permute-start.1 = (f32[32,128]{1,0:T(8,128)S(1)}, f32[32,128]{1,0:T(8,128)S(1)}, u32[]{:S(2)}, u32[]{:S(2)}) collective-permute-start(f32[32,128]{1,0:T(8,128)S(1)} %get-tuple-element.33.refs_3_), channel_id=1, source_target_pairs={{0,8},{4,12},{8,0},{12,4},{16,24},{20,28},{24,16},{28,20},{1,9},{5... | collective-permute-start | bytes 49160 | tf_op jit(solution)/shard_map/ppermute | solution.py:280
  6.2 3.7 %collective-permute-start.2 = (f32[32,128]{1,0:T(8,128)S(1)}, f32[32,128]{1,0:T(8,128)S(1)}, u32[]{:S(2)}, u32[]{:S(2)}) collective-permute-start(f32[32,128]{1,0:T(8,128)S(1)} %get-tuple-element.33.refs_3_), channel_id=1, source_target_pairs={{0,4},{4,0},{8,12},{12,8},{16,20},{20,16},{24,28},{28,24},{1,5},{5... | collective-permute-start | bytes 49160 | tf_op jit(solution)/shard_map/ppermute | solution.py:280
  15.9 9.7 %collective-permute-start.4 = (f32[8,128]{1,0:T(8,128)S(1)}, f32[8,128]{1,0:T(8,128)S(1)}, u32[]{:S(2)}, u32[]{:S(2)}) collective-permute-start(f32[8,128]{1,0:T(8,128)S(1)} %get-tuple-element.45), channel_id=1, source_target_pairs={{0,16},{4,20},{8,24},{12,28},{1,17},{5,21},{9,25},{13,29},{2,18},{... | collective-permute-start | bytes 12296 | tf_op jit(solution)/shard_map/ppermute | solution.py:292
  24.0 2.6 %collective-permute-start.3 = (f32[8,128]{1,0:T(8,128)S(1)}, f32[8,128]{1,0:T(8,128)S(1)}, u32[]{:S(2)}, u32[]{:S(2)}) collective-permute-start(f32[8,128]{1,0:T(8,128)S(1)} %get-tuple-element.43), channel_id=1, source_target_pairs={{0,16},{4,20},{8,24},{12,28},{1,17},{5,21},{9,25},{13,29},{2,18},{... | collective-permute-start | bytes 12296 | tf_op jit(solution)/shard_map/ppermute | solution.py:292

commit v9 on v6

v9 whole, which is shorter than its diff:
```python
import functools

import jax
import jax.numpy as jnp
from jax import lax
from jax.experimental import pallas as pl
from jax.experimental.pallas import tpu as pltpu
from jax.sharding import PartitionSpec as P

ITERS = 2
SPAN = 4
SIZE = 8
PAD = 16
F32 = jnp.float32
BF16 = jnp.bfloat16


def halves(value):
    high = value.astype(BF16)
    return high, (value - high.astype(F32)).astype(BF16)


def paired_rows(value):
    return jnp.concatenate(halves(value), axis=1)


def paired_cols(value):
    both = jnp.concatenate(halves(value), axis=1)
    return jnp.concatenate([both, both], axis=0)


def product(rows, cols):
    width = cols.shape[1]
    both = jnp.dot(paired_rows(rows), paired_cols(cols), preferred_element_type=F32)
    return both[:, :width] + both[:, width:]


def as_column(row):
    units = row.shape[1]
    return jnp.broadcast_to(row, (units, units)).T


def row_times(column, matrix):
    return jnp.sum(column * matrix, axis=0, keepdims=True)


def cell(gates, previous, rec_weight, rec_bias):
    units = previous.shape[1]
    rec = product(previous, rec_weight)
    update = jax.nn.sigmoid(gates[:, :units] + rec[:, :units])
    reset = jax.nn.sigmoid(gates[:, units : 2 * units] + rec[:, units : 2 * units])
    recur = rec[:, 2 * units :] + rec_bias
    cand = jnp.tanh(gates[:, 2 * units :] + reset * recur)
    stepped = (1.0 - update) * cand + update * previous
    return update, reset, recur, cand, stepped


def group():
    return lax.axis_index("tm") // SPAN


def through(state, one_map):
    units = state.shape[1]
    column = as_column(state - one_map[units + 1 : units + 2, :])
    return row_times(column, one_map[:units, :]) + one_map[units : units + 1, :]


def stacked(mat, vec):
    return jnp.concatenate([mat, jnp.broadcast_to(vec, (PAD, mat.shape[1]))], axis=0)


def join(mats, vecs, early, late, base, out):
    after = product(stacked(mats[early], vecs[early : early + 1, :] - base), mats[late])
    units = after.shape[1]
    mats[out] = after[:units]
    vecs[out : out + 1, :] = after[units : units + 1] + vecs[late : late + 1, :]


def layout(share):
    blocks = share // SIZE
    where = {(b, 1): (b + 1) * SIZE - 1 for b in range(blocks)}
    free, span = share, 2
    while span <= blocks:
        for b in range(0, blocks, span):
            where[(b, span)] = free
            free += 1
        span *= 2
    return where, -(-free // 8) * 8


def fold(parts, prev_ref, weight_ref, coef_refs, slots, pieces, share):
    update, reset, recur, cand, stepped = parts
    units = update.shape[1]
    previous = prev_ref[slots[0] * share : (slots[-1] + 1) * share, :]
    update_ref, coef_update_ref, coef_reset_ref, coef_cand_ref, step_ref = coef_refs
    common = (1.0 - update) * (1.0 - cand * cand)
    update_ref[...] = update
    coef_update_ref[...] = (previous - cand) * update * (1.0 - update)
    coef_reset_ref[...] = common * recur * reset * (1.0 - reset)
    coef_cand_ref[...] = common * reset
    step_ref[...] = stepped
    row = lax.broadcasted_iota(jnp.int32, (units, units), 0)
    col = lax.broadcasted_iota(jnp.int32, (units, units), 1)

    def slope(r):
        return (
            weight_ref[:, :units] * coef_update_ref[r : r + 1, :]
            + weight_ref[:, units : 2 * units] * coef_reset_ref[r : r + 1, :]
            + weight_ref[:, 2 * units :] * coef_cand_ref[r : r + 1, :]
        )

    for inner in range(SIZE):
        for i, k in enumerate(slots):
            mats, vecs = pieces[k]
            for t in range(inner, share, SIZE):
                r = i * share + t
                if inner == 0:
                    mats[t] = slope(r) + jnp.where(row == col, update_ref[r : r + 1, :], 0.0)
                    vecs[t : t + 1, :] = step_ref[r : r + 1, :]
                    continue
                taken = prev_ref[k * share + t : k * share + t + 1, :]
                before = stacked(mats[t - 1], vecs[t - 1 : t, :] - taken)
                after = product(before, slope(r)) + before * update_ref[r : r + 1, :]
                mats[t] = after[:units]
                vecs[t : t + 1, :] = after[units : units + 1] + step_ref[r : r + 1, :]
    where, _ = layout(share)
    for (b, span), out in where.items():
        if span > 1:
            second = b + span // 2
            for k in slots:
                base = prev_ref[k * share + second * SIZE : k * share + second * SIZE + 1, :]
                join(*pieces[k], where[(b, span // 2)], where[(second, span // 2)], base, out)


def share_map(share):
    return layout(share)[0][(0, share // SIZE)]


def slot_of(part):
    return lax.rem(lax.axis_index("tm"), SPAN) ^ part


def base_of(prev_ref, part, share):
    return prev_ref[pl.ds(slot_of(part) * share, 1), :]


def fold_shares(prev_ref, pieces, share, tops, top_scratch, map_ref, whole):
    mats, vecs = tops
    held_mats, held_vecs = top_scratch
    at = share_map(share)
    for k in range(SPAN):
        held_mats[k] = pieces[k][0][at]
        held_vecs[k : k + 1, :] = pieces[k][1][at : at + 1, :]
    for part in range(SPAN):
        mats[part] = held_mats[slot_of(part)]
        vecs[part : part + 1, :] = held_vecs[pl.ds(slot_of(part), 1), :]
    join(mats, vecs, 0, 1, base_of(prev_ref, 1, share), 4)
    if whole:
        units = map_ref.shape[1]
        join(mats, vecs, 2, 3, base_of(prev_ref, 3, share), 5)
        join(mats, vecs, 4, 5, base_of(prev_ref, 2, share), 6)
        map_ref[:units, :] = mats[6]
        map_ref[units : units + 1, :] = vecs[6:7, :]
        map_ref[units + 1 : units + 2, :] = base_of(prev_ref, 0, share)
        map_ref[units + 2 :, :] = jnp.zeros((6, units), F32)


def unfold(entering, prev_ref, pieces, tops, share, starts_ref, out_ref):
    top_mats, top_vecs = tops
    starts_ref[0:1, :] = entering
    column = as_column(entering - base_of(prev_ref, 0, share))
    middle = row_times(column, top_mats[4]) + top_vecs[4:5, :]
    starts_ref[1:2, :] = row_times(column, top_mats[0]) + top_vecs[0:1, :]
    starts_ref[2:3, :] = middle
    column = as_column(middle - base_of(prev_ref, 2, share))
    starts_ref[3:4, :] = row_times(column, top_mats[2]) + top_vecs[2:3, :]
    where, _ = layout(share)
    blocks = share // SIZE
    starts = {(0, k): starts_ref[pl.ds(slot_of(k), 1), :] for k in range(SPAN)}
    for b in sorted(range(blocks), key=lambda b: (bin(b).count("1"), -b)):
        for k in range(SPAN):
            mats, vecs = pieces[k]
            t, first = b * SIZE, k * share + b * SIZE
            column = as_column(starts[(b, k)] - prev_ref[first : first + 1, :])
            span = 1
            while b % (2 * span) == 0 and b + span < blocks:
                at = where[(b, span)]
                starts[(b + span, k)] = row_times(column, mats[at]) + vecs[at : at + 1, :]
                span *= 2
            for inner in range(SIZE):
                state = row_times(column, mats[t + inner]) + vecs[t + inner : t + inner + 1, :]
                out_ref[first + inner : first + inner + 1, :] = state


def shift_in(starts_ref, states_ref, prev_ref, share):
    steps = states_ref.shape[0]
    prev_ref[1:steps, :] = states_ref[0 : steps - 1, :]
    for k in range(SPAN):
        prev_ref[k * share : k * share + 1, :] = starts_ref[pl.ds(slot_of(k), 1), :]


def slots_in(refs):
    return [(mats.at[k], vecs.at[k]) for mats, vecs in zip(refs[0::2], refs[1::2]) for k in range(mats.shape[0])]


def weighted_square(states, stepped):
    steps = states.shape[0]
    share = steps // SPAN
    count = lax.axis_size("tm") // SPAN
    row = lax.broadcasted_iota(jnp.int32, states.shape, 0)
    position = group() * steps + slot_of(row // share) * share + row % share
    weights = (position.astype(F32) + 1.0) / (steps * count)
    return jnp.sum(weights * (states - stepped) ** 2, axis=(0, 1), keepdims=True)


def send_on(start, map_ref, sent_ref):
    sent_ref[...] = jnp.broadcast_to(through(start, map_ref), sent_ref.shape)


def fetch_kernel(
    inputs_hbm, start_hbm, in_weight_hbm, weight_hbm, update_bias_hbm, reset_bias_hbm, cand_bias_hbm,
    rec_bias_hbm,
    wide_ref, in_weight_ref, weight_ref, bias_ref, consts_ref,
    inputs_ref, start_ref, rec_bias_ref, sems
):
    units = weight_ref.shape[0]
    moves = [
        (inputs_hbm, inputs_ref), (in_weight_hbm, in_weight_ref), (weight_hbm, weight_ref),
        (update_bias_hbm, bias_ref.at[:, pl.ds(0, units)]),
        (reset_bias_hbm, bias_ref.at[:, pl.ds(units, units)]),
        (cand_bias_hbm, bias_ref.at[:, pl.ds(2 * units, units)]),
        (start_hbm, start_ref), (rec_bias_hbm, rec_bias_ref),
    ]
    copies = [pltpu.make_async_copy(src, dst, sems.at[i]) for i, (src, dst) in enumerate(moves)]
    for copy in copies:
        copy.start()
    for copy in copies:
        copy.wait()
    wide_ref[...] = inputs_ref[...].astype(F32)
    consts_ref[0:1, :] = start_ref[...]
    consts_ref[1:2, :] = rec_bias_ref[...]
    consts_ref[2:, :] = jnp.zeros((6, units), F32)


def own_kernel(
    own_ref, consts_ref, in_weight_ref, bias_ref, weight_ref,
    gates_ref, mats_ref, vecs_ref, prev_ref, *coef_refs
):
    share, units = own_ref.shape
    gates = jnp.dot(own_ref[...].astype(BF16), in_weight_ref[...], preferred_element_type=F32) + bias_ref[...]
    gates_ref[...] = gates
    at_start = (lax.axis_index("tm") == 0) & (lax.broadcasted_iota(jnp.int32, (share, units), 0) == 0)
    previous = jnp.where(at_start, consts_ref[0:1, :], 0.0)
    prev_ref[...] = previous
    parts = cell(gates, previous, weight_ref[...], consts_ref[1:2, :])
    fold(parts, prev_ref, weight_ref, coef_refs, [0], slots_in([mats_ref, vecs_ref]), share)


def first_kernel(
    at_front, whole, consts_ref, in_weight_ref, bias_ref, weight_ref, own_gates_ref, own_mats_ref, own_vecs_ref, *refs
):
    shares, refs = refs[: SPAN - 1], refs[SPAN - 1 :]
    gates_ref, sums_ref, prev_ref, top_mats, top_vecs, mats_ref, vecs_ref, sent_ref, map_ref, *scratch = refs
    top_scratch, coef_refs = scratch[:2], scratch[2:]
    steps, units = prev_ref.shape
    share = steps // SPAN

    @pl.when((group() == 0) == at_front)
    def _():
        sums_ref[...] = jnp.zeros(sums_ref.shape, F32)
        inputs = jnp.concatenate([one[...] for one in shares], axis=0).astype(BF16)
        gates = jnp.dot(inputs, in_weight_ref[...], preferred_element_type=F32) + bias_ref[...]
        gates_ref[:share, :] = own_gates_ref[...]
        gates_ref[share:, :] = gates
        previous = jnp.zeros((steps, units), F32)
        if at_front:
            row = lax.broadcasted_iota(jnp.int32, (steps, units), 0)
            previous = jnp.where(row == slot_of(0) * share, consts_ref[0:1, :], 0.0)
        prev_ref[...] = previous
        parts = cell(gates, previous[share:], weight_ref[...], consts_ref[1:2, :])
        pieces = slots_in([own_mats_ref, own_vecs_ref, mats_ref, vecs_ref])
        fold(parts, prev_ref, weight_ref, coef_refs, list(range(1, SPAN)), pieces, share)
        fold_shares(prev_ref, pieces, share, (top_mats, top_vecs), top_scratch, map_ref, whole)
        if at_front:
            send_on(consts_ref[0:1, :], map_ref, sent_ref)


def hop_kernel(sent_first_ref, map_ref, arrived_ref, sent_ref):
    state = through(arrived_ref[0:1, :], map_ref)
    sent_ref[...] = jnp.where(group() == 0, sent_first_ref[...], state)


def middle_kernel(
    newton, at_front, whole, held, start_ref, consts_ref, weight_ref, gates_ref, sums_ref, old_prev_ref, *refs
):
    old_tops, old, refs = refs[:2], refs[2:held], refs[held:]
    new_sums_ref, new_prev_ref, top_mats, top_vecs, mats_ref, vecs_ref, sent_ref, map_ref, *scratch = refs
    states_ref, starts_ref, top_scratch, coef_refs = scratch[0], scratch[1], scratch[2:4], scratch[4:]
    share = states_ref.shape[0] // SPAN

    @pl.when((group() == 0) == at_front)
    def _():
        entering = start_ref[0:1, :]
        unfold(entering, old_prev_ref, slots_in(old), old_tops, share, starts_ref, states_ref)
        shift_in(starts_ref, states_ref, new_prev_ref, share)
        parts = cell(gates_ref[...], new_prev_ref[...], weight_ref[...], consts_ref[1:2, :])
        add_sum(newton, sums_ref, states_ref, parts, new_sums_ref)
        pieces = slots_in([mats_ref, vecs_ref])
        fold(parts, new_prev_ref, weight_ref, coef_refs, list(range(SPAN)), pieces, share)
        fold_shares(new_prev_ref, pieces, share, (top_mats, top_vecs), top_scratch, map_ref, whole)
        if at_front:
            send_on(entering, map_ref, sent_ref)


def add_sum(newton, sums_ref, states_ref, parts, new_sums_ref):
    done = weighted_square(states_ref[...], parts[4])
    lane = lax.broadcasted_iota(jnp.int32, new_sums_ref.shape, 1)
    new_sums_ref[...] = jnp.where(lane == newton, done, sums_ref[...])


def last_kernel(newton, sides, held, consts_ref, weight_ref, *refs):
    sides_refs, refs = [refs[held * i : held * i + held] for i in range(sides)], refs[held * sides :]
    out_ref, new_sums_ref, prev_ref, states_ref, starts_ref = refs
    share = out_ref.shape[0]
    for side, (start_ref, gates_ref, sums_ref, old_prev_ref, *old) in enumerate(sides_refs):

        @pl.when((group() == 0) == (side == 0))
        def _():
            unfold(start_ref[0:1, :], old_prev_ref, slots_in(old[2:]), old[:2], share, starts_ref, states_ref)
            shift_in(starts_ref, states_ref, prev_ref, share)
            parts = cell(gates_ref[...], prev_ref[...], weight_ref[...], consts_ref[1:2, :])
            add_sum(newton, sums_ref, states_ref, parts, new_sums_ref)

    out_ref[...] = states_ref[:share, :]


def call(kernel, args, outs, scratch=(), space=pltpu.VMEM):
    args = [pltpu.with_memory_space_constraint(arg, space) for arg in args]
    return pl.pallas_call(
        kernel,
        out_shape=[jax.ShapeDtypeStruct(o, F32) if isinstance(o, tuple) else o for o in outs],
        in_specs=[pl.BlockSpec(memory_space=space)] * len(args),
        out_specs=[pl.BlockSpec(memory_space=pltpu.VMEM)] * len(outs),
        scratch_shapes=[pltpu.VMEM(one, F32) if isinstance(one, tuple) else one for one in scratch],
        compiler_params=pltpu.CompilerParams(vmem_limit_bytes=16 * 1024 * 1024),
    )(*args)


def exchanged(value, axis, by):
    return lax.ppermute(value, axis, [(i, i ^ by) for i in range(lax.axis_size(axis))])


def summed(value, axis, by=1):
    count = lax.axis_size(axis)
    while by < count:
        radix = min(4, count // by)
        terms = [value] + [exchanged(value, axis, k * by) for k in range(1, radix)]
        while len(terms) > 1:
            terms = [a + b for a, b in zip(terms[0::2], terms[1::2])]
        value = terms[0]
        by *= radix
    return value


def carry(sent, own_map):
    count = lax.axis_size("tm")
    onward = [(i, i + SPAN) for i in range(count - SPAN)]
    arrived = lax.ppermute(sent, "tm", onward)
    for _ in range(count // SPAN - 2):
        (further,) = call(hop_kernel, [sent, *own_map, arrived], [sent.shape])
        arrived = lax.ppermute(further, "tm", onward)
    return arrived


def per_device(
    inputs, h_start, in_weight, rec_weight, update_bias, reset_bias, cand_bias, rec_bias
):
    share, sequences = inputs.shape[0], inputs.shape[1]
    units = rec_weight.shape[0]
    row = lambda value: value.reshape(1, units)
    steps = share * SPAN
    rows, wide = (steps, units), (steps, 3 * units)
    sides = min(2, lax.axis_size("tm") // SPAN)
    slots = layout(share)[1]
    of_slots = lambda count: [(count, slots, units, units), (count, slots, units)]
    tops = [(8, units, units), (8, units)]
    top_scratch = [(SPAN, units, units), (8, units)]
    state_row, map_rows = (8, units), (units + 8, units)
    further = lax.axis_size("tm") // SPAN > 2
    ends = [([state_row], [map_rows])]
    if sides > 1:
        ends.append(([state_row, map_rows], []) if further else ([], [state_row, map_rows]))
    own, in_rows, weight, bias, consts = call(
        fetch_kernel,
        [inputs.reshape(share, -1), h_start, in_weight, rec_weight, row(update_bias), row(reset_bias),
         row(cand_bias), row(rec_bias)],
        [(share, units), jax.ShapeDtypeStruct(in_weight.shape, BF16), rec_weight.shape, (1, 3 * units),
         (8, units)],
        [pltpu.VMEM((share, units), BF16), (1, units), (1, units), pltpu.SemaphoreType.DMA((8,))],
        space=pltpu.HBM,
    )
    shares = [exchanged(own, "tm", k) for k in range(1, SPAN)]
    own_gates, *own_slot = call(
        own_kernel, [own, consts, in_rows, bias, weight], [(share, 3 * units)] + of_slots(1),
        [(share, units)] * 6,
    )
    held = []
    beside = []
    for side, (out, kept) in enumerate(ends):
        gates, sums, prev, top_mats, top_vecs, mats, vecs, *more = call(
            functools.partial(first_kernel, side == 0, side == 0 or further),
            [consts, in_rows, bias, weight, own_gates, *own_slot, *shares],
            [wide, (8, units), rows] + tops + of_slots(SPAN - 1) + out,
            kept + top_scratch + [(steps - share, units)] * 5,
        )
        held.append([gates, sums, prev, top_mats, top_vecs, *own_slot, mats, vecs])
        beside.append(more)
    for newton in range(ITERS):
        starts = [consts] + [carry(beside[0][0], beside[-1][1:])] * (sides - 1)
        if newton < ITERS - 1:
            for side, (out, kept) in enumerate(ends):
                solved = call(
                    functools.partial(
                        middle_kernel, newton, side == 0, side == 0 or further, len(held[side]) - 3
                    ),
                    [starts[side], consts, weight, *held[side]],
                    [(8, units), rows] + tops + of_slots(SPAN) + out,
                    kept + [rows, (8, units)] + top_scratch + [rows] * 5,
                )
                held[side] = [held[side][0], *solved[:6]]
                beside[side] = solved[6:]
        else:
            args = [one for side in range(sides) for one in (starts[side], *held[side])]
            states, total = call(
                functools.partial(last_kernel, newton, sides, len(held[0]) + 1), [consts, weight, *args],
                [(share, units), (8, units)], [rows, rows, (8, units)],
            )
    totals = summed(summed(total, "batch"), "tm", SPAN)[0, :ITERS]
    denom = lax.axis_size("batch") * sequences * units * (share * lax.axis_size("tm") + 1) / 2.0
    residual_norms = jnp.sqrt(totals / denom + 1e-06)
    return (states.reshape(share, sequences, units), residual_norms)


def solution(mesh):
    in_specs = (P("tm", "batch", None), P("batch", None), P(), P(), P(), P(), P(), P())
    out_specs = (P("tm", "batch", None), P())
    return jax.shard_map(
        per_device, mesh=mesh, in_specs=in_specs, out_specs=out_specs, check_vma=False
    )
```

time: 39 us -> 36.9 us (0.946)
  waiting for transfers between devices: 9.94 us -> 6.15 us
  Pallas kernels: 15.4 us -> 16.9 us
    ppermute x7, waiting for transfers between devices: 8.88 us -> 5.09 us  [exchanged(): lax.ppermute(value, axis, [(i, i ^ by) for i in range(lax.axis_size(axis))])]
    pallas_call x6 -> x7, Pallas kernels: 15.4 us -> 16.9 us  [call(): pl.pallas_call(kernel, out_shape=[jax.ShapeDtypeStruct(o, F32) if isinsta...]
  transfers between devices with their start and end apart: 9 -> 9, of which waited for: 7 -> 6; matrix products, arithmetic and copies ran while one was open for 0% -> 0% of each run, Pallas kernels for 18% -> 25%
where the time goes in v9:
time: 36.9 us; the launch traced here: 36.7 us
  Pallas kernels  16.9 us (46%)
  starting transfers between devices  12.4 us (34%)
  waiting for transfers between devices  6.15 us (17%)
  between operations  0.71 us (2%)
  other arithmetic  0.53 us (1%)
    pallas_call x7, Pallas kernels, call(): pl.pallas_call(kernel, out_shape=[jax.ShapeDtypeStruct(o, F32) if isinsta...  16.9 us
    ppermute x7, starting transfers between devices, exchanged(): lax.ppermute(value, axis, [(i, i ^ by) for i in range(lax.axis_size(axis))])  9.78 us
    ppermute x7, waiting for transfers between devices, exchanged(): lax.ppermute(value, axis, [(i, i ^ by) for i in range(lax.axis_size(axis))])  5.09 us
    ppermute x2, starting transfers between devices, carry(): arrived = lax.ppermute(sent, 'tm', onward)  2.58 us
    ppermute x2, waiting for transfers between devices, carry(): arrived = lax.ppermute(sent, 'tm', onward)  1.06 us
  transfers between devices with their start and end apart: 9, of which 6 were waited for; matrix products, arithmetic and copies ran while one was open for 0% of the time, Pallas kernels for 25%

profile of v9, /device:TPU:0, one launch (start us, length us, event | category | flops | bytes accessed | tf_op | source)
XLA Modules:
  0.0 36.7 jit_solution(11951655753373963384)
XLA Ops:
  0.6 1.1 %shard_map.95 = (f32[32,128]{1,0:T(8,128)S(1)}, bf16[128,384]{1,0:T(8,128)(2,1)S(1)}, f32[128,384]{1,0:T(8,128)S(1)}, f32[1,384]{1,0:T(1,128)S(1)}, f32[8,128]{1,0:T(8,128)S(1)}) custom-call(bf16[32,128]{1,0:T(8,128)(2,1)} %bitcast.10, f32[1,128]{1,0:T(1,128)} %start_hbm.1, bf16[128,384]{1,0:T(8,128)(2,1)} %in_weight_hbm.1, f32[128,384]{1,0:T(8,128)} %weight_hbm.1, ...), custom_call_target="tpu_custom_call" | custom-call | tf_op jit(solution)/shard_map/pallas_call | solution.py:339
  1.7 4.0 %collective-permute-start.2 = (f32[32,128]{1,0:T(8,128)S(1)}, f32[32,128]{1,0:T(8,128)S(1)}, u32[]{:S(2)}, u32[]{:S(2)}) collective-permute-start(f32[32,128]{1,0:T(8,128)S(1)} %get-tuple-element.44.own_ref), channel_id=1, source_target_pairs={{0,12},{4,8},{8,4},{12,0},{16,28},{20,24},{24,20},{28,16},{1,13},{... | collective-permute-start | bytes 49160 | tf_op jit(solution)/shard_map/ppermute | solution.py:350
  5.8 0.4 %collective-permute-start.1 = (f32[32,128]{1,0:T(8,128)S(1)}, f32[32,128]{1,0:T(8,128)S(1)}, u32[]{:S(2)}, u32[]{:S(2)}) collective-permute-start(f32[32,128]{1,0:T(8,128)S(1)} %get-tuple-element.44.own_ref), channel_id=1, source_target_pairs={{0,8},{4,12},{8,0},{12,4},{16,24},{20,28},{24,16},{28,20},{1,9},{5... | collective-permute-start | bytes 49160 | tf_op jit(solution)/shard_map/ppermute | solution.py:350
  6.2 0.2 collective-permute-start
  6.4 1.8 %shard_map.96 = (f32[32,384]{1,0:T(8,128)S(1)}, f32[1,40,128,128]{3,2,1,0:T(8,128)S(1)}, f32[1,40,128]{2,1,0:T(8,128)S(1)}) custom-call(f32[32,128]{1,0:T(8,128)S(1)} %get-tuple-element.44.own_ref, f32[8,128]{1,0:T(8,128)S(1)} %get-tuple-element.40.consts_ref.start_ref.refs_0_, bf16[128,384]{1,0:T(8,128)(2,1)S(1)} %get-tuple-element.42.in_weight_ref, ...), custom_call_target="tpu_custom_call" | custom-call | tf_op jit(solution)/shard_map/pallas_call | solution.py:339
  8.2 0.0 collective-permute-done.2.refs_2_
  8.2 1.3 %collective-permute-done.1.refs_1_ = f32[32,128]{1,0:T(8,128)S(1)} collective-permute-done((f32[32,128]{1,0:T(8,128)S(1)}, f32[32,128]{1,0:T(8,128)S(1)}, u32[]{:S(2)}, u32[]{:S(2)}) %collective-permute-start.1) | collective-permute-done | bytes 16416 | tf_op jit(solution)/shard_map/ppermute | solution.py:350
  9.5 0.4 %collective-permute-done.refs_0_ = f32[32,128]{1,0:T(8,128)S(1)} collective-permute-done((f32[32,128]{1,0:T(8,128)S(1)}, f32[32,128]{1,0:T(8,128)S(1)}, u32[]{:S(2)}, u32[]{:S(2)}) %collective-permute-start) | collective-permute-done | bytes 16416 | tf_op jit(solution)/shard_map/ppermute | solution.py:350
  9.9 4.7 %shard_map.97 = (f32[128,384]{1,0:T(8,128)S(1)}, f32[8,128]{1,0:T(8,128)S(1)}, f32[128,128]{1,0:T(8,128)S(1)}, f32[8,128,128]{2,1,0:T(8,128)S(1)}, f32[8,128]{1,...) custom-call(f32[8,128]{1,0:T(8,128)S(1)} %get-tuple-element.40.consts_ref.start_ref, ...), custom_call_target="tpu_custom_call" | custom-call | tf_op jit(solution)/shard_map/pallas_call | solution.py:339
  14.6 1.3 %collective-permute-start.4 = (f32[8,128]{1,0:T(8,128)S(1)}, f32[8,128]{1,0:T(8,128)S(1)}, u32[]{:S(2)}, u32[]{:S(2)}) collective-permute-start(f32[8,128]{1,0:T(8,128)S(1)} %get-tuple-element.63), channel_id=1, source_target_pairs={{0,16},{4,20},{8,24},{12,28},{1,17},{5,21},{9,25},{13,29},{2,18},{... | collective-permute-start | bytes 12296 | tf_op jit(solution)/shard_map/ppermute | solution.py:368
  15.9 7.1 %shard_map.98 = (f32[8,128]{1,0:T(8,128)S(1)}, f32[128,128]{1,0:T(8,128)S(1)}, f32[8,128,128]{2,1,0:T(8,128)S(1)}, f32[8,128]{1,0:T(8,128)S(1)}, f32[4,40,128,12...) custom-call(f32[8,128]{1,0:T(8,128)S(1)} %get-tuple-element.40.consts_ref.start_ref.refs_0_, ...), custom_call_target="tpu_custom_call" | custom-call | tf_op jit(solution)/shard_map/pallas_call | solution.py:339
  23.1 1.3 %collective-permute-start.3 = (f32[8,128]{1,0:T(8,128)S(1)}, f32[8,128]{1,0:T(8,128)S(1)}, u32[]{:S(2)}, u32[]{:S(2)}) collective-permute-start(f32[8,128]{1,0:T(8,128)S(1)} %get-tuple-element.61), channel_id=1, source_target_pairs={{0,16},{4,20},{8,24},{12,28},{1,17},{5,21},{9,25},{13,29},{2,18},{... | collective-permute-start | bytes 12296 | tf_op jit(solution)/shard_map/ppermute | solution.py:368
  24.4 0.2 shard_map.99
  24.6 0.0 collective-permute-done.4.start_ref
  24.6 1.1 %collective-permute-done.3.refs_8_ = f32[8,128]{1,0:T(8,128)S(1)} collective-permute-done((f32[8,128]{1,0:T(8,128)S(1)}, f32[8,128]{1,0:T(8,128)S(1)}, u32[]{:S(2)}, u32[]{:S(2)}) %collective-permute-start.3) | collective-permute-done | bytes 4128 | tf_op jit(solution)/shard_map/ppermute | solution.py:368
  25.7 2.0 %shard_map.101 = (f32[32,128]{1,0:T(8,128)}, f32[8,128]{1,0:T(8,128)S(1)}) custom-call(f32[8,128]{1,0:T(8,128)S(1)} %get-tuple-element.40.consts_ref.start_ref.refs_0_, f32[128,384]{1,0:T(8,128)S(1)} %get-tuple-element.41.weight_ref, f32[8,128]{1,0:T(8,128)S(1)} %get-tuple-element.40.consts_ref.start_ref.refs_0_, ...), custom_call_target="tpu_custom_call" | custom-call | tf_op jit(solution)/shard_map/pallas_call | solution.py:339
  27.7 0.0 collective-permute-start.7
  27.7 1.5 %collective-permute-start.6 = (f32[8,128]{1,0:T(8,128)S(1)}, f32[8,128]{1,0:T(8,128)S(1)}, u32[]{:S(2)}, u32[]{:S(2)}) collective-permute-start(f32[8,128]{1,0:T(8,128)S(1)} %get-tuple-element.77), channel_id=1, source_target_pairs={{0,2},{1,3},{2,0},{3,1},{4,6},{5,7},{6,4},{7,5},{8,10},{9,11},{10,... | collective-permute-start | bytes 12296 | tf_op jit(solution)/shard_map/ppermute | solution.py:350
  29.2 0.3 collective-permute-start.5
  29.5 1.2 %collective-permute-done.7 = f32[8,128]{1,0:T(8,128)S(1)} collective-permute-done((f32[8,128]{1,0:T(8,128)S(1)}, f32[8,128]{1,0:T(8,128)S(1)}, u32[]{:S(2)}, u32[]{:S(2)}) %collective-permute-start.7) | collective-permute-done | bytes 4128 | tf_op jit(solution)/shard_map/ppermute | solution.py:350
  30.7 0.6 %collective-permute-done.6 = f32[8,128]{1,0:T(8,128)S(1)} collective-permute-done((f32[8,128]{1,0:T(8,128)S(1)}, f32[8,128]{1,0:T(8,128)S(1)}, u32[]{:S(2)}, u32[]{:S(2)}) %collective-permute-start.6) | collective-permute-done | bytes 4128 | tf_op jit(solution)/shard_map/ppermute | solution.py:350
  31.3 0.0 collective-permute-done.5
  31.3 3.2 %collective-permute-start.8 = (f32[8,128]{1,0:T(8,128)S(1)}, f32[8,128]{1,0:T(8,128)S(1)}, u32[]{:S(2)}, u32[]{:S(2)}) collective-permute-start(f32[8,128]{1,0:T(8,128)S(1)} %add_add_fusion), channel_id=1, source_target_pairs={{0,16},{4,20},{8,24},{12,28},{16,0},{20,4},{24,8},{28,12},{1,17},{... | collective-permute-start | bytes 12296 | tf_op jit(solution)/shard_map/ppermute | solution.py:350
  34.6 1.6 %collective-permute-done.8 = f32[8,128]{1,0:T(8,128)S(1)} collective-permute-done((f32[8,128]{1,0:T(8,128)S(1)}, f32[8,128]{1,0:T(8,128)S(1)}, u32[]{:S(2)}, u32[]{:S(2)}) %collective-permute-start.8) | collective-permute-done | bytes 4128 | tf_op jit(solution)/shard_map/ppermute | solution.py:350
  36.2 0.5 %sqrt_bitcast_fusion = f32[2]{0:T(128)} fusion(f32[8,128]{1,0:T(8,128)S(1)} %add.19), kind=kLoop, calls=%fused_computation.1 | loop fusion | flops 4 | bytes 16 | tf_op jit(solution)/shard_map/sqrt | solution.py:440
  (3 shorter events, 0.0 us)
Async XLA Ops:
  1.7 6.5 %collective-permute-start.2 = (f32[32,128]{1,0:T(8,128)S(1)}, f32[32,128]{1,0:T(8,128)S(1)}, u32[]{:S(2)}, u32[]{:S(2)}) collective-permute-start(f32[32,128]{1,0:T(8,128)S(1)} %get-tuple-element.44.own_ref), channel_id=1, source_target_pairs={{0,12},{4,8},{8,4},{12,0},{16,28},{20,24},{24,20},{28,16},{1,13},{... | collective-permute-start | bytes 49160 | tf_op jit(solution)/shard_map/ppermute | solution.py:350
  5.8 3.7 %collective-permute-start.1 = (f32[32,128]{1,0:T(8,128)S(1)}, f32[32,128]{1,0:T(8,128)S(1)}, u32[]{:S(2)}, u32[]{:S(2)}) collective-permute-start(f32[32,128]{1,0:T(8,128)S(1)} %get-tuple-element.44.own_ref), channel_id=1, source_target_pairs={{0,8},{4,12},{8,0},{12,4},{16,24},{20,28},{24,16},{28,20},{1,9},{5... | collective-permute-start | bytes 49160 | tf_op jit(solution)/shard_map/ppermute | solution.py:350
  6.2 3.7 %collective-permute-start = (f32[32,128]{1,0:T(8,128)S(1)}, f32[32,128]{1,0:T(8,128)S(1)}, u32[]{:S(2)}, u32[]{:S(2)}) collective-permute-start(f32[32,128]{1,0:T(8,128)S(1)} %get-tuple-element.44.own_ref), channel_id=1, source_target_pairs={{0,4},{4,0},{8,12},{12,8},{16,20},{20,16},{24,28},{28,24},{1,5},{5... | collective-permute-start | bytes 49160 | tf_op jit(solution)/shard_map/ppermute | solution.py:350
  14.6 9.9 %collective-permute-start.4 = (f32[8,128]{1,0:T(8,128)S(1)}, f32[8,128]{1,0:T(8,128)S(1)}, u32[]{:S(2)}, u32[]{:S(2)}) collective-permute-start(f32[8,128]{1,0:T(8,128)S(1)} %get-tuple-element.63), channel_id=1, source_target_pairs={{0,16},{4,20},{8,24},{12,28},{1,17},{5,21},{9,25},{13,29},{2,18},{... | collective-permute-start | bytes 12296 | tf_op jit(solution)/shard_map/ppermute | solution.py:368
  23.1 2.6 %collective-permute-start.3 = (f32[8,128]{1,0:T(8,128)S(1)}, f32[8,128]{1,0:T(8,128)S(1)}, u32[]{:S(2)}, u32[]{:S(2)}) collective-permute-start(f32[8,128]{1,0:T(8,128)S(1)} %get-tuple-element.61), channel_id=1, source_target_pairs={{0,16},{4,20},{8,24},{12,28},{1,17},{5,21},{9,25},{13,29},{2,18},{... | collective-permute-start | bytes 12296 | tf_op jit(solution)/shard_map/ppermute | solution.py:368
  27.7 3.0 %collective-permute-start.7 = (f32[8,128]{1,0:T(8,128)S(1)}, f32[8,128]{1,0:T(8,128)S(1)}, u32[]{:S(2)}, u32[]{:S(2)}) collective-permute-start(f32[8,128]{1,0:T(8,128)S(1)} %get-tuple-element.77), channel_id=1, source_target_pairs={{0,3},{1,2},{2,1},{3,0},{4,7},{5,6},{6,5},{7,4},{8,11},{9,10},{10,... | collective-permute-start | bytes 12296 | tf_op jit(solution)/shard_map/ppermute | solution.py:350
  27.7 3.6 %collective-permute-start.6 = (f32[8,128]{1,0:T(8,128)S(1)}, f32[8,128]{1,0:T(8,128)S(1)}, u32[]{:S(2)}, u32[]{:S(2)}) collective-permute-start(f32[8,128]{1,0:T(8,128)S(1)} %get-tuple-element.77), channel_id=1, source_target_pairs={{0,2},{1,3},{2,0},{3,1},{4,6},{5,7},{6,4},{7,5},{8,10},{9,11},{10,... | collective-permute-start | bytes 12296 | tf_op jit(solution)/shard_map/ppermute | solution.py:350
  29.2 2.1 %collective-permute-start.5 = (f32[8,128]{1,0:T(8,128)S(1)}, f32[8,128]{1,0:T(8,128)S(1)}, u32[]{:S(2)}, u32[]{:S(2)}) collective-permute-start(f32[8,128]{1,0:T(8,128)S(1)} %get-tuple-element.77), channel_id=1, source_target_pairs={{0,1},{1,0},{2,3},{3,2},{4,5},{5,4},{6,7},{7,6},{8,9},{9,8},{10,11... | collective-permute-start | bytes 12296 | tf_op jit(solution)/shard_map/ppermute | solution.py:350
  31.3 4.8 %collective-permute-start.8 = (f32[8,128]{1,0:T(8,128)S(1)}, f32[8,128]{1,0:T(8,128)S(1)}, u32[]{:S(2)}, u32[]{:S(2)}) collective-permute-start(f32[8,128]{1,0:T(8,128)S(1)} %add_add_fusion), channel_id=1, source_target_pairs={{0,16},{4,20},{8,24},{12,28},{16,0},{20,4},{24,8},{28,12},{1,17},{... | collective-permute-start | bytes 12296 | tf_op jit(solution)/shard_map/ppermute | solution.py:350

commit v10 on v9

--- a/solution.py
+++ b/solution.py
@@ -268,7 +268,7 @@
     @pl.when((group() == 0) == at_front)
     def _():
         sums_ref[...] = jnp.zeros(sums_ref.shape, F32)
-        inputs = jnp.concatenate([one[...] for one in shares], axis=0).astype(BF16)
+        inputs = jnp.concatenate([one[...] for one in shares[::-1]], axis=0).astype(BF16)
         gates = jnp.dot(inputs, in_weight_ref[...], preferred_element_type=F32) + bias_ref[...]
         gates_ref[:share, :] = own_gates_ref[...]
         gates_ref[share:, :] = gates
@@ -318,20 +318,25 @@
     new_sums_ref[...] = jnp.where(lane == newton, done, sums_ref[...])
 
 
-def last_kernel(newton, sides, held, consts_ref, weight_ref, *refs):
-    sides_refs, refs = [refs[held * i : held * i + held] for i in range(sides)], refs[held * sides :]
-    out_ref, new_sums_ref, prev_ref, states_ref, starts_ref = refs
+def last_kernel(newton, at_front, held, start_ref, consts_ref, weight_ref, *refs):
+    (gates_ref, sums_ref, old_prev_ref, *old), refs = refs[:held], refs[held:]
+    *front, out_ref, new_sums_ref, prev_ref, states_ref, starts_ref = refs
     share = out_ref.shape[0]
-    for side, (start_ref, gates_ref, sums_ref, old_prev_ref, *old) in enumerate(sides_refs):
-
-        @pl.when((group() == 0) == (side == 0))
+
+    @pl.when((group() == 0) == at_front)
+    def _():
+        unfold(start_ref[0:1, :], old_prev_ref, slots_in(old[2:]), old[:2], share, starts_ref, states_ref)
+        shift_in(starts_ref, states_ref, prev_ref, share)
+        parts = cell(gates_ref[...], prev_ref[...], weight_ref[...], consts_ref[1:2, :])
+        add_sum(newton, sums_ref, states_ref, parts, new_sums_ref)
+        out_ref[...] = states_ref[:share, :]
+
+    if not at_front:
+
+        @pl.when(group() == 0)
         def _():
-            unfold(start_ref[0:1, :], old_prev_ref, slots_in(old[2:]), old[:2], share, starts_ref, states_ref)
-            shift_in(starts_ref, states_ref, prev_ref, share)
-            parts = cell(gates_ref[...], prev_ref[...], weight_ref[...], consts_ref[1:2, :])
-            add_sum(newton, sums_ref, states_ref, parts, new_sums_ref)
-
-    out_ref[...] = states_ref[:share, :]
+            out_ref[...] = front[0][...]
+            new_sums_ref[...] = front[1][...]
 
 
 def call(kernel, args, outs, scratch=(), space=pltpu.VMEM):
@@ -354,7 +359,7 @@
     count = lax.axis_size(axis)
     while by < count:
         radix = min(4, count // by)
-        terms = [value] + [exchanged(value, axis, k * by) for k in range(1, radix)]
+        terms = [exchanged(value, axis, k * by) for k in range(radix - 1, 0, -1)] + [value]
         while len(terms) > 1:
             terms = [a + b for a, b in zip(terms[0::2], terms[1::2])]
         value = terms[0]
@@ -399,7 +404,7 @@
         [pltpu.VMEM((share, units), BF16), (1, units), (1, units), pltpu.SemaphoreType.DMA((8,))],
         space=pltpu.HBM,
     )
-    shares = [exchanged(own, "tm", k) for k in range(1, SPAN)]
+    shares = [exchanged(own, "tm", k) for k in range(SPAN - 1, 0, -1)]
     own_gates, *own_slot = call(
         own_kernel, [own, consts, in_rows, bias, weight], [(share, 3 * units)] + of_slots(1),
         [(share, units)] * 6,
@@ -430,12 +435,22 @@
                 held[side] = [held[side][0], *solved[:6]]
                 beside[side] = solved[6:]
         else:
-            args = [one for side in range(sides) for one in (starts[side], *held[side])]
-            states, total = call(
-                functools.partial(last_kernel, newton, sides, len(held[0]) + 1), [consts, weight, *args],
-                [(share, units), (8, units)], [rows, rows, (8, units)],
-            )
-    totals = summed(summed(total, "batch"), "tm", SPAN)[0, :ITERS]
+            solved = []
+            for side in range(sides):
+                solved.append(call(
+                    functools.partial(last_kernel, newton, side == 0, len(held[side])),
+                    [starts[side], consts, weight, *held[side], *(solved[0] if side else [])],
+                    [(share, units), (8, units)], [rows, rows, (8, units)],
+                ))
+            states, total = solved[-1]
+    if sides > 1 and not further:
+        ahead = [(i, i + SPAN) for i in range(SPAN)]
+        to_others = lax.ppermute(solved[0][1], "tm", ahead)
+        to_first = lax.ppermute(total, "tm", [(j, i) for i, j in ahead])
+        total = total + (to_others + to_first)
+    elif further:
+        total = summed(total, "tm", SPAN)
+    totals = summed(total, "batch")[0, :ITERS]
     denom = lax.axis_size("batch") * sequences * units * (share * lax.axis_size("tm") + 1) / 2.0
     residual_norms = jnp.sqrt(totals / denom + 1e-06)
     return (states.reshape(share, sequences, units), residual_norms)

time: 36.9 us -> 38.8 us (1.051)
  waiting for transfers between devices: 6.15 us -> 8.6 us
  starting transfers between devices: 12.4 us -> 11.7 us
    ppermute x0 -> x2, waiting for transfers between devices: none -> 5.09 us  [the longest x1 5.09 us: per_device(): to_first = lax.ppermute(total, 'tm', [(j, i) for i, j in ahead])]
    ppermute x7 -> x6, starting transfers between devices: 9.78 us -> 6.55 us  [exchanged(): lax.ppermute(value, axis, [(i, i ^ by) for i in range(lax.axis_size(axis))])]
    ppermute x0 -> x2, starting transfers between devices: none -> 2.57 us  [the longest x1 1.29 us: per_device(): to_others = lax.ppermute(solved[0][1], 'tm', ahead)]
    ppermute x7 -> x6, waiting for transfers between devices: 5.09 us -> 3.5 us  [exchanged(): lax.ppermute(value, axis, [(i, i ^ by) for i in range(lax.axis_size(axis))])]
    ppermute x2, waiting for transfers between devices: 1.06 us -> 0.01 us  [carry(): arrived = lax.ppermute(sent, 'tm', onward)]
    pallas_call x7 -> x8, Pallas kernels: 16.9 us -> 16.9 us  [call(): pl.pallas_call(kernel, out_shape=[jax.ShapeDtypeStruct(o, F32) if isinsta...]
  transfers between devices with their start and end apart: 9 -> 10, of which waited for: 6 -> 5; matrix products, arithmetic and copies ran while one was open for 0% -> 0% of each run, Pallas kernels for 25% -> 29%
where the time goes in v10:
time: 38.8 us; the launch traced here: 38.5 us
  Pallas kernels  16.9 us (44%)
  starting transfers between devices  11.7 us (30%)
  waiting for transfers between devices  8.6 us (22%)
  between operations  0.75 us (2%)
  other arithmetic  0.53 us (1%)
    pallas_call x8, Pallas kernels, call(): pl.pallas_call(kernel, out_shape=[jax.ShapeDtypeStruct(o, F32) if isinsta...  16.9 us
    ppermute x6, starting transfers between devices, exchanged(): lax.ppermute(value, axis, [(i, i ^ by) for i in range(lax.axis_size(axis))])  6.55 us
    ppermute x1, waiting for transfers between devices, per_device(): to_first = lax.ppermute(total, 'tm', [(j, i) for i, j in ahead])  5.09 us
    ppermute x6, waiting for transfers between devices, exchanged(): lax.ppermute(value, axis, [(i, i ^ by) for i in range(lax.axis_size(axis))])  3.5 us
    ppermute x2, starting transfers between devices, carry(): arrived = lax.ppermute(sent, 'tm', onward)  2.58 us
    ppermute x1, starting transfers between devices, per_device(): to_others = lax.ppermute(solved[0][1], 'tm', ahead)  1.29 us
    ppermute x1, starting transfers between devices, per_device(): to_first = lax.ppermute(total, 'tm', [(j, i) for i, j in ahead])  1.28 us
  transfers between devices with their start and end apart: 10, of which 5 were waited for; matrix products, arithmetic and copies ran while one was open for 0% of the time, Pallas kernels for 29%

profile of v10, /device:TPU:0, one launch (start us, length us, event | category | flops | bytes accessed | tf_op | source)
XLA Modules:
  0.0 38.5 jit_solution(2920653568699802426)
XLA Ops:
  0.6 1.1 %shard_map.95 = (f32[32,128]{1,0:T(8,128)S(1)}, bf16[128,384]{1,0:T(8,128)(2,1)S(1)}, f32[128,384]{1,0:T(8,128)S(1)}, f32[1,384]{1,0:T(1,128)S(1)}, f32[8,128]{1,0:T(8,128)S(1)}) custom-call(bf16[32,128]{1,0:T(8,128)(2,1)} %bitcast.10, f32[1,128]{1,0:T(1,128)} %start_hbm.1, bf16[128,384]{1,0:T(8,128)(2,1)} %in_weight_hbm.1, f32[128,384]{1,0:T(8,128)} %weight_hbm.1, ...), custom_call_target="tpu_custom_call" | custom-call | tf_op jit(solution)/shard_map/pallas_call | solution.py:344
  1.7 4.0 %collective-permute-start = (f32[32,128]{1,0:T(8,128)S(1)}, f32[32,128]{1,0:T(8,128)S(1)}, u32[]{:S(2)}, u32[]{:S(2)}) collective-permute-start(f32[32,128]{1,0:T(8,128)S(1)} %get-tuple-element.46.own_ref), channel_id=1, source_target_pairs={{0,12},{4,8},{8,4},{12,0},{16,28},{20,24},{24,20},{28,16},{1,13},{... | collective-permute-start | bytes 49160 | tf_op jit(solution)/shard_map/ppermute | solution.py:355
  5.8 0.4 %collective-permute-start.1 = (f32[32,128]{1,0:T(8,128)S(1)}, f32[32,128]{1,0:T(8,128)S(1)}, u32[]{:S(2)}, u32[]{:S(2)}) collective-permute-start(f32[32,128]{1,0:T(8,128)S(1)} %get-tuple-element.46.own_ref), channel_id=1, source_target_pairs={{0,8},{4,12},{8,0},{12,4},{16,24},{20,28},{24,16},{28,20},{1,9},{5... | collective-permute-start | bytes 49160 | tf_op jit(solution)/shard_map/ppermute | solution.py:355
  6.2 0.2 collective-permute-start.2
  6.4 1.8 %shard_map.96 = (f32[32,384]{1,0:T(8,128)S(1)}, f32[1,40,128,128]{3,2,1,0:T(8,128)S(1)}, f32[1,40,128]{2,1,0:T(8,128)S(1)}) custom-call(f32[32,128]{1,0:T(8,128)S(1)} %get-tuple-element.46.own_ref, f32[8,128]{1,0:T(8,128)S(1)} %get-tuple-element.42.consts_ref.start_ref, bf16[128,384]{1,0:T(8,128)(2,1)S(1)} %get-tuple-element.44.in_weight_ref, ...), custom_call_target="tpu_custom_call" | custom-call | tf_op jit(solution)/shard_map/pallas_call | solution.py:344
  8.2 0.0 collective-permute-done.refs_0_
  8.2 1.3 %collective-permute-done.1.refs_1_ = f32[32,128]{1,0:T(8,128)S(1)} collective-permute-done((f32[32,128]{1,0:T(8,128)S(1)}, f32[32,128]{1,0:T(8,128)S(1)}, u32[]{:S(2)}, u32[]{:S(2)}) %collective-permute-start.1) | collective-permute-done | bytes 16416 | tf_op jit(solution)/shard_map/ppermute | solution.py:355
  9.5 0.4 %collective-permute-done.2.refs_2_ = f32[32,128]{1,0:T(8,128)S(1)} collective-permute-done((f32[32,128]{1,0:T(8,128)S(1)}, f32[32,128]{1,0:T(8,128)S(1)}, u32[]{:S(2)}, u32[]{:S(2)}) %collective-permute-start.2) | collective-permute-done | bytes 16416 | tf_op jit(solution)/shard_map/ppermute | solution.py:355
  9.9 4.8 %shard_map.97 = (f32[128,384]{1,0:T(8,128)S(1)}, f32[8,128]{1,0:T(8,128)S(1)}, f32[128,128]{1,0:T(8,128)S(1)}, f32[8,128,128]{2,1,0:T(8,128)S(1)}, f32[8,128]{1,...) custom-call(f32[8,128]{1,0:T(8,128)S(1)} %get-tuple-element.42.consts_ref.start_ref, ...), custom_call_target="tpu_custom_call" | custom-call | tf_op jit(solution)/shard_map/pallas_call | solution.py:344
  14.7 1.3 %collective-permute-start.4 = (f32[8,128]{1,0:T(8,128)S(1)}, f32[8,128]{1,0:T(8,128)S(1)}, u32[]{:S(2)}, u32[]{:S(2)}) collective-permute-start(f32[8,128]{1,0:T(8,128)S(1)} %get-tuple-element.59), channel_id=1, source_target_pairs={{0,16},{4,20},{8,24},{12,28},{1,17},{5,21},{9,25},{13,29},{2,18},{... | collective-permute-start | bytes 12296 | tf_op jit(solution)/shard_map/ppermute | solution.py:373
  16.0 7.0 %shard_map.98 = (f32[8,128]{1,0:T(8,128)S(1)}, f32[128,128]{1,0:T(8,128)S(1)}, f32[8,128,128]{2,1,0:T(8,128)S(1)}, f32[8,128]{1,0:T(8,128)S(1)}, f32[4,40,128,12...) custom-call(f32[8,128]{1,0:T(8,128)S(1)} %get-tuple-element.42.consts_ref.start_ref, ...), custom_call_target="tpu_custom_call" | custom-call | tf_op jit(solution)/shard_map/pallas_call | solution.py:344
  23.0 1.3 %collective-permute-start.3 = (f32[8,128]{1,0:T(8,128)S(1)}, f32[8,128]{1,0:T(8,128)S(1)}, u32[]{:S(2)}, u32[]{:S(2)}) collective-permute-start(f32[8,128]{1,0:T(8,128)S(1)} %get-tuple-element.57), channel_id=1, source_target_pairs={{0,16},{4,20},{8,24},{12,28},{1,17},{5,21},{9,25},{13,29},{2,18},{... | collective-permute-start | bytes 12296 | tf_op jit(solution)/shard_map/ppermute | solution.py:373
  24.3 1.6 %shard_map.101 = (f32[32,128]{1,0:T(8,128)S(1)}, f32[8,128]{1,0:T(8,128)S(1)}) custom-call(f32[8,128]{1,0:T(8,128)S(1)} %get-tuple-element.42.consts_ref.start_ref, f32[8,128]{1,0:T(8,128)S(1)} %get-tuple-element.42.consts_ref.start_ref, f32[128,384]{1,0:T(8,128)S(1)} %get-tuple-element.43.weight_ref, f32[128,384]{1,0:T(8,128)S(1)} %get-tuple-element.50.gates_ref.refs_0_, ...), custom_call_target="tpu_custom_call" | custom-call | tf_op jit(solution)/shard_map/pallas_call | solution.py:344
  25.9 1.3 %collective-permute-start.5 = (f32[8,128]{1,0:T(8,128)S(1)}, f32[8,128]{1,0:T(8,128)S(1)}, u32[]{:S(2)}, u32[]{:S(2)}) collective-permute-start(f32[8,128]{1,0:T(8,128)S(1)} %get-tuple-element.79.refs_8_), channel_id=1, source_target_pairs={{0,16},{4,20},{8,24},{12,28},{1,17},{5,21},{9,25},{13,29},{2,18},{... | collective-permute-start | bytes 12296 | tf_op jit(solution)/shard_map/ppermute | solution.py:448
  27.2 0.0 collective-permute-done.4.start_ref
  27.3 0.0 collective-permute-done.3.start_ref
  27.3 0.6 %shard_map.102 = (f32[32,128]{1,0:T(8,128)}, f32[8,128]{1,0:T(8,128)S(1)}) custom-call(f32[8,128]{1,0:T(8,128)S(1)} %collective-permute-done.3.start_ref, f32[8,128]{1,0:T(8,128)S(1)} %get-tuple-element.42.consts_ref.start_ref, f32[128,384]{1,0:T(8,128)S(1)} %get-tuple-element.43.weight_ref, f32[128,384]{1,0:T(8,128)S(1)} %get-tuple-element.58.gates_ref.refs_0_, ...), custom_call_target="tpu_custom_call" | custom-call | tf_op jit(solution)/shard_map/pallas_call | solution.py:344
  27.9 1.3 %collective-permute-start.6 = (f32[8,128]{1,0:T(8,128)S(1)}, f32[8,128]{1,0:T(8,128)S(1)}, u32[]{:S(2)}, u32[]{:S(2)}) collective-permute-start(f32[8,128]{1,0:T(8,128)S(1)} %get-tuple-element.81), channel_id=1, source_target_pairs={{16,0},{20,4},{24,8},{28,12},{17,1},{21,5},{25,9},{29,13},{18,2},{... | collective-permute-start | bytes 12296 | tf_op jit(solution)/shard_map/ppermute | solution.py:449
  29.2 0.0 collective-permute-done.5
  29.2 5.1 %collective-permute-done.6 = f32[8,128]{1,0:T(8,128)S(1)} collective-permute-done((f32[8,128]{1,0:T(8,128)S(1)}, f32[8,128]{1,0:T(8,128)S(1)}, u32[]{:S(2)}, u32[]{:S(2)}) %collective-permute-start.6) | collective-permute-done | bytes 4128 | tf_op jit(solution)/shard_map/ppermute | solution.py:449
  34.3 0.0 collective-permute-start.7
  34.3 1.5 %collective-permute-start.8 = (f32[8,128]{1,0:T(8,128)S(1)}, f32[8,128]{1,0:T(8,128)S(1)}, u32[]{:S(2)}, u32[]{:S(2)}) collective-permute-start(f32[8,128]{1,0:T(8,128)S(1)} %add_add_fusion.1), channel_id=1, source_target_pairs={{0,2},{1,3},{2,0},{3,1},{4,6},{5,7},{6,4},{7,5},{8,10},{9,11},{10,... | collective-permute-start | bytes 12296 | tf_op jit(solution)/shard_map/ppermute | solution.py:355
  35.8 0.3 collective-permute-start.9
  36.2 1.2 %collective-permute-done.7 = f32[8,128]{1,0:T(8,128)S(1)} collective-permute-done((f32[8,128]{1,0:T(8,128)S(1)}, f32[8,128]{1,0:T(8,128)S(1)}, u32[]{:S(2)}, u32[]{:S(2)}) %collective-permute-start.7) | collective-permute-done | bytes 4128 | tf_op jit(solution)/shard_map/ppermute | solution.py:355
  37.3 0.6 %collective-permute-done.8 = f32[8,128]{1,0:T(8,128)S(1)} collective-permute-done((f32[8,128]{1,0:T(8,128)S(1)}, f32[8,128]{1,0:T(8,128)S(1)}, u32[]{:S(2)}, u32[]{:S(2)}) %collective-permute-start.8) | collective-permute-done | bytes 4128 | tf_op jit(solution)/shard_map/ppermute | solution.py:355
  38.0 0.0 collective-permute-done.9
  38.0 0.5 %sqrt_bitcast_fusion = f32[2]{0:T(128)} fusion(f32[8,128]{1,0:T(8,128)S(1)} %add_add_fusion), kind=kLoop, calls=%fused_computation.2 | loop fusion | flops 4 | bytes 16 | tf_op jit(solution)/shard_map/sqrt | solution.py:455
  (4 shorter events, 0.1 us)
Async XLA Ops:
  1.7 6.5 %collective-permute-start = (f32[32,128]{1,0:T(8,128)S(1)}, f32[32,128]{1,0:T(8,128)S(1)}, u32[]{:S(2)}, u32[]{:S(2)}) collective-permute-start(f32[32,128]{1,0:T(8,128)S(1)} %get-tuple-element.46.own_ref), channel_id=1, source_target_pairs={{0,12},{4,8},{8,4},{12,0},{16,28},{20,24},{24,20},{28,16},{1,13},{... | collective-permute-start | bytes 49160 | tf_op jit(solution)/shard_map/ppermute | solution.py:355
  5.8 3.7 %collective-permute-start.1 = (f32[32,128]{1,0:T(8,128)S(1)}, f32[32,128]{1,0:T(8,128)S(1)}, u32[]{:S(2)}, u32[]{:S(2)}) collective-permute-start(f32[32,128]{1,0:T(8,128)S(1)} %get-tuple-element.46.own_ref), channel_id=1, source_target_pairs={{0,8},{4,12},{8,0},{12,4},{16,24},{20,28},{24,16},{28,20},{1,9},{5... | collective-permute-start | bytes 49160 | tf_op jit(solution)/shard_map/ppermute | solution.py:355
  6.2 3.7 %collective-permute-start.2 = (f32[32,128]{1,0:T(8,128)S(1)}, f32[32,128]{1,0:T(8,128)S(1)}, u32[]{:S(2)}, u32[]{:S(2)}) collective-permute-start(f32[32,128]{1,0:T(8,128)S(1)} %get-tuple-element.46.own_ref), channel_id=1, source_target_pairs={{0,4},{4,0},{8,12},{12,8},{16,20},{20,16},{24,28},{28,24},{1,5},{5... | collective-permute-start | bytes 49160 | tf_op jit(solution)/shard_map/ppermute | solution.py:355
  14.7 12.5 %collective-permute-start.4 = (f32[8,128]{1,0:T(8,128)S(1)}, f32[8,128]{1,0:T(8,128)S(1)}, u32[]{:S(2)}, u32[]{:S(2)}) collective-permute-start(f32[8,128]{1,0:T(8,128)S(1)} %get-tuple-element.59), channel_id=1, source_target_pairs={{0,16},{4,20},{8,24},{12,28},{1,17},{5,21},{9,25},{13,29},{2,18},{... | collective-permute-start | bytes 12296 | tf_op jit(solution)/shard_map/ppermute | solution.py:373
  23.0 4.3 %collective-permute-start.3 = (f32[8,128]{1,0:T(8,128)S(1)}, f32[8,128]{1,0:T(8,128)S(1)}, u32[]{:S(2)}, u32[]{:S(2)}) collective-permute-start(f32[8,128]{1,0:T(8,128)S(1)} %get-tuple-element.57), channel_id=1, source_target_pairs={{0,16},{4,20},{8,24},{12,28},{1,17},{5,21},{9,25},{13,29},{2,18},{... | collective-permute-start | bytes 12296 | tf_op jit(solution)/shard_map/ppermute | solution.py:373
  25.9 3.3 %collective-permute-start.5 = (f32[8,128]{1,0:T(8,128)S(1)}, f32[8,128]{1,0:T(8,128)S(1)}, u32[]{:S(2)}, u32[]{:S(2)}) collective-permute-start(f32[8,128]{1,0:T(8,128)S(1)} %get-tuple-element.79.refs_8_), channel_id=1, source_target_pairs={{0,16},{4,20},{8,24},{12,28},{1,17},{5,21},{9,25},{13,29},{2,18},{... | collective-permute-start | bytes 12296 | tf_op jit(solution)/shard_map/ppermute | solution.py:448
  27.9 6.4 %collective-permute-start.6 = (f32[8,128]{1,0:T(8,128)S(1)}, f32[8,128]{1,0:T(8,128)S(1)}, u32[]{:S(2)}, u32[]{:S(2)}) collective-permute-start(f32[8,128]{1,0:T(8,128)S(1)} %get-tuple-element.81), channel_id=1, source_target_pairs={{16,0},{20,4},{24,8},{28,12},{17,1},{21,5},{25,9},{29,13},{18,2},{... | collective-permute-start | bytes 12296 | tf_op jit(solution)/shard_map/ppermute | solution.py:449
  34.3 3.0 %collective-permute-start.7 = (f32[8,128]{1,0:T(8,128)S(1)}, f32[8,128]{1,0:T(8,128)S(1)}, u32[]{:S(2)}, u32[]{:S(2)}) collective-permute-start(f32[8,128]{1,0:T(8,128)S(1)} %add_add_fusion.1), channel_id=1, source_target_pairs={{0,3},{1,2},{2,1},{3,0},{4,7},{5,6},{6,5},{7,4},{8,11},{9,10},{10,... | collective-permute-start | bytes 12296 | tf_op jit(solution)/shard_map/ppermute | solution.py:355
  34.3 3.6 %collective-permute-start.8 = (f32[8,128]{1,0:T(8,128)S(1)}, f32[8,128]{1,0:T(8,128)S(1)}, u32[]{:S(2)}, u32[]{:S(2)}) collective-permute-start(f32[8,128]{1,0:T(8,128)S(1)} %add_add_fusion.1), channel_id=1, source_target_pairs={{0,2},{1,3},{2,0},{3,1},{4,6},{5,7},{6,4},{7,5},{8,10},{9,11},{10,... | collective-permute-start | bytes 12296 | tf_op jit(solution)/shard_map/ppermute | solution.py:355
  35.8 2.1 %collective-permute-start.9 = (f32[8,128]{1,0:T(8,128)S(1)}, f32[8,128]{1,0:T(8,128)S(1)}, u32[]{:S(2)}, u32[]{:S(2)}) collective-permute-start(f32[8,128]{1,0:T(8,128)S(1)} %add_add_fusion.1), channel_id=1, source_target_pairs={{0,1},{1,0},{2,3},{3,2},{4,5},{5,4},{6,7},{7,6},{8,9},{9,8},{10,11... | collective-permute-start | bytes 12296 | tf_op jit(solution)/shard_map/ppermute | solution.py:355
